TPU v7x, 32 devices: a whole 2x2x4 slice. The times are simulated.
32 devices in a mesh: section: 2 (over y), dp: 16 (over z, x, core).
Axes of the slice: x: 2, y: 2, z: 4, core: 2. Of those that a mesh axis runs over, the one named last changes fastest.
Arguments:
- level_input: bfloat16 [4, 16, 64, 768], P(None, 'dp', 'section'), may hold values from -6 to 6
- cotangent: bfloat16 [4, 16, 64, 768], P(None, 'dp', 'section'), may hold values from -6 to 6
- class_table: bfloat16 [1000, 768], P(None, 'dp'), may hold values from -6 to 6
- conv_in: bfloat16 [2, 13824, 768], P('section', 'dp'), may hold values from -0.078125 to 0.078125
- conv_out: bfloat16 [2, 6912, 768], P('section', 'dp'), may hold values from -0.078125 to 0.078125
- embed_proj: bfloat16 [2, 768, 1536], P('section', 'dp'), may hold values from -0.21875 to 0.21875
- skip_proj: bfloat16 [2, 1536, 768], P('section', 'dp'), may hold values from -0.15625 to 0.15625
- qkv_proj: bfloat16 [2, 768, 2304], P('section', 'dp'), may hold values from -0.21875 to 0.21875
- out_proj: bfloat16 [2, 768, 768], P('section', 'dp'), may hold values from -0.625 to 0.625
- gains: bfloat16 [2, 3072], P('section', 'dp'), may hold values from 0.099609375 to 1.8984375
- biases: bfloat16 [2, 9216], P('section', 'dp'), may hold values from -3 to 3
- noise_pairs: int32 [4, 16, 2], P(None, 'dp'), may hold values from 0 to 39
- classes: int32 [4, 16], P(None, 'dp'), may hold values from 0 to 999
Outputs:
- level_output: bfloat16 [4, 16, 64, 768], P(None, 'dp', 'section')
- input_grad: float32 [4, 16, 64, 768], P(None, 'dp', 'section')
- class_table_grad: float32 [1000, 768], P(None, 'dp')
- conv_in_grad: float32 [2, 13824, 768], P('section', 'dp')
- conv_out_grad: float32 [2, 6912, 768], P('section', 'dp')
- embed_proj_grad: float32 [2, 768, 1536], P('section', 'dp')
- skip_proj_grad: float32 [2, 1536, 768], P('section', 'dp')
- qkv_proj_grad: float32 [2, 768, 2304], P('section', 'dp')
- out_proj_grad: float32 [2, 768, 768], P('section', 'dp')
- gains_grad: float32 [2, 3072], P('section', 'dp')
- biases_grad: float32 [2, 9216], P('section', 'dp')
All inputs are finite; a program needn't handle non-finite values.
Results may differ from a plain program's by a relative error of at most 0.023.
Values may be sent and summed in bfloat16 or wider, within the bound.
No kernel may reach another device: no remote copies, remote signals or barrier semaphores. Data moves between devices by JAX's collectives and lax.ppermute only.
A program may use at most 256 MiB of HBM per device.

v0:
```python
from functools import partial
import math

import jax
import jax.numpy as jnp
from jax import lax
from jax.sharding import PartitionSpec as P

WIDTH = 768
EMBED = 768
CLASSES = 1000
HEAD_DIM = 64
GROUPS = 32
SIDE = 8
LEVELS = 40
MICRO = 4
PIXELS = 64


EPS = 1e-05
SIGMA_LOW = 0.002
SIGMA_HIGH = 80.0


def passed_along(value, axis, steps):
    count = lax.axis_size(axis)
    initial, last = (max(0, -steps), min(count, count - steps))
    return lax.ppermute(value, axis, [(source, source + steps) for source in range(initial, last)])


def product(left_side, right_side):
    return jnp.dot(left_side, right_side, preferred_element_type=jnp.float32)


def product_back(left_side, right_side):
    return lax.dot_general(
        left_side, right_side, (((1,), (1,)), ((), ())), preferred_element_type=jnp.float32
    )


def outer_sum(left_side, right_side):
    return lax.dot_general(
        left_side, right_side, (((0,), (0,)), ((), ())), preferred_element_type=jnp.float32
    )


def column_total(values):
    return jnp.sum(values.astype(jnp.float32).reshape(-1, values.shape[-1]), axis=0)


def group_norm(values, gain_row, bias_row):
    images, pixels, channels = values.shape
    grouped = values.reshape(images, pixels, GROUPS, channels // GROUPS)
    centered = grouped - jnp.mean(grouped, axis=(1, 3), keepdims=True)
    spread = jnp.mean(centered * centered, axis=(1, 3), keepdims=True)
    normed = (centered * lax.rsqrt(spread + EPS)).reshape(images, pixels, channels)
    return normed * gain_row + bias_row


def columns(values):
    images, pixels, channels = values.shape
    planes = values.reshape(images, SIDE, SIDE, channels)
    padded = jnp.pad(planes, ((0, 0), (1, 1), (1, 1), (0, 0)))
    pieces = [
        padded[:, tap_row : tap_row + SIDE, tap_col : tap_col + SIDE, :]
        for tap_row in range(3)
        for tap_col in range(3)
    ]
    return jnp.concatenate(pieces, axis=-1).reshape(images * pixels, 9 * channels)


def columns_back(folded, images, channels):
    tapped = folded.reshape(images, SIDE, SIDE, 9, channels)
    total = jnp.zeros((images, SIDE + 2, SIDE + 2, channels), jnp.float32)
    for tap_index in range(9):
        tap_row = tap_index // 3
        tap_col = tap_index % 3
        total = total + jnp.pad(
            tapped[:, :, :, tap_index, :],
            ((0, 0), (tap_row, 2 - tap_row), (tap_col, 2 - tap_col), (0, 0)),
        )
    return total[:, 1 : SIDE + 1, 1 : SIDE + 1, :].reshape(images, SIDE * SIDE, channels)


def noise_features(pair_ids):
    fraction = pair_ids.astype(jnp.float32) / (LEVELS - 1)
    top_root = SIGMA_HIGH ** (1.0 / 7.0)
    bottom_root = SIGMA_LOW ** (1.0 / 7.0)
    sigmas = (top_root + fraction * (bottom_root - top_root)) ** 7
    log_scale = 250.0 * jnp.log(sigmas)
    quarter = EMBED // 4
    frequency = jnp.exp(-math.log(10000.0) * jnp.arange(quarter, dtype=jnp.float32) / quarter)
    angles = log_scale[..., None] * frequency
    return jnp.concatenate(
        [
            jnp.cos(angles[..., 0, :]),
            jnp.sin(angles[..., 0, :]),
            jnp.cos(angles[..., 1, :]),
            jnp.sin(angles[..., 1, :]),
        ],
        axis=-1,
    )


def embed_rows(pair_ids, class_ids, table_full):
    onehot = (class_ids[:, None] == lax.broadcasted_iota(jnp.int32, (1, CLASSES), 1)).astype(
        jnp.bfloat16
    )
    return (noise_features(pair_ids) + product(onehot, table_full), onehot)


def input_piece(hidden, skipped, gain_rows, bias_rows, decoder_flag):
    first_half = jax.nn.silu(group_norm(hidden, gain_rows[0], bias_rows[0]))
    second_half = jax.nn.silu(group_norm(skipped, gain_rows[1], bias_rows[1])) * decoder_flag
    return (first_half, second_half)


def middle_piece(conv_one, scale_shift, gain_rows, bias_rows):
    channels = conv_one.shape[-1]
    normed = group_norm(conv_one, gain_rows[2], bias_rows[5])
    return jax.nn.silu(
        normed * (1.0 + scale_shift[:, None, :channels]) + scale_shift[:, None, channels:]
    )


def attend_piece(residual, gain_rows, bias_rows):
    return group_norm(residual, gain_rows[3], bias_rows[8])


def unpack_weights(gathered):
    return (
        gathered[0][0],
        gathered[1][0],
        gathered[2][0],
        gathered[3][0],
        gathered[4][0],
        gathered[5][0],
        gathered[6][0].astype(jnp.float32).reshape(4, WIDTH),
        gathered[7][0].astype(jnp.float32).reshape(12, WIDTH),
    )


def split_heads(project, images, pixels, channels):
    head_count = channels // HEAD_DIM
    queries = project[:, :channels].reshape(images, pixels, head_count, HEAD_DIM)
    keys_h = project[:, channels : 2 * channels].reshape(images, pixels, head_count, HEAD_DIM)
    values_h = project[:, 2 * channels :].reshape(images, pixels, head_count, HEAD_DIM)
    return (queries, keys_h, values_h)


def section_forward(hidden_b, skipped_b, embedding, weights_now, decoder_flag, is_decoder):
    conv_in_w, conv_out_w, embed_w, skip_w, qkv_w, out_w, gain_rows, bias_rows = weights_now
    images, pixels, channels = hidden_b.shape
    row_count = images * pixels
    hidden = hidden_b.astype(jnp.float32)
    skipped = skipped_b.astype(jnp.float32)
    first_half, second_half = input_piece(hidden, skipped, gain_rows, bias_rows, decoder_flag)
    joined = jnp.concatenate(
        [first_half.astype(jnp.bfloat16), second_half.astype(jnp.bfloat16)], axis=-1
    )
    conv_one = (product(columns(joined), conv_in_w) + bias_rows[2]).reshape(
        images, pixels, channels
    )
    embed_b = embedding.astype(jnp.bfloat16)
    scale_shift = product(embed_b, embed_w) + jnp.concatenate([bias_rows[3], bias_rows[4]])
    middle = middle_piece(conv_one, scale_shift, gain_rows, bias_rows).astype(jnp.bfloat16)
    conv_two = (product(columns(middle), conv_out_w) + bias_rows[6]).reshape(
        images, pixels, channels
    )
    paired = jnp.concatenate([hidden_b, skipped_b], axis=-1)
    through = (product(paired.reshape(row_count, 2 * channels), skip_w) + bias_rows[7]).reshape(
        images, pixels, channels
    )
    residual = conv_two + jnp.where(is_decoder, through, hidden)
    attend_in = (
        attend_piece(residual, gain_rows, bias_rows)
        .astype(jnp.bfloat16)
        .reshape(row_count, channels)
    )
    bias_qkv = jnp.concatenate([bias_rows[9], jnp.zeros_like(bias_rows[9]), bias_rows[10]])
    project = (product(attend_in, qkv_w) + bias_qkv).astype(jnp.bfloat16)
    queries, keys_h, values_h = split_heads(project, images, pixels, channels)
    scores = jnp.einsum(
        "bqhd,bkhd->bhqk", queries, keys_h, preferred_element_type=jnp.float32
    ) / math.sqrt(HEAD_DIM)
    log_total = jax.nn.logsumexp(scores, axis=-1, keepdims=True)
    attention = jnp.exp(scores - log_total)
    mixed_b = jnp.einsum(
        "bhqk,bkhd->bqhd",
        attention.astype(jnp.bfloat16),
        values_h,
        preferred_element_type=jnp.float32,
    )
    mixed_b = mixed_b.reshape(row_count, channels).astype(jnp.bfloat16)
    result = residual + (product(mixed_b, out_w) + bias_rows[11]).reshape(images, pixels, channels)
    kept_list = (
        joined,
        conv_one,
        scale_shift,
        embed_b,
        middle,
        paired,
        residual,
        attend_in,
        project,
        log_total,
        mixed_b,
    )
    return (result, kept_list)


def section_backward(grad_out, kept_list, weights_now, decoder_flag, is_decoder):
    conv_in_w, conv_out_w, embed_w, skip_w, qkv_w, out_w, gain_rows, bias_rows = weights_now
    (
        joined,
        conv_one,
        scale_shift,
        embed_b,
        middle,
        paired,
        residual,
        attend_in,
        project,
        log_total,
        mixed_b,
    ) = kept_list
    images, pixels, channels = residual.shape
    row_count = images * pixels
    head_count = channels // HEAD_DIM
    head_root = math.sqrt(HEAD_DIM)
    grad_top = grad_out.reshape(row_count, channels).astype(jnp.bfloat16)
    grad_mixed = (
        product_back(grad_top, out_w)
        .astype(jnp.bfloat16)
        .reshape(images, pixels, head_count, HEAD_DIM)
    )
    queries, keys_h, values_h = split_heads(project, images, pixels, channels)
    scores = (
        jnp.einsum("bqhd,bkhd->bhqk", queries, keys_h, preferred_element_type=jnp.float32)
        / head_root
    )
    attention = jnp.exp(scores - log_total)
    grad_attention = jnp.einsum(
        "bqhd,bkhd->bhqk", grad_mixed, values_h, preferred_element_type=jnp.float32
    )
    grad_values = jnp.einsum(
        "bhqk,bqhd->bkhd",
        attention.astype(jnp.bfloat16),
        grad_mixed,
        preferred_element_type=jnp.float32,
    )
    grad_scores = attention * (
        grad_attention - jnp.sum(grad_attention * attention, axis=-1, keepdims=True)
    )
    grad_scores = grad_scores.astype(jnp.bfloat16)
    grad_queries = (
        jnp.einsum("bhqk,bkhd->bqhd", grad_scores, keys_h, preferred_element_type=jnp.float32)
        / head_root
    )
    grad_keys = (
        jnp.einsum("bhqk,bqhd->bkhd", grad_scores, queries, preferred_element_type=jnp.float32)
        / head_root
    )
    grad_project = jnp.concatenate(
        [
            grad_queries.reshape(row_count, channels),
            grad_keys.reshape(row_count, channels),
            grad_values.reshape(row_count, channels),
        ],
        axis=-1,
    ).astype(jnp.bfloat16)
    grad_attend = product_back(grad_project, qkv_w).reshape(images, pixels, channels)
    attend_back = jax.vjp(attend_piece, residual, gain_rows, bias_rows)[1]
    grad_from_norm, gain_attend, bias_attend = attend_back(grad_attend)
    grad_resid = grad_out + grad_from_norm
    flat_resid = grad_resid.astype(jnp.bfloat16).reshape(row_count, channels)
    grad_middle = columns_back(product_back(flat_resid, conv_out_w), images, channels)
    middle_back = jax.vjp(middle_piece, conv_one, scale_shift, gain_rows, bias_rows)[1]
    grad_conv, grad_scale, gain_middle, bias_middle = middle_back(grad_middle)
    grad_conv_b = grad_conv.astype(jnp.bfloat16).reshape(row_count, channels)
    grad_scale_b = grad_scale.astype(jnp.bfloat16)
    grad_embedding = product_back(grad_scale_b, embed_w)
    grad_joined = columns_back(product_back(grad_conv_b, conv_in_w), images, 2 * channels)
    hidden = paired[..., :channels].astype(jnp.float32)
    skipped = paired[..., channels:].astype(jnp.float32)
    input_back = jax.vjp(
        partial(input_piece, decoder_flag=decoder_flag), hidden, skipped, gain_rows, bias_rows
    )[1]
    grad_hidden, grad_skipped, gain_input, bias_input = input_back(
        (grad_joined[..., :channels], grad_joined[..., channels:])
    )
    grad_paired = product_back(flat_resid, skip_w).reshape(images, pixels, 2 * channels)
    grad_hidden = grad_hidden + jnp.where(is_decoder, grad_paired[..., :channels], grad_resid)
    grad_skipped = grad_skipped + grad_paired[..., channels:]
    gain_part = gain_attend + gain_middle + gain_input
    bias_part = bias_attend + bias_middle + bias_input
    stored = (grad_conv_b, grad_scale_b, flat_resid, grad_project, grad_top, grad_embedding)
    return (grad_hidden, grad_skipped, gain_part, bias_part, stored)


def on_device(
    level_input,
    cotangent,
    class_table,
    conv_in,
    conv_out,
    embed_proj,
    skip_proj,
    qkv_proj,
    out_proj,
    gains,
    biases,
    noise_pairs,
    classes,
):
    sections = lax.axis_size("section")
    section_id = lax.axis_index("section")
    ticks = MICRO + sections - 1
    is_decoder = section_id >= sections // 2
    decoder_flag = is_decoder.astype(jnp.float32)
    inputs_full, grads_full = (
        lax.all_gather(level_input, "section", axis=2, tiled=True),
        lax.all_gather(cotangent, "section", axis=2, tiled=True),
    )
    gathered = (
        lax.all_gather(conv_in, "dp", axis=1, tiled=True),
        lax.all_gather(conv_out, "dp", axis=1, tiled=True),
        lax.all_gather(embed_proj, "dp", axis=1, tiled=True),
        lax.all_gather(skip_proj, "dp", axis=1, tiled=True),
        lax.all_gather(qkv_proj, "dp", axis=1, tiled=True),
        lax.all_gather(out_proj, "dp", axis=1, tiled=True),
        lax.all_gather(gains, "dp", axis=1, tiled=True),
        lax.all_gather(biases, "dp", axis=1, tiled=True),
        lax.all_gather(class_table, "dp", axis=1, tiled=True),
    )
    weights_fwd = unpack_weights(gathered)
    table_full = gathered[8]
    images = level_input.shape[1]
    head_count = WIDTH // HEAD_DIM
    row_count = images * PIXELS
    grid_shape = (MICRO, images, PIXELS, WIDTH)
    kept_init = (
        jnp.zeros((MICRO, images, PIXELS, 2 * WIDTH), jnp.bfloat16),
        jnp.zeros(grid_shape, jnp.float32),
        jnp.zeros((MICRO, images, 2 * WIDTH), jnp.float32),
        jnp.zeros((MICRO, images, EMBED), jnp.bfloat16),
        jnp.zeros(grid_shape, jnp.bfloat16),
        jnp.zeros((MICRO, images, PIXELS, 2 * WIDTH), jnp.bfloat16),
        jnp.zeros(grid_shape, jnp.float32),
        jnp.zeros((MICRO, row_count, WIDTH), jnp.bfloat16),
        jnp.zeros((MICRO, row_count, 3 * WIDTH), jnp.bfloat16),
        jnp.zeros((MICRO, images, head_count, PIXELS, 1), jnp.float32),
        jnp.zeros((MICRO, row_count, WIDTH), jnp.bfloat16),
    )

    def forward_tick(tick_index, state_now):
        incoming, skip_store, kept_store, result_store = state_now
        micro_now = tick_index - section_id
        is_active = jnp.logical_and(micro_now >= 0, micro_now < MICRO)
        slot_index = jnp.clip(micro_now, 0, MICRO - 1)
        level_now = lax.dynamic_index_in_dim(inputs_full, slot_index, 0, keepdims=False)
        hidden_b = jnp.where(section_id == 0, level_now, incoming)
        skipped_b = lax.dynamic_index_in_dim(skip_store, slot_index, 0, keepdims=False)

        def forward_active_pass(stores):
            kept_now, results_now = stores
            pair_ids = lax.dynamic_index_in_dim(noise_pairs, slot_index, 0, keepdims=False)
            class_ids = lax.dynamic_index_in_dim(classes, slot_index, 0, keepdims=False)
            embedding = jax.nn.silu(embed_rows(pair_ids, class_ids, table_full)[0])
            result, kept_list = section_forward(
                hidden_b, skipped_b, embedding, weights_fwd, decoder_flag, is_decoder
            )
            kept_now = tuple(
                (
                    lax.dynamic_update_index_in_dim(buffers, entry_now, slot_index, 0)
                    for buffers, entry_now in zip(kept_now, kept_list)
                )
            )
            results_now = lax.dynamic_update_index_in_dim(results_now, result, slot_index, 0)
            return (result.astype(jnp.bfloat16), kept_now, results_now)

        def forward_resting_pass(stores):
            return (jnp.zeros_like(incoming), stores[0], stores[1])

        outgoing, kept_store, result_store = lax.cond(
            is_active, forward_active_pass, forward_resting_pass, (kept_store, result_store)
        )
        incoming = passed_along(outgoing, "section", 1)
        every_section = lax.all_gather(outgoing[None], "section", axis=0, tiled=True)
        mirrored = lax.dynamic_index_in_dim(
            every_section, sections - 1 - section_id, 0, keepdims=False
        )
        source_micro = tick_index - (sections - 1 - section_id)
        takes_skip = is_decoder & (source_micro >= 0) & (source_micro < MICRO)
        source_slot = jnp.clip(source_micro, 0, MICRO - 1)
        skip_store = jnp.where(
            takes_skip,
            lax.dynamic_update_index_in_dim(skip_store, mirrored, source_slot, 0),
            skip_store,
        )
        return (incoming, skip_store, kept_store, result_store)

    forward_init = (
        jnp.zeros((images, PIXELS, WIDTH), jnp.bfloat16),
        jnp.zeros(grid_shape, jnp.bfloat16),
        kept_init,
        jnp.zeros(grid_shape, jnp.float32),
    )
    forward_done = lax.fori_loop(0, ticks, forward_tick, forward_init)
    kept_store = forward_done[2]
    result_store = forward_done[3]
    grad_init = (
        jnp.zeros((MICRO, row_count, WIDTH), jnp.bfloat16),
        jnp.zeros((MICRO, images, 2 * WIDTH), jnp.bfloat16),
        jnp.zeros((MICRO, row_count, WIDTH), jnp.bfloat16),
        jnp.zeros((MICRO, row_count, 3 * WIDTH), jnp.bfloat16),
        jnp.zeros((MICRO, row_count, WIDTH), jnp.bfloat16),
        jnp.zeros((MICRO, images, EMBED), jnp.float32),
    )

    def backward_tick(tick_index, state_now):
        incoming_grad, skip_grads, grad_store, gain_sum, bias_sum, input_store = state_now
        micro_now = tick_index - (sections - 1 - section_id)
        is_active = jnp.logical_and(micro_now >= 0, micro_now < MICRO)
        slot_index = jnp.clip(micro_now, 0, MICRO - 1)
        top_now = lax.dynamic_index_in_dim(grads_full, slot_index, 0, keepdims=False)
        from_next = jnp.where(section_id == sections - 1, top_now, incoming_grad).astype(
            jnp.float32
        )
        from_skip = lax.dynamic_index_in_dim(skip_grads, slot_index, 0, keepdims=False).astype(
            jnp.float32
        )
        grad_out = from_next + jnp.where(is_decoder, 0.0, from_skip)

        def backward_active_pass(stores):
            grads_now, gain_now, bias_now, inputs_now = stores
            kept_list = tuple(
                (
                    lax.dynamic_index_in_dim(buffers, slot_index, 0, keepdims=False)
                    for buffers in kept_store
                )
            )
            grad_hidden, grad_skipped, gain_part, bias_part, stored = section_backward(
                grad_out, kept_list, weights_fwd, decoder_flag, is_decoder
            )
            grads_now = tuple(
                (
                    lax.dynamic_update_index_in_dim(buffers, entry_now, slot_index, 0)
                    for buffers, entry_now in zip(grads_now, stored)
                )
            )
            inputs_now = lax.dynamic_update_index_in_dim(inputs_now, grad_hidden, slot_index, 0)
            return (
                grad_hidden.astype(jnp.bfloat16),
                grad_skipped.astype(jnp.bfloat16),
                grads_now,
                gain_now + gain_part,
                bias_now + bias_part,
                inputs_now,
            )

        def backward_resting_pass(stores):
            return (
                jnp.zeros_like(incoming_grad),
                jnp.zeros_like(incoming_grad),
                stores[0],
                stores[1],
                stores[2],
                stores[3],
            )

        send_back, send_skip, grad_store, gain_sum, bias_sum, input_store = lax.cond(
            is_active,
            backward_active_pass,
            backward_resting_pass,
            (grad_store, gain_sum, bias_sum, input_store),
        )
        incoming_grad = passed_along(send_back, "section", -1)
        every_section = lax.all_gather(send_skip[None], "section", axis=0, tiled=True)
        mirrored = lax.dynamic_index_in_dim(
            every_section, sections - 1 - section_id, 0, keepdims=False
        )
        source_micro = tick_index - section_id
        takes_skip = jnp.logical_not(is_decoder) & (source_micro >= 0) & (source_micro < MICRO)
        source_slot = jnp.clip(source_micro, 0, MICRO - 1)
        skip_grads = jnp.where(
            takes_skip,
            lax.dynamic_update_index_in_dim(skip_grads, mirrored, source_slot, 0),
            skip_grads,
        )
        return (incoming_grad, skip_grads, grad_store, gain_sum, bias_sum, input_store)

    backward_init = (
        jnp.zeros((images, PIXELS, WIDTH), jnp.bfloat16),
        jnp.zeros(grid_shape, jnp.bfloat16),
        grad_init,
        jnp.zeros((4, WIDTH), jnp.float32),
        jnp.zeros((12, WIDTH), jnp.float32),
        jnp.zeros(grid_shape, jnp.float32),
    )
    backward_done = lax.fori_loop(0, ticks, backward_tick, backward_init)
    grad_store, gain_sum, bias_sum, input_store = (
        backward_done[2],
        backward_done[3],
        backward_done[4],
        backward_done[5],
    )
    (
        grad_conv_all,
        grad_scale_all,
        grad_resid_all,
        grad_project_all,
        grad_top_all,
        grad_embed_all,
    ) = grad_store
    all_rows = MICRO * row_count
    all_images = MICRO * images
    conv_in_grad = outer_sum(
        columns(kept_store[0].reshape(all_images, PIXELS, 2 * WIDTH)),
        grad_conv_all.reshape(all_rows, WIDTH),
    )
    conv_out_grad = outer_sum(
        columns(kept_store[4].reshape(all_images, PIXELS, WIDTH)),
        grad_resid_all.reshape(all_rows, WIDTH),
    )
    embed_grad = outer_sum(
        kept_store[3].reshape(all_images, EMBED), grad_scale_all.reshape(all_images, 2 * WIDTH)
    )
    skip_grad = decoder_flag * outer_sum(
        kept_store[5].reshape(all_rows, 2 * WIDTH), grad_resid_all.reshape(all_rows, WIDTH)
    )
    qkv_grad = outer_sum(
        kept_store[7].reshape(all_rows, WIDTH), grad_project_all.reshape(all_rows, 3 * WIDTH)
    )
    out_grad = outer_sum(
        kept_store[10].reshape(all_rows, WIDTH), grad_top_all.reshape(all_rows, WIDTH)
    )
    conv_total = column_total(grad_conv_all)
    scale_total = column_total(grad_scale_all)
    resid_total = column_total(grad_resid_all)
    project_total = column_total(grad_project_all)
    top_total = column_total(grad_top_all)
    bias_grad = jnp.stack(
        [
            bias_sum[0],
            bias_sum[1],
            conv_total,
            scale_total[:WIDTH],
            scale_total[WIDTH:],
            bias_sum[5],
            resid_total,
            decoder_flag * resid_total,
            bias_sum[8],
            project_total[:WIDTH],
            project_total[2 * WIDTH :],
            top_total,
        ]
    )
    pre_all, onehot_all = embed_rows(
        noise_pairs.reshape(all_images, 2), classes.reshape(all_images), table_full
    )
    silu_back = jax.vjp(jax.nn.silu, pre_all)[1]
    grad_pre = silu_back(grad_embed_all.reshape(all_images, EMBED))[0]
    table_grad = lax.dot_general(
        onehot_all.astype(jnp.float32),
        grad_pre,
        (((0,), (0,)), ((), ())),
        precision=lax.Precision.HIGHEST,
        preferred_element_type=jnp.float32,
    )
    summed = (
        lax.psum_scatter(
            conv_in_grad[None].astype(jnp.bfloat16), "dp", scatter_dimension=1, tiled=True
        ).astype(jnp.float32),
        lax.psum_scatter(
            conv_out_grad[None].astype(jnp.bfloat16), "dp", scatter_dimension=1, tiled=True
        ).astype(jnp.float32),
        lax.psum_scatter(
            embed_grad[None].astype(jnp.bfloat16), "dp", scatter_dimension=1, tiled=True
        ).astype(jnp.float32),
        lax.psum_scatter(
            skip_grad[None].astype(jnp.bfloat16), "dp", scatter_dimension=1, tiled=True
        ).astype(jnp.float32),
        lax.psum_scatter(
            qkv_grad[None].astype(jnp.bfloat16), "dp", scatter_dimension=1, tiled=True
        ).astype(jnp.float32),
        lax.psum_scatter(
            out_grad[None].astype(jnp.bfloat16), "dp", scatter_dimension=1, tiled=True
        ).astype(jnp.float32),
        lax.psum_scatter(
            gain_sum.reshape(1, 4 * WIDTH).astype(jnp.bfloat16),
            "dp",
            scatter_dimension=1,
            tiled=True,
        ).astype(jnp.float32),
        lax.psum_scatter(
            bias_grad.reshape(1, 12 * WIDTH).astype(jnp.bfloat16),
            "dp",
            scatter_dimension=1,
            tiled=True,
        ).astype(jnp.float32),
        lax.psum_scatter(
            table_grad.astype(jnp.bfloat16), "dp", scatter_dimension=1, tiled=True
        ).astype(jnp.float32),
    )
    table_part = lax.psum(summed[8].astype(jnp.bfloat16), "section").astype(jnp.float32)
    output_sum, input_sum = (
        lax.psum_scatter(
            jnp.where(section_id == sections - 1, result_store, 0.0).astype(jnp.bfloat16),
            "section",
            scatter_dimension=2,
            tiled=True,
        ).astype(jnp.float32),
        lax.psum_scatter(
            jnp.where(section_id == 0, input_store, 0.0).astype(jnp.bfloat16),
            "section",
            scatter_dimension=2,
            tiled=True,
        ).astype(jnp.float32),
    )
    return (
        output_sum.astype(jnp.bfloat16),
        input_sum,
        table_part,
        summed[0],
        summed[1],
        summed[2],
        summed[3],
        summed[4],
        summed[5],
        summed[6],
        summed[7],
    )


def solution(mesh):
    placed = (
        P(None, "dp", "section", None),
        P(None, "dp", "section", None),
        P(None, "dp"),
        P("section", "dp", None),
        P("section", "dp", None),
        P("section", "dp", None),
        P("section", "dp", None),
        P("section", "dp", None),
        P("section", "dp", None),
        P("section", "dp"),
        P("section", "dp"),
        P(None, "dp", None),
        P(None, "dp"),
    )
    return jax.shard_map(
        on_device,
        mesh=mesh,
        in_specs=placed,
        out_specs=(
            P(None, "dp", "section", None),
            P(None, "dp", "section", None),
            P(None, "dp"),
            P("section", "dp", None),
            P("section", "dp", None),
            P("section", "dp", None),
            P("section", "dp", None),
            P("section", "dp", None),
            P("section", "dp", None),
            P("section", "dp"),
            P("section", "dp"),
        ),
        check_vma=False,
    )
```

profile of v0, /device:TPU:0, one launch (start us, length us, event | category | flops | bytes accessed | tf_op | source)
XLA Modules:
  0.0 2756.7 jit_solution(6040735370493856327)
XLA Ops:
  15.1 63.1 %all-reduce.34 = (bf16[3072]{0:T(1024)(128)(2,1)S(1)}, bf16[9216]{0:T(1024)(128)(2,1)S(1)}) all-reduce(bf16[3072]{0:T(1024)(128)(2,1)S(1)} %dynamic-update-slice.10, bf16[9216]{0:T(1024)(128)(2,1)S(1)} %dynamic-update-slice.11), channel_id=1, replica_groups=mesh['section'=2,'dp'=16] {'dp'}, use_global_device_ids=true, to_apply=%add.32 | all-reduce | flops 12288 | bytes 49152
  80.9 8.3 all_gather.51
  89.2 6.4 all_gather.61
  100.4 35.6 %all-gather.18.cloned.1.call-done = bf16[1,768,1536]{2,1,0:T(8,128)(2,1)} async-done(((bf16[1,48,1536]{2,1,0:T(8,128)(2,1)}), bf16[1,768,1536]{2,1,0:T(8,128)(2,1)}) %all-gather.18.cloned.1.call-update) | async-done | bytes 2359312 | tf_op jit(solution)/shard_map/all_gather | solution.py:328
  135.9 43.3 %all-gather.22.cloned.1.call-done = bf16[1,1536,768]{2,1,0:T(8,128)(2,1)} async-done(((bf16[1,96,768]{2,1,0:T(8,128)(2,1)}), bf16[1,1536,768]{2,1,0:T(8,128)(2,1)}) %all-gather.22.cloned.1.call-update) | async-done | bytes 2359312 | tf_op jit(solution)/shard_map/all_gather | solution.py:329
  179.2 48.1 %all-gather.24.cloned.1.call-done = bf16[1,768,2304]{2,1,0:T(8,128)(2,1)} async-done(((bf16[1,48,2304]{2,1,0:T(8,128)(2,1)}), bf16[1,768,2304]{2,1,0:T(8,128)(2,1)}) %all-gather.24.cloned.1.call-update) | async-done | bytes 3538960 | tf_op jit(solution)/shard_map/all_gather | solution.py:330
  227.4 89.9 %all-gather.20.cloned.1.call-done = bf16[1,6912,768]{2,1,0:T(8,128)(2,1)} async-done(((bf16[1,432,768]{2,1,0:T(8,128)(2,1)}), bf16[1,6912,768]{2,1,0:T(8,128)(2,1)}) %all-gather.20.cloned.1.call-update) | async-done | bytes 10616848 | tf_op jit(solution)/shard_map/all_gather | solution.py:327
  317.2 109.9 %all-gather.14.cloned.1.call-done = bf16[1,13824,768]{2,1,0:T(8,128)(2,1)} async-done(((bf16[1,864,768]{2,1,0:T(8,128)(2,1)}), bf16[1,13824,768]{2,1,0:T(8,128)(2,1)}) %all-gather.14.cloned.1.call-update) | async-done | bytes 21233680 | tf_op jit(solution)/shard_map/all_gather | solution.py:326
  437.8 488.4 %while.76 = (s32[]{:T(128)}, bf16[1,64,768]{2,1,0:T(8,128)(2,1)}, bf16[4,1,64,768]{3,2,1,0:T(8,128)(2,1)}, bf16[4,1,64,1536]{3,2,1,0:T(8,128)(2,1)}, f32[4,1,64,...) while((s32[]{:T(128)}, bf16[1,64,768]{2,1,0:T(8,128)(2,1)}, ...), condition=%wide.region_21.22_spmd, body=%wide.region_0.21_spmd.sunk | while | flops 2517693184 | bytes 70438664 | solution.py:409
  437.8 86.8 %conditional.4 = (bf16[1,64,768]{2,1,0:T(8,128)(2,1)}, bf16[4,1,64,1536]{3,2,1,0:T(8,128)(2,1)}, f32[4,1,64,768]{3,2,1,0:T(8,128)}, f32[4,1,1536]{2,1,0:T(1,128)...) conditional(s32[]{:T(128)} %convert_element_type.821, ...), branch_computations={%region_1.1_spmd, %region_2.20_spmd} | conditional | flops 2517644032 | bytes 69454312 | solution.py:385
  473.4 10.3 fusion.227
  494.4 7.3 fusion.228
  526.5 5.9 all-gather.4
  534.0 86.7 %conditional.4 = (bf16[1,64,768]{2,1,0:T(8,128)(2,1)}, bf16[4,1,64,1536]{3,2,1,0:T(8,128)(2,1)}, f32[4,1,64,768]{3,2,1,0:T(8,128)}, f32[4,1,1536]{2,1,0:T(1,128)...) conditional(s32[]{:T(128)} %convert_element_type.821, ...), branch_computations={%region_1.1_spmd, %region_2.20_spmd} | conditional | flops 2517644032 | bytes 69454312 | solution.py:385
  569.5 10.3 fusion.227
  590.6 7.3 fusion.228
  620.7 4.4 collective-permute-start
  625.1 5.6 all-gather.4
  632.3 86.7 %conditional.4 = (bf16[1,64,768]{2,1,0:T(8,128)(2,1)}, bf16[4,1,64,1536]{3,2,1,0:T(8,128)(2,1)}, f32[4,1,64,768]{3,2,1,0:T(8,128)}, f32[4,1,1536]{2,1,0:T(1,128)...) conditional(s32[]{:T(128)} %convert_element_type.821, ...), branch_computations={%region_1.1_spmd, %region_2.20_spmd} | conditional | flops 2517644032 | bytes 69454312 | solution.py:385
  667.8 10.3 fusion.227
  688.8 7.3 fusion.228
  719.0 4.1 collective-permute-start
  723.1 5.6 all-gather.4
  730.3 86.7 %conditional.4 = (bf16[1,64,768]{2,1,0:T(8,128)(2,1)}, bf16[4,1,64,1536]{3,2,1,0:T(8,128)(2,1)}, f32[4,1,64,768]{3,2,1,0:T(8,128)}, f32[4,1,1536]{2,1,0:T(1,128)...) conditional(s32[]{:T(128)} %convert_element_type.821, ...), branch_computations={%region_1.1_spmd, %region_2.20_spmd} | conditional | flops 2517644032 | bytes 69454312 | solution.py:385
  765.8 10.3 fusion.227
  786.8 7.3 fusion.228
  817.0 4.0 collective-permute-start
  821.0 5.6 all-gather.4
  828.8 90.1 %collective-permute-start = (bf16[1,64,768]{2,1,0:T(8,128)(2,1)}, bf16[1,64,768]{2,1,0:T(8,128)(2,1)}, u32[]{:S(2)}, u32[]{:S(2)}) collective-permute-start(bf16[1,64,768]{2,1,0:T(8,128)(2,1)} %get-tuple-element.2792), channel_id=1, source_target_pairs={{0,16},{1,17},{2,18},{3,19},{4,20},{5,21},{6,22},{7,23},{8,24},{9,... | collective-permute-start | bytes 294920 | tf_op jit(solution)/shard_map/while/body/eval_jaxpr/ppermute | solution.py:28
  919.0 5.6 all-gather.4
  933.5 970.3 %while.77 = (s32[]{:T(128)}, bf16[1,64,768]{2,1,0:T(8,128)(2,1)}, bf16[4,1,64,768]{3,2,1,0:T(8,128)(2,1)}, bf16[4,64,768]{2,1,0:T(8,128)(2,1)}, bf16[4,1,1536]{2...) while((s32[]{:T(128)}, bf16[1,64,768]{2,1,0:T(8,128)(2,1)}, ...), condition=%wide.region_69.70_spmd, body=%wide.region_23.69_spmd.sunk | while | flops 2539750912 | bytes 102959152 | solution.py:501
  937.9 187.1 %all-gather.5 = bf16[2,64,768]{2,1,0:T(8,128)(2,1)} all-gather(bf16[1,64,768]{2,1,0:T(8,128)(2,1)} %get-tuple-element.2840), channel_id=3, replica_groups=mesh['section'=2,'dp'=16] {'section'}, dimensions={0}, use_global_device_ids=true | all-gather | bytes 294912 | tf_op jit(solution)/shard_map/while/body/eval_jaxpr/all_gather | solution.py:479
  1128.2 181.4 %conditional.5 = (bf16[1,64,768]{2,1,0:T(8,128)(2,1)}, bf16[1,64,768]{2,1,0:T(8,128)(2,1)}, bf16[4,64,768]{2,1,0:T(8,128)(2,1)}, bf16[4,1,1536]{2,1,0:T(2,128)(2...) conditional(s32[]{:T(128)} %convert_element_type.823, ...), branch_computations={%region_24.24_spmd, %region_25.68_spmd} | conditional | flops 2539603456 | bytes 101581592 | solution.py:472
  1228.9 7.5 convolution_bitcast_fusion.2
  1259.7 10.8 convolution_bitcast_fusion
  1310.9 8.3 all-gather.5
  1322.4 181.4 %conditional.5 = (bf16[1,64,768]{2,1,0:T(8,128)(2,1)}, bf16[1,64,768]{2,1,0:T(8,128)(2,1)}, bf16[4,64,768]{2,1,0:T(8,128)(2,1)}, bf16[4,1,1536]{2,1,0:T(2,128)(2...) conditional(s32[]{:T(128)} %convert_element_type.823, ...), branch_computations={%region_24.24_spmd, %region_25.68_spmd} | conditional | flops 2539603456 | bytes 101581592 | solution.py:472
  1423.2 7.5 convolution_bitcast_fusion.2
  1454.0 10.8 convolution_bitcast_fusion
  1505.2 8.3 all-gather.5
  1516.7 181.4 %conditional.5 = (bf16[1,64,768]{2,1,0:T(8,128)(2,1)}, bf16[1,64,768]{2,1,0:T(8,128)(2,1)}, bf16[4,64,768]{2,1,0:T(8,128)(2,1)}, bf16[4,1,1536]{2,1,0:T(2,128)(2...) conditional(s32[]{:T(128)} %convert_element_type.823, ...), branch_computations={%region_24.24_spmd, %region_25.68_spmd} | conditional | flops 2539603456 | bytes 101581592 | solution.py:472
  1594.9 3.6 fusion.218
  1617.4 7.5 convolution_bitcast_fusion.2
  1648.2 10.8 convolution_bitcast_fusion
  1699.4 8.3 all-gather.5
  1710.9 181.4 %conditional.5 = (bf16[1,64,768]{2,1,0:T(8,128)(2,1)}, bf16[1,64,768]{2,1,0:T(8,128)(2,1)}, bf16[4,64,768]{2,1,0:T(8,128)(2,1)}, bf16[4,1,1536]{2,1,0:T(2,128)(2...) conditional(s32[]{:T(128)} %convert_element_type.823, ...), branch_computations={%region_24.24_spmd, %region_25.68_spmd} | conditional | flops 2539603456 | bytes 101581592 | solution.py:472
  1789.1 3.6 fusion.218
  1811.7 7.5 convolution_bitcast_fusion.2
  1842.4 10.8 convolution_bitcast_fusion
  1893.6 8.3 all-gather.5
  1919.0 47.0 %reduce-scatter.20.cloned.1.call-done = bf16[1000,48]{0,1:T(8,128)(2,1)} async-done(((bf16[1000,768]{0,1:T(8,128)(2,1)}), bf16[1000,48]{0,1:T(8,128)(2,1)}) %reduce-scatter.20.cloned.1.call-update) | async-done | bytes 96016 | tf_op jit(solution)/shard_map/reduce_scatter | solution.py:602
  1976.2 5.8 fusion.194
  1993.4 12.2 fusion.193
  2007.4 18.2 reduce-scatter.34.cloned.1.call-done
  2027.1 64.2 %reduce-scatter.36.cloned.1.call-done = bf16[576,1]{1,0:T(8,128)(2,1)} async-done(((bf16[9216,1]{1,0:T(8,128)(2,1)}), bf16[576,1]{1,0:T(8,128)(2,1)}) %reduce-scatter.36.cloned.1.call-update) | async-done | bytes 1168
  2092.9 13.5 reduce-scatter.18.cloned.1.call-done
  2108.0 60.4 %reduce-scatter.32.cloned.1.call-done = bf16[1,48,768]{2,1,0:T(8,128)(2,1)} async-done(((bf16[1,768,768]{2,1,0:T(8,128)(2,1)}), bf16[1,48,768]{2,1,0:T(8,128)(2,1)}) %reduce-scatter.32.cloned.1.call-update) | async-done | bytes 73744 | tf_op jit(solution)/shard_map/reduce_scatter | solution.py:587
  2170.0 20.8 all-reduce.37.cloned.1.call-done
  2192.4 65.0 %reduce-scatter.28.cloned.1.call-done = bf16[1,96,768]{2,1,0:T(8,128)(2,1)} async-done(((bf16[1,1536,768]{2,1,0:T(8,128)(2,1)}), bf16[1,96,768]{2,1,0:T(8,128)(2,1)}) %reduce-scatter.28.cloned.1.call-update) | async-done | bytes 147472 | tf_op jit(solution)/shard_map/reduce_scatter | solution.py:581
  2259.0 65.0 %reduce-scatter.26.cloned.1.call-done = bf16[1,48,1536]{2,1,0:T(8,128)(2,1)} async-done(((bf16[1,768,1536]{2,1,0:T(8,128)(2,1)}), bf16[1,48,1536]{2,1,0:T(8,128)(2,1)}) %reduce-scatter.26.cloned.1.call-update) | async-done | bytes 147472 | tf_op jit(solution)/shard_map/reduce_scatter | solution.py:578
  2325.7 69.3 %reduce-scatter.30.cloned.1.call-done = bf16[1,48,2304]{2,1,0:T(8,128)(2,1)} async-done(((bf16[1,768,2304]{2,1,0:T(8,128)(2,1)}), bf16[1,48,2304]{2,1,0:T(8,128)(2,1)}) %reduce-scatter.30.cloned.1.call-update) | async-done | bytes 221200 | tf_op jit(solution)/shard_map/reduce_scatter | solution.py:584
  2396.7 121.4 %reduce-scatter.24.cloned.1.call-done = bf16[1,432,768]{2,1,0:T(8,128)(2,1)} async-done(((bf16[1,6912,768]{2,1,0:T(8,128)(2,1)}), bf16[1,432,768]{2,1,0:T(8,128)(2,1)}) %reduce-scatter.24.cloned.1.call-update) | async-done | bytes 663568 | tf_op jit(solution)/shard_map/reduce_scatter | solution.py:575
  2520.3 214.2 %reduce-scatter.22.cloned.1.call-done = bf16[1,864,768]{2,1,0:T(8,128)(2,1)} async-done(((bf16[1,13824,768]{2,1,0:T(8,128)(2,1)}), bf16[1,864,768]{2,1,0:T(8,128)(2,1)}) %reduce-scatter.22.cloned.1.call-update) | async-done | bytes 1327120 | tf_op jit(solution)/shard_map/reduce_scatter | solution.py:572
  2737.5 12.2 reduce-scatter.16.cloned.1.call-done
  (1517 shorter events, 1043.8 us)
Async XLA Ops:
  7.2 73.7 %copy-start.51 = (bf16[4,1,32,768]{3,2,1,0:T(8,128)(2,1)S(1)}, bf16[4,1,32,768]{3,2,1,0:T(8,128)(2,1)}, u32[]{:S(2)}) copy-start(bf16[4,1,32,768]{3,2,1,0:T(8,128)(2,1)} %param.21) | copy-start | bytes 589828
  7.2 82.0 %copy-start.52 = (bf16[4,1,32,768]{3,2,1,0:T(8,128)(2,1)S(1)}, bf16[4,1,32,768]{3,2,1,0:T(8,128)(2,1)}, u32[]{:S(2)}) copy-start(bf16[4,1,32,768]{3,2,1,0:T(8,128)(2,1)} %param.22) | copy-start | bytes 589828
  7.2 88.6 %all-gather.16.cloned.1.call-start = ((), (), s32[]{:S(2)}) async-start(), calls=%async_computation.12 | async-start | bytes 1671168 | tf_op jit(solution)/shard_map/all_gather | solution.py:334
  8.0 92.4 %all-gather.26.cloned.1.call-start = ((), (), s32[]{:S(2)}) async-start(), calls=%async_computation.17 | async-start | bytes 1253376 | tf_op jit(solution)/shard_map/all_gather | solution.py:331
  8.7 127.2 %all-gather.18.cloned.1.call-start = ((), (), s32[]{:S(2)}) async-start(), calls=%async_computation.13 | async-start | bytes 2506752 | tf_op jit(solution)/shard_map/all_gather | solution.py:328
  9.5 169.8 %all-gather.22.cloned.1.call-start = ((), (), s32[]{:S(2)}) async-start(), calls=%async_computation.15 | async-start | bytes 2506752 | tf_op jit(solution)/shard_map/all_gather | solution.py:329
  10.0 217.3 %all-gather.24.cloned.1.call-start = ((), (), s32[]{:S(2)}) async-start(), calls=%async_computation.16 | async-start | bytes 3760128 | tf_op jit(solution)/shard_map/all_gather | solution.py:330
  10.6 306.6 %all-gather.20.cloned.1.call-start = ((), (), s32[]{:S(2)}) async-start(), calls=%async_computation.14 | async-start | bytes 11280384 | tf_op jit(solution)/shard_map/all_gather | solution.py:327
  11.2 415.9 %all-gather.14.cloned.1.call-start = ((), (), s32[]{:S(2)}) async-start(), calls=%async_computation.11 | async-start | bytes 22560768 | tf_op jit(solution)/shard_map/all_gather | solution.py:326
  11.9 1954.0 %reduce-scatter.20.cloned.1.call-start = ((), (), s32[]{:S(2)}) async-start(), calls=%async_computation.20 | async-start | bytes 1671168 | tf_op jit(solution)/shard_map/reduce_scatter | solution.py:602
  511.9 10.6 copy-start.35
  511.9 10.6 copy-start.40
  511.9 10.6 copy-start.41
  511.9 10.6 copy-start.42
  524.6 9.5 collective-permute-start
  608.1 10.6 copy-start.35
  608.1 10.6 copy-start.40
  608.1 10.6 copy-start.41
  608.1 10.6 copy-start.42
  620.7 11.6 collective-permute-start
  706.4 10.6 copy-start.35
  706.4 10.6 copy-start.40
  706.4 10.6 copy-start.41
  706.4 10.6 copy-start.42
  719.0 11.3 collective-permute-start
  804.4 10.6 copy-start.35
  804.4 10.6 copy-start.40
  804.4 10.6 copy-start.41
  804.4 10.6 copy-start.42
  817.0 11.2 collective-permute-start
  828.8 97.3 %collective-permute-start = (bf16[1,64,768]{2,1,0:T(8,128)(2,1)}, bf16[1,64,768]{2,1,0:T(8,128)(2,1)}, u32[]{:S(2)}, u32[]{:S(2)}) collective-permute-start(bf16[1,64,768]{2,1,0:T(8,128)(2,1)} %get-tuple-element.2792), channel_id=1, source_target_pairs={{0,16},{1,17},{2,18},{3,19},{4,20},{5,21},{6,22},{7,23},{8,24},{9,... | collective-permute-start | bytes 294920 | tf_op jit(solution)/shard_map/while/body/eval_jaxpr/ppermute | solution.py:28
  936.6 190.0 %collective-permute-start.1 = (bf16[1,64,768]{2,1,0:T(8,128)(2,1)}, bf16[1,64,768]{2,1,0:T(8,128)(2,1)}, u32[]{:S(2)}, u32[]{:S(2)}) collective-permute-start(bf16[1,64,768]{2,1,0:T(8,128)(2,1)} %get-tuple-element.2839), channel_id=1, source_target_pairs={{16,0},{17,1},{18,2},{19,3},{20,4},{21,5},{22,6},{23,7},{24,8},{25... | collective-permute-start | bytes 294920 | tf_op jit(solution)/shard_map/while/body/eval_jaxpr/ppermute | solution.py:28
  1259.7 10.8 copy-start.15
  1259.7 10.8 copy-start.39
  1259.7 10.8 copy-start.49
  1309.6 11.2 collective-permute-start.1
  1453.9 10.8 copy-start.15
  1453.9 10.8 copy-start.39
  1454.0 10.8 copy-start.49
  1466.9 8.0 copy-start.27
  1503.9 11.2 collective-permute-start.1
  1648.2 10.8 copy-start.15
  1648.2 10.8 copy-start.39
  1648.2 10.8 copy-start.49
  1661.1 8.0 copy-start.27
  1698.1 11.2 collective-permute-start.1
  1842.4 10.8 copy-start.15
  1842.4 10.8 copy-start.39
  1842.4 10.8 copy-start.49
  1855.4 8.0 copy-start.27
  1855.4 8.0 copy-start.31
  1892.3 11.2 collective-permute-start.1
  1907.3 118.3 %reduce-scatter.34.cloned.1.call-start = ((), (), s32[]{:S(2)}) async-start(), calls=%async_computation.28 | async-start | bytes 835584
  1913.8 177.4 %reduce-scatter.36.cloned.1.call-start = ((), (), s32[]{:S(2)}) async-start(), calls=%async_computation.29 | async-start | bytes 2506752
  1915.5 190.9 %reduce-scatter.18.cloned.1.call-start = ((), (), s32[]{:S(2)}) async-start(), calls=%async_computation.19 | async-start | bytes 589824 | tf_op jit(solution)/shard_map/reduce_scatter | solution.py:614
  1917.3 48.8 %copy-start.17 = (bf16[4,1,64,1536]{3,2,1,0:T(8,128)(2,1)S(1)}, bf16[4,1,64,1536]{3,2,1,0:T(8,128)(2,1)}, u32[]{:S(2)}) copy-start(bf16[4,1,64,1536]{3,2,1,0:T(8,128)(2,1)} %get-tuple-element.3164) | copy-start | bytes 2359300
  1917.3 251.2 %reduce-scatter.32.cloned.1.call-start = ((), (), s32[]{:S(2)}) async-start(), calls=%async_computation.27 | async-start | bytes 1253376 | tf_op jit(solution)/shard_map/reduce_scatter | solution.py:587
  1918.9 271.9 %all-reduce.37.cloned.1.call-start = ((), (), s32[]{:S(2)}) async-start(), calls=%async_computation.21 | async-start | bytes 196608 | tf_op jit(solution)/shard_map/psum | solution.py:606
  1966.0 291.4 %reduce-scatter.28.cloned.1.call-start = ((), (), s32[]{:S(2)}) async-start(), calls=%async_computation.25 | async-start | bytes 2506752 | tf_op jit(solution)/shard_map/reduce_scatter | solution.py:581
  1968.4 355.6 %reduce-scatter.26.cloned.1.call-start = ((), (), s32[]{:S(2)}) async-start(), calls=%async_computation.24 | async-start | bytes 2506752 | tf_op jit(solution)/shard_map/reduce_scatter | solution.py:578
  1971.6 423.4 %reduce-scatter.30.cloned.1.call-start = ((), (), s32[]{:S(2)}) async-start(), calls=%async_computation.26 | async-start | bytes 3760128 | tf_op jit(solution)/shard_map/reduce_scatter | solution.py:584
  1974.6 543.5 %reduce-scatter.24.cloned.1.call-start = ((), (), s32[]{:S(2)}) async-start(), calls=%async_computation.23 | async-start | bytes 11280384 | tf_op jit(solution)/shard_map/reduce_scatter | solution.py:575
  1982.0 752.5 %reduce-scatter.22.cloned.1.call-start = ((), (), s32[]{:S(2)}) async-start(), calls=%async_computation.22 | async-start | bytes 22560768 | tf_op jit(solution)/shard_map/reduce_scatter | solution.py:572
  2005.6 744.1 %reduce-scatter.16.cloned.1.call-start = ((), (), s32[]{:S(2)}) async-start(), calls=%async_computation.18 | async-start | bytes 589824 | tf_op jit(solution)/shard_map/reduce_scatter | solution.py:608
  (129 other events, 444.5 us)
Sparse Core Ops, SparseCore 0:
  10.4 42.6 all-gather.15
  55.3 37.0 all-gather.25
  94.7 41.1 all-gather.17
  138.1 41.0 all-gather.21
  181.3 45.9 all-gather.23
  229.5 87.6 all-gather.19
  318.8 108.2 all-gather.13
  1907.5 58.4 reduce-scatter.19
  1969.9 55.6 reduce-scatter.33
  2029.2 61.9 reduce-scatter.35
  2094.2 12.1 reduce-scatter.17
  2110.4 58.0 reduce-scatter.31
  2170.7 20.0 all-reduce.36
  2194.4 62.9 reduce-scatter.27
  2262.0 61.9 reduce-scatter.25
  2327.8 67.1 reduce-scatter.29
  2398.8 119.1 reduce-scatter.23
  2522.0 212.4 reduce-scatter.21
  2737.4 12.2 reduce-scatter.15
where the time goes:
time: 2790 us; the launch traced here: 2760 us
  waiting for transfers between devices  1100 us (39%)
  local copies, waits for them, and re-layouts  505 us (18%)
  other arithmetic  392 us (14%)
  blocking collectives  326 us (12%)
  matrix products  299 us (11%)
  starting transfers between devices  112 us (4%)
    all_gather x5, blocking collectives, backward_tick(): lax.all_gather(send_skip[None], 'section', axis=0, tiled=True)  220 us
    reduce_scatter x1, waiting for transfers between devices, on_device(): lax.psum_scatter(conv_in_grad[None].astype(jnp.bfloat16), 'dp', scatter_d...  214 us
    reduce_scatter x1, waiting for transfers between devices, on_device(): lax.psum_scatter(conv_out_grad[None].astype(jnp.bfloat16), 'dp', scatter_...  121 us
    dot_general x29, matrix products, product(): return jnp.dot(left_side, right_side, preferred_element_type=jnp.float32)  119 us
    dot_general x24, matrix products, product_back(): lax.dot_general(left_side, right_side, (((1,), (1,)), ((), ())), preferre...  115 us
    ppermute x10, starting transfers between devices, passed_along(): lax.ppermute(value, axis, [(source, source + steps) for source in range(i...  111 us
    all_gather x1, waiting for transfers between devices, on_device(): lax.all_gather(conv_in, 'dp', axis=1, tiled=True)  110 us
    all_gather x1, waiting for transfers between devices, on_device(): lax.all_gather(conv_out, 'dp', axis=1, tiled=True)  89.9 us
  transfers between devices with their start and end apart: 29, of which 17 were waited for; matrix products, arithmetic and copies ran while one was open for 3% of the time, Pallas kernels for 0%

commit v1 on v0

v1 whole, which is shorter than its diff:
```python
from functools import partial
import math

import jax
import jax.numpy as jnp
import numpy as np
from jax import lax
from jax.experimental import pallas as pl
from jax.experimental.pallas import tpu as pltpu
from jax.sharding import PartitionSpec as P

WIDTH = 768
EMBED = 768
CLASSES = 1000
HEAD_DIM = 64
GROUPS = 32
SIDE = 8
LEVELS = 40
MICRO = 4
PIXELS = 64
TAPS = 9

EPS = 1e-05
SIGMA_LOW = 0.002
SIGMA_HIGH = 80.0

F32 = jnp.float32
BF16 = jnp.bfloat16
LANE = 128
CHUNKS = WIDTH // LANE
PER_GROUP = WIDTH // GROUPS
GROUP_SHARE = 1.0 / (PER_GROUP * PIXELS)
VMEM_LIMIT = 56 * 2**20

GAIN = 0
BIAS = 4

GROUP_OF = (np.arange(WIDTH)[:, None] // PER_GROUP == np.arange(LANE)[None, :]).astype(np.float32)


def lanes(chunk):
    return pl.ds(chunk * LANE, LANE)


def dot(left, right):
    return jnp.dot(left, right, preferred_element_type=F32)


def dot_nt(left, right):
    return lax.dot_general(left, right, (((1,), (1,)), ((), ())), preferred_element_type=F32)


def dot_tn(left, right):
    return lax.dot_general(left, right, (((0,), (0,)), ((), ())), preferred_element_type=F32)


def octet_sum(values, octets):
    width = values.shape[-1]
    partial_sums = values.reshape(SIDE, octets, width).sum(axis=0).reshape(octets // 8, 8, width)
    totals = jnp.sum(partial_sums, axis=1, keepdims=True)
    return jnp.broadcast_to(totals, partial_sums.shape).reshape(octets, width)


def over_rows(stat):
    octets, width = stat.shape
    return jnp.broadcast_to(stat[None], (SIDE, octets, width)).reshape(SIDE * octets, width)


def in_parts(values):
    first = values.astype(BF16)
    rest = values - first.astype(F32)
    second = rest.astype(BF16)
    third = (rest - second.astype(F32)).astype(BF16)
    return jnp.concatenate([first, second, third], axis=0)


def group_mean(sums, group_of, group_of_t):
    count = sums.shape[0]
    grouped = dot(in_parts(sums), group_of)
    grouped = (grouped[:count] + grouped[count : 2 * count] + grouped[2 * count :]) * GROUP_SHARE
    spread = dot(in_parts(grouped), group_of_t)
    return spread[:count] + spread[count : 2 * count] + spread[2 * count :]


def norm_stats(read, octets, group_of, group_of_t):
    sums = jnp.concatenate([octet_sum(read(c), octets) for c in range(CHUNKS)], axis=1)
    mean = group_mean(sums, group_of, group_of_t)
    squares = []
    for c in range(CHUNKS):
        centered = read(c) - over_rows(mean[:, c * LANE : (c + 1) * LANE])
        squares.append(octet_sum(centered * centered, octets))
    spread = group_mean(jnp.concatenate(squares, axis=1), group_of, group_of_t)
    return mean, lax.rsqrt(spread + EPS)


def normed_chunk(values, stat_ref, c):
    mean = stat_ref[0, :, lanes(c)]
    inv = stat_ref[1, :, lanes(c)]
    return (values - over_rows(mean)) * over_rows(inv)


def sigmoid(values):
    return 1.0 / (1.0 + jnp.exp(-values))


def silu_slope(values):
    gate = sigmoid(values)
    return gate * (1.0 + values * (1.0 - gate))


def put_shifted(planes, base, values, c, octets):
    rows = values.shape[0]
    column = lax.broadcasted_iota(jnp.int32, values.shape, 0) & 7
    before = jnp.where(column != 0, pltpu.roll(values, 1, 0), 0.0)
    after = jnp.where(column != 7, pltpu.roll(values, rows - 1, 0), 0.0)
    planes[base, pl.ds(octets, rows), lanes(c)] = before.astype(BF16)
    planes[base + 1, pl.ds(octets, rows), lanes(c)] = values.astype(BF16)
    planes[base + 2, pl.ds(octets, rows), lanes(c)] = after.astype(BF16)


def clear_edges(planes, octets):
    count, rows, width = planes.shape
    edge = jnp.zeros((count, octets, width), BF16)
    planes[:, pl.ds(0, octets), :] = edge
    planes[:, pl.ds(rows - octets, octets), :] = edge


def row_total(values):
    return jnp.sum(values, axis=0, keepdims=True)


def norm_back(read_grad, read_normed, gain_of, stat_ref, octets, tables, write, sums_out):
    group_of, group_of_t = tables
    first, second = [], []
    for c in range(CHUNKS):
        grad = read_grad(c)
        first.append(octet_sum(grad, octets))
        second.append(octet_sum(grad * read_normed(c), octets))
    first = jnp.concatenate(first, axis=1)
    second = jnp.concatenate(second, axis=1)
    sums_out(first, second)
    gain = gain_of(None)
    both = group_mean(jnp.concatenate([first * gain, second * gain], axis=0), group_of, group_of_t)
    for c in range(CHUNKS):
        part = slice(c * LANE, (c + 1) * LANE)
        inv = over_rows(stat_ref[1, :, lanes(c)])
        mean_one = over_rows(both[:octets, part])
        mean_two = over_rows(both[octets:, part])
        write(c, inv * (gain_of(c) * read_grad(c) - mean_one - read_normed(c) * mean_two))


def conv_in_forward(decoder, octets, *refs):
    if decoder:
        hidden, skipped, weights, params, group_of, group_of_t = refs[:6]
        conv_one, stat_h, stat_s, turned_h, turned_s, planes, held, sems = refs[6:]
        sides = ((hidden, stat_h, turned_h, 0), (skipped, stat_s, turned_s, 1))
    else:
        hidden, weights, params, group_of, group_of_t = refs[:5]
        conv_one, stat_h, turned_h, planes, held, sems = refs[5:]
        sides = ((hidden, stat_h, turned_h, 0),)
    span = WIDTH * len(sides)
    copies = [
        pltpu.make_async_copy(
            weights.at[pl.ds(tap * 2 * WIDTH, span)], held.at[pl.ds(tap * span, span)], sems.at[tap]
        )
        for tap in range(TAPS)
    ]
    for copy in copies:
        copy.start()
    rows = hidden.shape[0]
    tables = (group_of[...], group_of_t[...])
    clear_edges(planes, octets)
    for source, stat, turned, which in sides:
        mean, inv = norm_stats(lambda c: source[:, lanes(c)].astype(F32), octets, *tables)
        stat[0] = mean
        stat[1] = inv
        for c in range(CHUNKS):
            normed = normed_chunk(source[:, lanes(c)].astype(F32), stat, c)
            value = (
                normed * params[pl.ds(GAIN + which, 1), lanes(c)]
                + params[pl.ds(BIAS + which, 1), lanes(c)]
            )
            value = value * sigmoid(value)
            put_shifted(planes, 3 * which, value, c, octets)
            turned[lanes(c), :] = value.T.astype(BF16)
    for tap in range(TAPS):
        copies[tap].wait()
        for half in range(len(sides)):
            part = dot(
                planes[3 * half + tap % 3, pl.ds(octets * (tap // 3), rows), :],
                held[pl.ds(tap * span + half * WIDTH, WIDTH), :],
            )
            if tap == 0 and half == 0:
                conv_one[...] = part + params[pl.ds(BIAS + 2, 1), :]
            else:
                conv_one[...] += part


class Rest:
    def __init__(self, source, sems, pieces):
        self.source, self.sems, self.pieces = source, sems, pieces
        self.offset, self.waits = 0, {}

    def fetch(self, name, total, held, at_once=True):
        share = total // self.pieces
        copies = []
        for piece in range(self.pieces):
            copies.append(
                pltpu.make_async_copy(
                    self.source.at[piece, pl.ds(self.offset, share)],
                    held.at[pl.ds(piece * share, share)],
                    self.sems.at[len(self.waits), piece],
                )
            )
        self.waits[name] = (share, copies, [False] * self.pieces)
        self.offset += share
        if at_once:
            for copy in copies:
                copy.start()

    def need(self, name, stop):
        share, copies, done = self.waits[name]
        for piece, copy in enumerate(copies):
            if piece * share < stop and not done[piece]:
                copy.wait()
                done[piece] = True


def rest_rows():
    return {
        "conv_out": TAPS * WIDTH,
        "query": WIDTH,
        "key": WIDTH,
        "value": WIDTH,
        "out": WIDTH,
        "skip": 2 * WIDTH,
    }


def head_mask(rows):
    return lax.broadcasted_iota(jnp.int32, (rows, LANE), 1) < HEAD_DIM


def image_bias(rows, images):
    row_image = lax.rem(lax.shift_right_logical(lax.broadcasted_iota(jnp.int32, (rows, rows), 0), 3), images)
    column_image = lax.rem(lax.shift_right_logical(lax.broadcasted_iota(jnp.int32, (rows, rows), 1), 3), images)
    return jnp.where(row_image == column_image, 0.0, -1e30).astype(F32)


def attention_of(queries, keys, apart):
    scores = dot_nt(queries, keys) * (1.0 / math.sqrt(HEAD_DIM)) + apart
    weight = jnp.exp(scores - jnp.max(scores, axis=1, keepdims=True))
    return weight * (1.0 / jnp.sum(weight, axis=1, keepdims=True))


def block_forward(decoder, octets, pieces, *refs):
    if decoder:
        conv_one, hidden, skipped, modulation, rest, params, group_of, group_of_t = refs[:8]
        refs = refs[8:]
    else:
        conv_one, hidden, modulation, rest, params, group_of, group_of_t = refs[:7]
        refs = refs[7:]
    result, residual, stat_c, stat_r, attend, project, mixed, turned, planes, apart = refs[:10]
    held_conv, held_qkv, held_out, held_skip, sems = refs[10:]
    weights = Rest(rest, sems, pieces)
    weights.fetch("conv_out", TAPS * WIDTH, held_conv)
    for index, name in enumerate(("query", "key", "value")):
        weights.fetch(name, WIDTH, held_qkv.at[index])
    weights.fetch("out", WIDTH, held_out)
    if decoder:
        weights.fetch("skip", 2 * WIDTH, held_skip)
    rows = conv_one.shape[0]
    tables = (group_of[...], group_of_t[...])
    clear_edges(planes, octets)
    apart[...] = image_bias(rows, octets // 8)
    mean, inv = norm_stats(lambda c: conv_one[:, lanes(c)], octets, *tables)
    stat_c[0] = mean
    stat_c[1] = inv
    for c in range(CHUNKS):
        normed = (
            normed_chunk(conv_one[:, lanes(c)], stat_c, c) * params[pl.ds(GAIN + 2, 1), lanes(c)]
            + params[pl.ds(BIAS + 5, 1), lanes(c)]
        )
        scale = over_rows(modulation[:, lanes(c)])
        shift = over_rows(modulation[:, lanes(CHUNKS + c)])
        value = normed * (1.0 + scale) + shift
        value = value * sigmoid(value)
        put_shifted(planes, 0, value, c, octets)
        turned[lanes(c), :] = value.T.astype(BF16)
    for tap in range(TAPS):
        weights.need("conv_out", (tap + 1) * WIDTH)
        part = dot(
            planes[tap % 3, pl.ds(octets * (tap // 3), rows), :], held_conv[pl.ds(tap * WIDTH, WIDTH), :]
        )
        if tap == 0:
            residual[...] = part + params[pl.ds(BIAS + 6, 1), :]
        else:
            residual[...] += part
    if decoder:
        weights.need("skip", 2 * WIDTH)
        residual[...] += (
            dot(hidden[...], held_skip[pl.ds(0, WIDTH), :])
            + dot(skipped[...], held_skip[pl.ds(WIDTH, WIDTH), :])
            + params[pl.ds(BIAS + 7, 1), :]
        )
    else:
        residual[...] += hidden[...].astype(F32)
    mean, inv = norm_stats(lambda c: residual[:, lanes(c)], octets, *tables)
    stat_r[0] = mean
    stat_r[1] = inv
    for c in range(CHUNKS):
        attend[:, lanes(c)] = (
            normed_chunk(residual[:, lanes(c)], stat_r, c) * params[pl.ds(GAIN + 3, 1), lanes(c)]
            + params[pl.ds(BIAS + 8, 1), lanes(c)]
        ).astype(BF16)
    for index, (name, bias) in enumerate((("query", 9), ("key", None), ("value", 10))):
        weights.need(name, WIDTH)
        part = dot(attend[...], held_qkv[index])
        if bias is not None:
            part = part + params[pl.ds(BIAS + bias, 1), :]
        project[:, pl.ds(index * WIDTH, WIDTH)] = part.astype(BF16)
    left = head_mask(rows)
    for pair in range(CHUNKS):
        queries = project[:, lanes(pair)]
        keys_h = project[:, lanes(CHUNKS + pair)]
        values_h = project[:, lanes(2 * CHUNKS + pair)]
        parts = []
        for half in (left, jnp.logical_not(left)):
            chosen = jnp.where(half, queries, jnp.zeros_like(queries))
            attention = attention_of(chosen, keys_h, apart[...])
            parts.append(dot(attention.astype(BF16), values_h))
        mixed[:, lanes(pair)] = jnp.where(left, parts[0], parts[1]).astype(BF16)
    weights.need("out", WIDTH)
    result[...] = (
        residual[...] + dot(mixed[...], held_out[...]) + params[pl.ds(BIAS + 11, 1), :]
    ).astype(BF16)


def block_backward(decoder, octets, pieces, *refs):
    grad_out, project, residual, stat_r, conv_one, stat_c, modulation, rest, params, group_of, group_of_t = refs[:11]
    grad_top, grad_project, grad_resid, grad_resid_b, grad_conv_b, grad_mod, sums = refs[11:18]
    scratch, grad_mixed, planes, apart, held_conv, held_qkv, held_out, sems = refs[18:]
    weights = Rest(rest, sems, pieces)
    weights.fetch("conv_out", TAPS * WIDTH, held_conv, False)
    for index, name in enumerate(("query", "key", "value")):
        weights.fetch(name, WIDTH, held_qkv.at[index], False)
    weights.fetch("out", WIDTH, held_out, False)
    for name in ("out", "query", "key", "value", "conv_out"):
        for copy in weights.waits[name][1]:
            copy.start()
    rows = conv_one.shape[0]
    tables = (group_of[...], group_of_t[...])
    sums[...] = jnp.zeros(sums.shape, F32)
    clear_edges(planes, octets)
    apart[...] = image_bias(rows, octets // 8)

    def put_sum(row, c, values):
        sums[pl.ds(row, 1), lanes(c)] = row_total(values)

    top = grad_out[...].astype(BF16)
    grad_top[...] = top
    for c in range(CHUNKS):
        put_sum(BIAS + 11, c, grad_top[:, lanes(c)].astype(F32))
    weights.need("out", WIDTH)
    grad_mixed[...] = dot_nt(top, held_out[...]).astype(BF16)
    left = head_mask(rows)
    root = 1.0 / math.sqrt(HEAD_DIM)
    for pair in range(CHUNKS):
        queries = project[:, lanes(pair)]
        keys_h = project[:, lanes(CHUNKS + pair)]
        values_h = project[:, lanes(2 * CHUNKS + pair)]
        grads_h = grad_mixed[:, lanes(pair)]
        parts = []
        for half in (left, jnp.logical_not(left)):
            chosen = jnp.where(half, queries, jnp.zeros_like(queries))
            chosen_grad = jnp.where(half, grads_h, jnp.zeros_like(grads_h))
            attention = attention_of(chosen, keys_h, apart[...])
            grad_attention = dot_nt(chosen_grad, values_h)
            weighted = grad_attention * attention
            grad_scores = (weighted - attention * jnp.sum(weighted, axis=1, keepdims=True)).astype(BF16)
            parts.append(
                (
                    dot(grad_scores, keys_h) * root,
                    dot_tn(grad_scores, queries) * root,
                    dot_tn(attention.astype(BF16), grads_h),
                )
            )
        for index in range(3):
            joined = jnp.where(left, parts[0][index], parts[1][index]).astype(BF16)
            grad_project[:, lanes(index * CHUNKS + pair)] = joined
            if index == 0:
                put_sum(BIAS + 9, pair, joined.astype(F32))
            if index == 2:
                put_sum(BIAS + 10, pair, joined.astype(F32))
    for index, name in enumerate(("query", "key", "value")):
        weights.need(name, WIDTH)
        part = dot_nt(grad_project[:, pl.ds(index * WIDTH, WIDTH)], held_qkv[index])
        if index == 0:
            scratch[...] = part
        else:
            scratch[...] += part

    def gain_attend(c):
        return params[pl.ds(GAIN + 3, 1), :] if c is None else params[pl.ds(GAIN + 3, 1), lanes(c)]

    def sums_attend(first, second):
        sums[pl.ds(BIAS + 8, 1), :] = row_total(first) * 0.125
        sums[pl.ds(GAIN + 3, 1), :] = row_total(second) * 0.125

    def write_resid(c, grad):
        total = grad_out[:, lanes(c)].astype(F32) + grad
        grad_resid[:, lanes(c)] = total
        rounded = total.astype(BF16)
        grad_resid_b[:, lanes(c)] = rounded
        rounded = rounded.astype(F32)
        put_shifted(planes, 0, rounded, c, octets)
        put_sum(BIAS + 6, c, rounded)
        if decoder:
            put_sum(BIAS + 7, c, rounded)

    norm_back(
        lambda c: scratch[:, lanes(c)],
        lambda c: normed_chunk(residual[:, lanes(c)], stat_r, c),
        gain_attend,
        stat_r,
        octets,
        tables,
        write_resid,
        sums_attend,
    )
    for tap in range(TAPS):
        weights.need("conv_out", (tap + 1) * WIDTH)
        part = dot_nt(
            planes[2 - tap % 3, pl.ds(octets * (2 - tap // 3), rows), :],
            held_conv[pl.ds(tap * WIDTH, WIDTH), :],
        )
        if tap == 0:
            scratch[...] = part
        else:
            scratch[...] += part
    for c in range(CHUNKS):
        normed = (
            normed_chunk(conv_one[:, lanes(c)], stat_c, c) * params[pl.ds(GAIN + 2, 1), lanes(c)]
            + params[pl.ds(BIAS + 5, 1), lanes(c)]
        )
        scale = over_rows(modulation[:, lanes(c)])
        shift = over_rows(modulation[:, lanes(CHUNKS + c)])
        scratch[:, lanes(c)] = scratch[:, lanes(c)] * silu_slope(normed * (1.0 + scale) + shift)

    def gain_middle(c):
        if c is None:
            return params[pl.ds(GAIN + 2, 1), :] * (1.0 + modulation[:, pl.ds(0, WIDTH)])
        return over_rows(params[pl.ds(GAIN + 2, 1), lanes(c)] * (1.0 + modulation[:, lanes(c)]))

    def sums_middle(first, second):
        scaled = 1.0 + modulation[:, pl.ds(0, WIDTH)]
        sums[pl.ds(BIAS + 5, 1), :] = row_total(first * scaled) * 0.125
        sums[pl.ds(GAIN + 2, 1), :] = row_total(second * scaled) * 0.125
        grad_scale = (
            params[pl.ds(GAIN + 2, 1), :] * second + params[pl.ds(BIAS + 5, 1), :] * first
        ).astype(BF16)
        grad_shift = first.astype(BF16)
        grad_mod[:, pl.ds(0, WIDTH)] = grad_scale
        grad_mod[:, pl.ds(WIDTH, WIDTH)] = grad_shift
        sums[pl.ds(BIAS + 3, 1), :] = row_total(grad_scale.astype(F32)) * 0.125
        sums[pl.ds(BIAS + 4, 1), :] = row_total(grad_shift.astype(F32)) * 0.125

    def write_conv(c, grad):
        rounded = grad.astype(BF16)
        grad_conv_b[:, lanes(c)] = rounded
        put_sum(BIAS + 2, c, rounded.astype(F32))

    norm_back(
        lambda c: scratch[:, lanes(c)],
        lambda c: normed_chunk(conv_one[:, lanes(c)], stat_c, c),
        gain_middle,
        stat_c,
        octets,
        tables,
        write_conv,
        sums_middle,
    )


def conv_in_backward(decoder, octets, pieces, *refs):
    if decoder:
        grad_conv, hidden, skipped, stat_h, stat_s, grad_resid, grad_resid_b, weights, rest = refs[:9]
        params, group_of, group_of_t, grad_hidden, grad_skipped, sums = refs[9:15]
        scratch, planes, held, held_skip, sems, rest_sems = refs[15:]
        sides = ((hidden, stat_h, grad_hidden, 0), (skipped, stat_s, grad_skipped, 1))
    else:
        grad_conv, hidden, stat_h, grad_resid, weights, params, group_of, group_of_t = refs[:8]
        grad_hidden, sums, scratch, planes, held, sems = refs[8:]
        sides = ((hidden, stat_h, grad_hidden, 0),)
    span = WIDTH * len(sides)
    copies = [
        pltpu.make_async_copy(
            weights.at[pl.ds(tap * 2 * WIDTH, span)], held.at[pl.ds(tap * span, span)], sems.at[tap]
        )
        for tap in range(TAPS)
    ]
    for copy in copies:
        copy.start()
    if decoder:
        skip_weights = Rest(rest, rest_sems, pieces)
        skip_weights.offset = sum(
            count // pieces for name, count in rest_rows().items() if name != "skip"
        )
        skip_weights.fetch("skip", 2 * WIDTH, held_skip)
    rows = hidden.shape[0]
    tables = (group_of[...], group_of_t[...])
    sums[...] = jnp.zeros(sums.shape, F32)
    clear_edges(planes, octets)
    for c in range(CHUNKS):
        put_shifted(planes, 0, grad_conv[:, lanes(c)].astype(F32), c, octets)
    for tap in range(TAPS):
        copies[tap].wait()
        for _, _, _, half in sides:
            part = dot_nt(
                planes[2 - tap % 3, pl.ds(octets * (2 - tap // 3), rows), :],
                held[pl.ds(tap * span + half * WIDTH, WIDTH), :],
            )
            if tap == 0:
                scratch[half] = part
            else:
                scratch[half] += part
    if decoder:
        skip_weights.need("skip", 2 * WIDTH)
    for source, stat, target, which in sides:

        def normed_of(c, source=source, stat=stat):
            return normed_chunk(source[:, lanes(c)].astype(F32), stat, c)

        def gain_input(c, which=which):
            row = pl.ds(GAIN + which, 1)
            return params[row, :] if c is None else params[row, lanes(c)]

        for c in range(CHUNKS):
            value = normed_of(c) * gain_input(c) + params[pl.ds(BIAS + which, 1), lanes(c)]
            scratch[which, :, lanes(c)] = scratch[which, :, lanes(c)] * silu_slope(value)

        def sums_input(first, second, which=which):
            sums[pl.ds(BIAS + which, 1), :] = row_total(first) * 0.125
            sums[pl.ds(GAIN + which, 1), :] = row_total(second) * 0.125

        if decoder:
            target[...] = dot_nt(grad_resid_b[...], held_skip[pl.ds(which * WIDTH, WIDTH), :])

        def write_input(c, grad, target=target):
            if decoder:
                target[:, lanes(c)] += grad
            else:
                target[:, lanes(c)] = grad + grad_resid[:, lanes(c)]

        norm_back(
            lambda c, which=which: scratch[which, :, lanes(c)],
            normed_of,
            gain_input,
            stat,
            octets,
            tables,
            write_input,
            sums_input,
        )


def shape(dims, kind):
    return jax.ShapeDtypeStruct(dims, kind)


IN_VMEM = pl.BlockSpec(memory_space=pltpu.VMEM)
IN_HBM = pl.BlockSpec(memory_space=pl.ANY)


def call(body, operands, far, outputs, scratch, flops, name):
    moved = sum(int(np.prod(v.shape)) * v.dtype.itemsize for v in (*operands, *outputs))
    return pl.pallas_call(
        body,
        out_shape=outputs,
        in_specs=[IN_HBM if index in far else IN_VMEM for index in range(len(operands))],
        out_specs=[IN_VMEM] * len(outputs),
        scratch_shapes=scratch,
        compiler_params=pltpu.CompilerParams(vmem_limit_bytes=VMEM_LIMIT),
        cost_estimate=pl.CostEstimate(flops=flops, bytes_accessed=moved, transcendentals=0),
        name=name,
    )(*operands)


def run_conv_in(decoder, hidden, skipped, weights, params, tables):
    rows = hidden.shape[0]
    octets = rows // SIDE
    sides = 2 if decoder else 1
    inputs = [hidden, skipped] if decoder else [hidden]
    outputs = [shape((rows, WIDTH), F32)]
    outputs += [shape((2, octets, WIDTH), F32)] * sides
    outputs += [shape((WIDTH, rows), BF16)] * sides
    return call(
        partial(conv_in_forward, decoder, octets),
        [*inputs, weights, params, *tables],
        {len(inputs)},
        outputs,
        [
            pltpu.VMEM((3 * sides, rows + 2 * octets, WIDTH), BF16),
            pltpu.VMEM((sides * TAPS * WIDTH, WIDTH), BF16),
            pltpu.SemaphoreType.DMA((TAPS,)),
        ],
        2 * rows * sides * TAPS * WIDTH * WIDTH,
        "conv_in_forward",
    )


def run_block(decoder, conv_one, hidden, skipped, modulation, rest, params, tables):
    rows = hidden.shape[0]
    octets = rows // SIDE
    pieces = rest.shape[0]
    inputs = [conv_one, hidden, skipped] if decoder else [conv_one, hidden]
    outputs = [
        shape((rows, WIDTH), BF16),
        shape((rows, WIDTH), F32),
        shape((2, octets, WIDTH), F32),
        shape((2, octets, WIDTH), F32),
        shape((rows, WIDTH), BF16),
        shape((rows, 3 * WIDTH), BF16),
        shape((rows, WIDTH), BF16),
        shape((WIDTH, rows), BF16),
    ]
    return call(
        partial(block_forward, decoder, octets, pieces),
        [*inputs, modulation, rest, params, *tables],
        {len(inputs) + 1},
        outputs,
        [
            pltpu.VMEM((3, rows + 2 * octets, WIDTH), BF16),
            pltpu.VMEM((rows, rows), F32),
            pltpu.VMEM((TAPS * WIDTH, WIDTH), BF16),
            pltpu.VMEM((3, WIDTH, WIDTH), BF16),
            pltpu.VMEM((WIDTH, WIDTH), BF16),
            pltpu.VMEM((2 * WIDTH, WIDTH), BF16),
            pltpu.SemaphoreType.DMA((6, pieces)),
        ],
        2 * rows * (TAPS + 6) * WIDTH * WIDTH,
        "block_forward",
    )


def run_block_back(decoder, grad_out, project, residual, stat_r, conv_one, stat_c, modulation, rest, params, tables):
    rows = residual.shape[0]
    octets = rows // SIDE
    pieces = rest.shape[0]
    outputs = [
        shape((rows, WIDTH), BF16),
        shape((rows, 3 * WIDTH), BF16),
        shape((rows, WIDTH), F32),
        shape((rows, WIDTH), BF16),
        shape((rows, WIDTH), BF16),
        shape((octets, 2 * WIDTH), BF16),
        shape((16, WIDTH), F32),
    ]
    return call(
        partial(block_backward, decoder, octets, pieces),
        [grad_out, project, residual, stat_r, conv_one, stat_c, modulation, rest, params, *tables],
        {7},
        outputs,
        [
            pltpu.VMEM((rows, WIDTH), F32),
            pltpu.VMEM((rows, WIDTH), BF16),
            pltpu.VMEM((3, rows + 2 * octets, WIDTH), BF16),
            pltpu.VMEM((rows, rows), F32),
            pltpu.VMEM((TAPS * WIDTH, WIDTH), BF16),
            pltpu.VMEM((3, WIDTH, WIDTH), BF16),
            pltpu.VMEM((WIDTH, WIDTH), BF16),
            pltpu.SemaphoreType.DMA((6, pieces)),
        ],
        2 * rows * (TAPS + 6) * WIDTH * WIDTH,
        "block_backward",
    )


def run_conv_in_back(decoder, grad_conv, hidden, skipped, stat_h, stat_s, grad_resid, grad_resid_b, weights, rest, params, tables):
    rows = hidden.shape[0]
    octets = rows // SIDE
    sides = 2 if decoder else 1
    pieces = rest.shape[0]
    if decoder:
        inputs = [grad_conv, hidden, skipped, stat_h, stat_s, grad_resid, grad_resid_b, weights, rest]
        far = {7, 8}
    else:
        inputs = [grad_conv, hidden, stat_h, grad_resid, weights]
        far = {4}
    scratch = [
        pltpu.VMEM((sides, rows, WIDTH), F32),
        pltpu.VMEM((3, rows + 2 * octets, WIDTH), BF16),
        pltpu.VMEM((sides * TAPS * WIDTH, WIDTH), BF16),
    ]
    if decoder:
        scratch.append(pltpu.VMEM((2 * WIDTH, WIDTH), BF16))
    scratch.append(pltpu.SemaphoreType.DMA((TAPS,)))
    if decoder:
        scratch.append(pltpu.SemaphoreType.DMA((1, pieces)))
    return call(
        partial(conv_in_backward, decoder, octets, pieces),
        [*inputs, params, *tables],
        far,
        [shape((rows, WIDTH), F32)] * sides + [shape((16, WIDTH), F32)],
        scratch,
        2 * rows * sides * TAPS * WIDTH * WIDTH,
        "conv_in_backward",
    )


def tap_slices_kernel(rows_in, rows_out, octets, place, fields, cols_in, cols_out):
    lane = lax.broadcasted_iota(jnp.int32, (1, SIDE * octets), 1)
    grid_row = lax.div(lane, octets)
    grid_column = lane & 7
    for rows, base, channels, target in (
        (rows_in, 0, 2 * WIDTH, cols_in),
        (rows_out, 2 * WIDTH, WIDTH, cols_out),
    ):
        block = rows // TAPS
        per_tap = channels // block
        for index in range(TAPS):
            position = place[0] * TAPS + index
            tap = lax.div(position, per_tap)
            start = pl.multiple_of(base + lax.rem(position, per_tap) * block, 16)
            down = lax.div(tap, 3) - 1
            across = lax.rem(tap, 3) - 1
            values = fields[0, pl.ds(start, block), :].astype(F32)
            width = SIDE * octets
            moved = pltpu.roll(values, lax.rem(width - (octets * down + across), width), 1)
            inside = (
                (grid_row + down >= 0)
                & (grid_row + down < SIDE)
                & (grid_column + across >= 0)
                & (grid_column + across < 8)
            )
            target[pl.ds(index * block, block), :] = jnp.where(inside, moved, 0.0).astype(BF16)


def tap_slices_plain(fields, rows, base, channels, place, octets):
    pieces, _, width = fields.shape
    spots = place * rows + jnp.arange(rows)
    taps = spots // channels
    values = jnp.take(fields, base + spots % channels, axis=1)
    lane = jnp.arange(width)
    total = jnp.zeros_like(values)
    for tap in range(TAPS):
        down, across = tap // 3 - 1, tap % 3 - 1
        row, column = lane // octets + down, lane % 8 + across
        inside = (row >= 0) & (row < SIDE) & (column >= 0) & (column < 8)
        moved = jnp.roll(values, -(octets * down + across), axis=2)
        total = jnp.where((taps == tap)[None, :, None] & inside, moved, total)
    return total.transpose(1, 0, 2).reshape(rows, pieces * width)


def tap_slices(fields, rows_in, rows_out, place, octets):
    pieces, height, width = fields.shape
    if rows_in % (TAPS * 16) or rows_out % (TAPS * 16):
        return (
            tap_slices_plain(fields, rows_in, 0, 2 * WIDTH, place, octets),
            tap_slices_plain(fields, rows_out, 2 * WIDTH, WIDTH, place, octets),
        )
    return pl.pallas_call(
        partial(tap_slices_kernel, rows_in, rows_out, octets),
        grid_spec=pltpu.PrefetchScalarGridSpec(
            num_scalar_prefetch=1,
            grid=(pieces,),
            in_specs=[pl.BlockSpec((1, height, width), lambda piece, place: (piece, 0, 0))],
            out_specs=[
                pl.BlockSpec((rows_in, width), lambda piece, place: (0, piece)),
                pl.BlockSpec((rows_out, width), lambda piece, place: (0, piece)),
            ],
        ),
        out_shape=[
            shape((rows_in, pieces * width), BF16),
            shape((rows_out, pieces * width), BF16),
        ],
        compiler_params=pltpu.CompilerParams(vmem_limit_bytes=VMEM_LIMIT),
        cost_estimate=pl.CostEstimate(
            flops=0, bytes_accessed=4 * pieces * height * width, transcendentals=0
        ),
        name="tap_slices",
    )(place.reshape(1).astype(jnp.int32), fields)


def gather_doubling(value, axis):
    count, index = lax.axis_size(axis), lax.axis_index(axis)
    value = value[None]
    step = 1
    while step < count:
        other = lax.ppermute(value, axis, [(i, i ^ step) for i in range(count)])
        value = jnp.where(
            (index // step) % 2 == 0,
            jnp.concatenate([value, other], axis=0),
            jnp.concatenate([other, value], axis=0),
        )
        step *= 2
    return value


def scatter_halving(value, axis):
    count, index = lax.axis_size(axis), lax.axis_index(axis)
    step = count // 2
    while step:
        upper = (index // step) % 2 == 1
        keep = jnp.where(upper, value[step:], value[:step])
        send = jnp.where(upper, value[:step], value[step:])
        value = keep + lax.ppermute(send, axis, [(i, i ^ step) for i in range(count)])
        step //= 2
    return value[0]


def moved(value, source, target):
    return lax.ppermute(value, "section", [(source, target)])


def to_rows(value):
    micro, images, pixels, channels = value.shape
    count = micro * images
    return (
        value.reshape(count, pixels // 8, 8, channels).transpose(1, 0, 2, 3).reshape(-1, channels)
    )


def from_rows(value, images):
    count = MICRO * images
    channels = value.shape[-1]
    grid_rows = value.shape[0] // (8 * count)
    planes = value.reshape(grid_rows, count, 8, channels).transpose(1, 0, 2, 3)
    return planes.reshape(MICRO, images, grid_rows * 8, channels)


def noise_columns(pair_ids, columns):
    fraction = pair_ids.astype(F32) / (LEVELS - 1)
    top_root = SIGMA_HIGH ** (1.0 / 7.0)
    bottom_root = SIGMA_LOW ** (1.0 / 7.0)
    sigmas = (top_root + fraction * (bottom_root - top_root)) ** 7
    log_scale = 250.0 * jnp.log(sigmas)
    quarter = EMBED // 4
    kind = columns // quarter
    frequency = jnp.exp(-math.log(10000.0) * (columns % quarter).astype(F32) / quarter)
    angles = jnp.where(kind < 2, log_scale[:, :1], log_scale[:, 1:]) * frequency
    return jnp.where(kind % 2 == 0, jnp.cos(angles), jnp.sin(angles))


def on_device(
    level_input,
    cotangent,
    class_table,
    conv_in,
    conv_out,
    embed_proj,
    skip_proj,
    qkv_proj,
    out_proj,
    gains,
    biases,
    noise_pairs,
    classes,
):
    sections = lax.axis_size("section")
    section_id = lax.axis_index("section")
    shards = lax.axis_size("dp")
    shard_id = lax.axis_index("dp")
    images = level_input.shape[1]
    count = MICRO * images
    octets = 8 * count
    rows = SIDE * octets
    tables = (jnp.asarray(GROUP_OF, BF16), jnp.asarray(GROUP_OF.T, BF16))

    conv_in_full = lax.all_gather(conv_in[0], "dp", axis=0, tiled=True)
    qkv_parts = [qkv_proj[0][:, part * WIDTH : (part + 1) * WIDTH] for part in range(3)]
    rest_full = lax.all_gather(
        jnp.concatenate([conv_out[0], *qkv_parts, out_proj[0], skip_proj[0]], axis=0), "dp", axis=0
    )
    if any((total // shards) % 16 for total in rest_rows().values()):
        offset, whole = 0, []
        for total in rest_rows().values():
            share = total // shards
            whole.append(rest_full[:, offset : offset + share].reshape(total, WIDTH))
            offset += share
        rest_full = jnp.concatenate(whole, axis=0)[None]

    gain_share, bias_share = gains.shape[1], biases.shape[1]
    small = jnp.concatenate(
        [
            gains[0].astype(F32),
            biases[0].astype(F32),
            noise_pairs.reshape(-1).astype(F32),
            classes.reshape(-1).astype(F32),
        ]
    )
    spare = -small.shape[0] % LANE
    every = gather_doubling(jnp.pad(small, (0, spare))[None], "dp")[:, 0]
    cut = gain_share + bias_share
    params = jnp.concatenate(
        [every[:, :gain_share].reshape(4, WIDTH), every[:, gain_share:cut].reshape(12, WIDTH)],
        axis=0,
    )
    all_images = shards * count
    pair_ids = every[:, cut : cut + 2 * count].reshape(all_images, 2)
    class_ids = every[:, cut + 2 * count : cut + 3 * count].reshape(all_images).astype(jnp.int32)

    slice_width = class_table.shape[1]
    columns = shard_id * slice_width + jnp.arange(slice_width)[None, :]
    onehot = (class_ids[:, None] == jnp.arange(CLASSES)[None, :]).astype(BF16)
    pre = noise_columns(pair_ids, columns) + dot(onehot, class_table)
    embed_b = jax.nn.silu(pre).astype(BF16)
    shares = dot(embed_b, embed_proj[0]).reshape(shards, count, 2 * WIDTH)
    modulation = lax.all_to_all(shares, "dp", 0, 0).sum(axis=0)
    modulation = modulation + params[BIAS + 3 : BIAS + 5].reshape(1, 2 * WIDTH)
    modulation = jnp.repeat(modulation, 8, axis=0)

    level_own, top_own = to_rows(level_input), to_rows(cotangent)
    level_rows = jnp.concatenate(
        [level_own] + [moved(level_own, source, 0) for source in range(1, sections)], axis=0
    )
    top_rows = jnp.concatenate(
        [moved(top_own, source, sections - 1) for source in range(sections - 1)] + [top_own], axis=0
    )

    kept = []
    skips = {}
    hidden = level_rows
    result = None
    for tick in range(sections):
        decoder = tick >= sections // 2
        mirror = sections - 1 - tick
        skipped = skips[tick] if decoder else None
        outs = run_conv_in(decoder, hidden, skipped, conv_in_full, params, tables)
        if decoder:
            conv_one, stat_h, stat_s, turned_h, turned_s = outs
        else:
            conv_one, stat_h, turned_h = outs
            stat_s, turned_s = None, jnp.zeros_like(turned_h)
        result, residual, stat_c, stat_r, attend, project, mixed, turned_w = run_block(
            decoder, conv_one, hidden, skipped, modulation, rest_full, params, tables
        )
        kept.append(
            {
                "hidden": hidden,
                "skipped": skipped,
                "conv_one": conv_one,
                "stat_h": stat_h,
                "stat_s": stat_s,
                "stat_c": stat_c,
                "stat_r": stat_r,
                "residual": residual,
                "attend": attend,
                "project": project,
                "mixed": mixed,
                "fields": jnp.concatenate([turned_h, turned_s, turned_w], axis=0),
            }
        )
        if tick < sections - 1:
            hidden = moved(result, tick, tick + 1)
            if not decoder:
                skips[mirror] = hidden if mirror == tick + 1 else moved(result, tick, mirror)

    def own(values):
        chosen = values[0]
        for tick in range(1, sections):
            chosen = jnp.where(section_id == tick, values[tick], chosen)
        return chosen

    fields = lax.all_gather(own([entry["fields"] for entry in kept]), "dp", axis=0)
    cols_in, cols_out = tap_slices(fields, conv_in.shape[1], conv_out.shape[1], shard_id, octets)

    def to_owners(value, source):
        share = rows // sections
        pieces = [value[index * share : (index + 1) * share] for index in range(sections)]
        total = jnp.where(section_id == source, pieces[source], jnp.zeros_like(pieces[source]))
        for target in range(sections):
            if target != source:
                total = total + moved(pieces[target].astype(BF16), source, target).astype(value.dtype)
        return from_rows(total, images)

    level_output = to_owners(result, sections - 1)

    grads = [None] * sections
    skip_grads = {}
    grad_out = top_rows
    grad_hidden = None
    for tick in reversed(range(sections)):
        decoder = tick >= sections // 2
        mirror = sections - 1 - tick
        entry = kept[tick]
        if not decoder and tick in skip_grads:
            grad_out = grad_out.astype(F32) + skip_grads[tick].astype(F32)
        top, grad_project, grad_resid, grad_resid_b, grad_conv_b, grad_mod, sums_block = run_block_back(
            decoder,
            grad_out,
            entry["project"],
            entry["residual"],
            entry["stat_r"],
            entry["conv_one"],
            entry["stat_c"],
            modulation,
            rest_full,
            params,
            tables,
        )
        outs = run_conv_in_back(
            decoder,
            grad_conv_b,
            entry["hidden"],
            entry["skipped"],
            entry["stat_h"],
            entry["stat_s"],
            grad_resid,
            grad_resid_b,
            conv_in_full,
            rest_full,
            params,
            tables,
        )
        grad_hidden = outs[0]
        if decoder:
            if mirror == tick - 1:
                grad_out = moved((grad_hidden + outs[1]).astype(BF16), tick, mirror)
            else:
                skip_grads[mirror] = moved(outs[1].astype(BF16), tick, mirror)
        if tick > 0 and not (decoder and mirror == tick - 1):
            grad_out = moved(grad_hidden.astype(BF16), tick, tick - 1)
        grads[tick] = {
            "top": top,
            "project": grad_project,
            "resid": grad_resid_b,
            "conv": grad_conv_b,
            "mod": grad_mod.reshape(count, 8, 2 * WIDTH)[:, 0],
            "sums": sums_block + outs[-1],
        }
    input_grad = to_owners(grad_hidden, 0)

    def picked(name):
        return own([entry[name] for entry in grads])

    def kept_own(name):
        return own([entry[name] for entry in kept])

    is_decoder = section_id >= sections // 2
    resid_all = lax.all_gather(picked("resid"), "dp", axis=0, tiled=True)
    conv_all = lax.all_gather(picked("conv"), "dp", axis=0, tiled=True)
    conv_out_grad = dot(cols_out, resid_all)
    conv_in_grad = dot(cols_in, conv_all)

    resid_own = picked("resid")
    decoder_entries = [
        jnp.concatenate([entry["hidden"], entry["skipped"] if entry["skipped"] is not None else entry["hidden"]], axis=1)
        for entry in kept
    ]
    skip_part = dot_tn(own(decoder_entries), resid_own)
    skip_part = jnp.where(is_decoder, skip_part, 0.0).astype(BF16)
    qkv_part = dot_tn(kept_own("attend"), picked("project")).astype(BF16)
    out_part = dot_tn(kept_own("mixed"), picked("top")).astype(BF16)
    share = WIDTH // shards
    skip_split = skip_part.reshape(shards, 2, share, WIDTH)
    small_grads = lax.psum_scatter(
        jnp.concatenate(
            [
                qkv_part,
                out_part,
                skip_split[:, 0].reshape(WIDTH, WIDTH),
                skip_split[:, 1].reshape(WIDTH, WIDTH),
            ],
            axis=1,
        ),
        "dp",
        scatter_dimension=0,
        tiled=True,
    ).astype(F32)
    qkv_grad = small_grads[:, : 3 * WIDTH]
    out_grad = small_grads[:, 3 * WIDTH : 4 * WIDTH]
    skip_grad = jnp.concatenate(
        [small_grads[:, 4 * WIDTH : 5 * WIDTH], small_grads[:, 5 * WIDTH :]], axis=0
    )

    sums = picked("sums")
    summed = scatter_halving(
        jnp.concatenate(
            [sums[:4].reshape(shards, gain_share), sums[4:].reshape(shards, bias_share)], axis=1
        ),
        "dp",
    )
    gains_grad, biases_grad = summed[:gain_share], summed[gain_share:]

    mod_all = gather_doubling(picked("mod"), "dp").reshape(all_images, 2 * WIDTH)
    embed_grad = dot_tn(embed_b, mod_all)
    grad_embed = lax.psum(dot_nt(mod_all, embed_proj[0]), "section")
    grad_pre = jax.vjp(jax.nn.silu, pre)[1](grad_embed)[0]
    table_grad = lax.dot_general(
        onehot.astype(F32),
        grad_pre,
        (((0,), (0,)), ((), ())),
        precision=lax.Precision.HIGHEST,
        preferred_element_type=F32,
    )
    return (
        level_output,
        input_grad,
        table_grad,
        conv_in_grad[None],
        conv_out_grad[None],
        embed_grad[None],
        skip_grad[None],
        qkv_grad[None],
        out_grad[None],
        gains_grad[None],
        biases_grad[None],
    )


def solution(mesh):
    placed = (
        P(None, "dp", "section", None),
        P(None, "dp", "section", None),
        P(None, "dp"),
        P("section", "dp", None),
        P("section", "dp", None),
        P("section", "dp", None),
        P("section", "dp", None),
        P("section", "dp", None),
        P("section", "dp", None),
        P("section", "dp"),
        P("section", "dp"),
        P(None, "dp", None),
        P(None, "dp"),
    )
    return jax.shard_map(
        on_device,
        mesh=mesh,
        in_specs=placed,
        out_specs=(
            P(None, "dp", "section", None),
            P(None, "dp", "section", None),
            P(None, "dp"),
            P("section", "dp", None),
            P("section", "dp", None),
            P("section", "dp", None),
            P("section", "dp", None),
            P("section", "dp", None),
            P("section", "dp", None),
            P("section", "dp"),
            P("section", "dp"),
        ),
        check_vma=False,
    )
```

time: 2790 us -> 714 us (0.26)
  waiting for transfers between devices: 1100 us -> 450 us
  local copies, waits for them, and re-layouts: 505 us -> 16.8 us
  other arithmetic: 392 us -> 17.5 us
  blocking collectives: 326 us -> 7.04 us
  matrix products: 299 us -> 23.6 us
  Pallas kernels: 0 us -> 136 us
  starting transfers between devices: 112 us -> 36.2 us
    reduce_scatter x9 -> x1, waiting for transfers between devices: 668 us -> 24 us  [on_device(): lax.psum_scatter(jnp.concatenate([qkv_part, out_part, skip_split[:, 0].re...]
    dot_general x88 -> x10, matrix products: 299 us -> 23.6 us  [the longest x4 19 us: dot(): return jnp.dot(left, right, preferred_element_type=F32)]
    all_gather x12 -> x0, blocking collectives: 263 us -> none  [the longest x5 220 us: backward_tick(): lax.all_gather(send_skip[None], 'section', axis=0, tiled=True)]
    reduce_sum x173 -> x1, other arithmetic: 204 us -> 0.07 us  [on_device(): modulation = lax.all_to_all(shares, 'dp', 0, 0).sum(axis=0)]
    pallas_call x0 -> x9, Pallas kernels: none -> 136 us  [the longest x8 119 us: call(): pl.pallas_call(body, out_shape=outputs, in_specs=[IN_HBM if index in far...]
    reduce_sum x96 -> x0, local copies, waits for them, and re-layouts: 106 us -> none  [the longest x48 53 us: group_norm(): centered = grouped - jnp.mean(grouped, axis=(1, 3), keepdims=True)]
    broadcast_in_dim x111 -> x4, local copies, waits for them, and re-layouts: 87.3 us -> 1.47 us  [the longest x1 0.79 us: on_device(): qkv_grad[None]]
    unnamed x21 -> x6, waiting for transfers between devices: 86.9 us -> 1.27 us
  transfers between devices with their start and end apart: 29 -> 25, of which waited for: 17 -> 20; matrix products, arithmetic and copies ran while one was open for 3% -> 5% of each run, Pallas kernels for 0% -> 5%
where the time goes in v1:
time: 714 us; the launch traced here: 703 us
  waiting for transfers between devices  450 us (63%)
  Pallas kernels  136 us (19%)
  starting transfers between devices  36.2 us (5%)
  matrix products  23.6 us (3%)
  other arithmetic  17.5 us (2%)
  local copies, waits for them, and re-layouts  16.8 us (2%)
  between operations  15.3 us (2%)
    pallas_call x8, Pallas kernels, call(): pl.pallas_call(body, out_shape=outputs, in_specs=[IN_HBM if index in far...  119 us
    all_gather x1, waiting for transfers between devices, on_device(): lax.all_gather(own([entry['fields'] for entry in kept]), 'dp', axis=0)  96.4 us
    all_gather x1, waiting for transfers between devices, on_device(): lax.all_gather(jnp.concatenate([conv_out[0], *qkv_parts, out_proj[0], ski...  89.2 us
    all_gather x1, waiting for transfers between devices, on_device(): conv_in_full = lax.all_gather(conv_in[0], 'dp', axis=0, tiled=True)  76.2 us
    all_gather x1, waiting for transfers between devices, on_device(): resid_all = lax.all_gather(picked('resid'), 'dp', axis=0, tiled=True)  52.1 us
    all_gather x1, waiting for transfers between devices, on_device(): conv_all = lax.all_gather(picked('conv'), 'dp', axis=0, tiled=True)  46.9 us
    ppermute x6, waiting for transfers between devices, moved(): return lax.ppermute(value, 'section', [(source, target)])  34.5 us
    reduce_scatter x1, waiting for transfers between devices, on_device(): lax.psum_scatter(jnp.concatenate([qkv_part, out_part, skip_split[:, 0].re...  24 us
  transfers between devices with their start and end apart: 25, of which 20 were waited for; matrix products, arithmetic and copies ran while one was open for 5% of the time, Pallas kernels for 5%

profile of v1, /device:TPU:0, one launch (start us, length us, event | category | flops | bytes accessed | tf_op | source)
XLA Modules:
  0.0 703.0 jit_solution(14149667725274563427)
XLA Ops:
  8.5 1.0 copy-done.3
  11.2 2.9 collective-permute-start.2
  14.1 1.6 collective-permute-done.2
  15.7 2.2 collective-permute-start.3
  17.9 1.7 collective-permute-done.3
  19.6 3.1 collective-permute-start.4
  22.7 2.4 collective-permute-done.4
  26.0 1.0 copy.67
  27.0 6.5 all-to-all-start
  33.7 1.3 collective-permute-start
  35.9 6.9 collective-permute-done
  43.6 8.8 %all-to-all-done = f32[16,4,1536]{2,1,0:T(4,128)S(1)} async-done(((f32[16,4,1536]{2,1,0:T(4,128)}), f32[16,4,1536]{2,1,0:T(4,128)S(1)}, u32[]{:S(2)}, u32[]{:S(2)}) %all-to-all-start) | async-done | bytes 393248 | tf_op jit(solution)/shard_map/all_to_all | solution.py:909
  53.2 76.2 %all-gather.14.cloned.1.call-done = bf16[1,13824,768]{2,1,0:T(8,128)(2,1)} async-done(((bf16[1,864,768]{2,1,0:T(8,128)(2,1)}), bf16[1,13824,768]{2,1,0:T(8,128)(2,1)}) %all-gather.14.cloned.1.call-update) | async-done | bytes 21233680 | tf_op jit(solution)/shard_map/all_gather | solution.py:870
  129.4 8.2 %conv_in_forward.2 = (f32[256,768]{1,0:T(8,128)}, f32[2,32,768]{2,1,0:T(8,128)}, bf16[768,256]{1,0:T(8,128)(2,1)}) custom-call(bf16[256,768]{1,0:T(8,128)(2,1)} %pad_maximum_fusion.1.refs_0_.refs_1_, bf16[13824,768]{1,0:T(8,128)(2,1)} %bitcast.97, f32[16,768]{1,0:T(8,128)} %pad_maximum_fusion.3.refs_2_.refs_4_.refs_3_.refs_5_.refs_8_.refs_9_, ...), custom_call_target="tpu_custom_call" | custom-call | flops 2717908992 | bytes 23445504 | tf_op jit(solution)/shard_map/conv_in_forward/pallas_call | solution.py:577
  137.6 89.2 %all-gather.16.cloned.1.call-done = bf16[11520,768]{1,0:T(8,128)(2,1)} async-done(((bf16[720,768]{1,0:T(8,128)(2,1)}), bf16[11520,768]{1,0:T(8,128)(2,1)}) %all-gather.16.cloned.1.call-update) | async-done | bytes 17694736 | tf_op jit(solution)/shard_map/all_gather | solution.py:872
  226.8 14.8 %block_forward.2 = (bf16[256,768]{1,0:T(8,128)(2,1)}, f32[256,768]{1,0:T(8,128)}, f32[2,32,768]{2,1,0:T(8,128)}, f32[2,32,768]{2,1,0:T(8,128)}, bf16[256,768]{1,...) custom-call(f32[256,768]{1,0:T(8,128)} %get-tuple-element.56.refs_0_.refs_4_, ...), custom_call_target="tpu_custom_call" | custom-call | flops 4529848320 | bytes 23445504 | tf_op jit(solution)/shard_map/block_forward/pallas_call | solution.py:577
  241.5 3.4 collective-permute-start.5
  245.0 1.6 collective-permute-start.7
  246.6 11.5 %collective-permute-done.7 = bf16[128,768]{1,0:T(8,128)(2,1)S(1)} collective-permute-done((bf16[128,768]{1,0:T(8,128)(2,1)S(1)}, bf16[128,768]{1,0:T(8,128)(2,1)S(1)}, u32[]{:S(2)}, u32[]{:S(2)}) %collective-permute-start.7) | collective-permute-done | bytes 196640 | tf_op jit(solution)/shard_map/ppermute | solution.py:813
  259.7 13.3 %conv_in_forward.3 = (f32[256,768]{1,0:T(8,128)}, f32[2,32,768]{2,1,0:T(8,128)}, f32[2,32,768]{2,1,0:T(8,128)}, bf16[768,256]{1,0:T(8,128)(2,1)}, bf16[768,256]{1,0:T(8,128)(2,1)}) custom-call(bf16[256,768]{1,0:T(8,128)(2,1)} %copy-done.1, bf16[256,768]{1,0:T(8,128)(2,1)} %copy-done.1, bf16[13824,768]{1,0:T(8,128)(2,1)} %bitcast.98, ...), custom_call_target="tpu_custom_call" | custom-call | flops 5435817984 | bytes 24428544 | tf_op jit(solution)/shard_map/conv_in_forward/pallas_call | solution.py:577
  273.0 16.6 %block_forward.3 = (bf16[256,768]{1,0:T(8,128)(2,1)}, f32[256,768]{1,0:T(8,128)}, f32[2,32,768]{2,1,0:T(8,128)}, f32[2,32,768]{2,1,0:T(8,128)}, bf16[256,768]{1,...) custom-call(f32[256,768]{1,0:T(8,128)} %get-tuple-element.58.refs_0_.refs_4_, ...), custom_call_target="tpu_custom_call" | custom-call | flops 4529848320 | bytes 23838720 | tf_op jit(solution)/shard_map/block_forward/pallas_call | solution.py:577
  289.6 21.1 %block_backward.2 = (bf16[256,768]{1,0:T(8,128)(2,1)}, bf16[256,2304]{1,0:T(8,128)(2,1)}, f32[256,768]{1,0:T(8,128)}, bf16[256,768]{1,0:T(8,128)(2,1)}, bf16[256...) custom-call(bf16[256,768]{1,0:T(8,128)(2,1)} %pad_maximum_fusion.2.refs_0_, ...), custom_call_target="tpu_custom_call" | custom-call | flops 4529848320 | bytes 25165824 | tf_op jit(solution)/shard_map/block_backward/pallas_call | solution.py:577
  310.7 14.4 %conv_in_backward.2 = (f32[256,768]{1,0:T(8,128)}, f32[256,768]{1,0:T(8,128)}, f32[16,768]{1,0:T(8,128)}) custom-call(bf16[256,768]{1,0:T(8,128)(2,1)} %get-tuple-element.64.refs_0_, bf16[256,768]{1,0:T(8,128)(2,1)} %copy-done.1, bf16[256,768]{1,0:T(8,128)(2,1)} %copy-done.1, f32[2,32,768]{2,1,0:T(8,128)} %get-tuple-element.65.refs_3_, ...), custom_call_target="tpu_custom_call" | custom-call | flops 5435817984 | bytes 43745280 | tf_op jit(solution)/shard_map/conv_in_backward/pallas_call | solution.py:577
  325.1 1.4 add_convert_fusion
  326.5 1.7 collective-permute-start.8
  328.2 10.8 %collective-permute-done.8.refs_0_ = bf16[256,768]{1,0:T(8,128)(2,1)S(1)} collective-permute-done((bf16[256,768]{1,0:T(8,128)(2,1)S(1)}, bf16[256,768]{1,0:T(8,128)(2,1)S(1)}, u32[]{:S(2)}, u32[]{:S(2)}) %collective-permute-start.8) | collective-permute-done | bytes 393248 | tf_op jit(solution)/shard_map/ppermute | solution.py:813
  339.7 21.1 %block_backward.3 = (bf16[256,768]{1,0:T(8,128)(2,1)}, bf16[256,2304]{1,0:T(8,128)(2,1)}, f32[256,768]{1,0:T(8,128)}, bf16[256,768]{1,0:T(8,128)(2,1)}, bf16[256...) custom-call(bf16[256,768]{1,0:T(8,128)(2,1)} %copy-done.24, ...), custom_call_target="tpu_custom_call" | custom-call | flops 4529848320 | bytes 25165824 | tf_op jit(solution)/shard_map/block_backward/pallas_call | solution.py:577
  360.8 1.1 broadcast_select_fusion
  361.9 0.8 select_convert_fusion
  365.1 1.2 convolution_convert_fusion
  366.3 3.4 pad_maximum_fusion
  369.8 0.9 copy-done.14
  371.2 4.9 maximum_select_fusion
  377.6 1.3 collective-permute-start.6
  378.9 0.9 slice.156
  379.8 5.3 collective-permute-done.6
  385.8 9.7 %conv_in_backward.3 = (f32[256,768]{1,0:T(8,128)}, f32[16,768]{1,0:T(8,128)}) custom-call(bf16[256,768]{1,0:T(8,128)(2,1)} %get-tuple-element.75.refs_0_, bf16[256,768]{1,0:T(8,128)(2,1)} %pad_maximum_fusion.1.refs_0_.refs_1_, f32[2,32,768]{2,1,0:T(8,128)} %get-tuple-element.76.refs_2_, f32[256,768]{1,0:T(8,128)} %get-tuple-element.77.refs_3_, ...), custom_call_target="tpu_custom_call" | custom-call | flops 2717908992 | bytes 24281088 | tf_op jit(solution)/shard_map/conv_in_backward/pallas_call | solution.py:577
  395.6 0.8 add_select_fusion
  396.5 1.1 slice.216
  397.5 1.4 collective-permute-start.9
  399.0 1.0 slice.157
  400.2 2.4 collective-permute-start.14
  402.7 3.1 collective-permute-done.14
  405.9 1.1 collective-permute-start.15
  407.0 1.3 collective-permute-start.11
  408.3 1.6 collective-permute-done.15
  409.9 1.6 collective-permute-start.16
  411.5 1.0 collective-permute-start.12
  412.5 1.2 collective-permute-done.16
  413.8 2.8 collective-permute-done.12
  416.7 2.6 collective-permute-start.13
  420.5 5.6 collective-permute-done.13
  426.6 7.0 %psum.7 = f32[64,48]{0,1:T(8,128)S(1)} all-reduce(f32[64,48]{0,1:T(8,128)S(1)} %fusion.20), channel_id=1, replica_groups=mesh['section'=2,'dp'=16] {'section'}, use_global_device_ids=true, to_apply=%region_1.2 | all-reduce | flops 3072 | bytes 24576 | tf_op jit(solution)/shard_map/psum | solution.py:1088
  433.6 0.9 convolution_bitcast_fusion
  434.5 1.0 fusion.17
  436.3 24.0 %reduce-scatter.2.cloned.1.call-done = bf16[48,4608]{1,0:T(8,128)(2,1)} async-done(((bf16[768,4608]{1,0:T(8,128)(2,1)}), bf16[48,4608]{1,0:T(8,128)(2,1)}) %reduce-scatter.2.cloned.1.call-update) | async-done | bytes 442384 | tf_op jit(solution)/shard_map/reduce_scatter | solution.py:1057
  460.4 1.1 convert_element_type.85
  461.4 0.9 fusion.47
  464.6 96.4 %all-gather.8.cloned.1.call-done.fields = bf16[16,2304,256]{2,1,0:T(8,128)(2,1)} async-done(((bf16[1,2304,256]{2,1,0:T(8,128)(2,1)}), bf16[16,2304,256]{2,1,0:T(8,128)(2,1)}) %all-gather.8.cloned.1.call-update) | async-done | bytes 18874384 | tf_op jit(solution)/shard_map/all_gather | solution.py:965
  561.0 17.3 %tap_slices.1 = (bf16[864,4096]{1,0:T(8,128)(2,1)}, bf16[432,4096]{1,0:T(8,128)(2,1)}) custom-call(s32[1]{0:T(128)} %bitcast.36.place, bf16[16,2304,256]{2,1,0:T(8,128)(2,1)} %all-gather.8.cloned.1.call-done.fields), custom_call_target="tpu_custom_call" | custom-call | bytes 37748736 | tf_op jit(solution)/shard_map/tap_slices/pallas_call | solution.py:762
  578.3 46.9 %all-gather.10.cloned.1.call-done = bf16[4096,768]{1,0:T(8,128)(2,1)} async-done(((bf16[256,768]{1,0:T(8,128)(2,1)}), bf16[4096,768]{1,0:T(8,128)(2,1)}) %all-gather.10.cloned.1.call-update) | async-done | bytes 6291472 | tf_op jit(solution)/shard_map/all_gather | solution.py:1042
  625.3 10.7 %convolution_bitcast_fusion.1 = f32[1,864,768]{2,1,0:T(8,128)} fusion(bf16[864,4096]{1,0:T(8,128)(2,1)} %get-tuple-element.86, bf16[4096,768]{1,0:T(8,128)(2,1)} %all-gather.10.cloned.1.call-done), kind=kOutput, calls=%fused_computation.4 | convolution fusion | flops 5435817984 | bytes 16023552 | tf_op jit(solution)/shard_map/dot_general | solution.py:46
  636.0 52.1 %all-gather.12.cloned.1.call-done = bf16[4096,768]{1,0:T(8,128)(2,1)} async-done(((bf16[256,768]{1,0:T(8,128)(2,1)}), bf16[4096,768]{1,0:T(8,128)(2,1)}) %all-gather.12.cloned.1.call-update) | async-done | bytes 6291472 | tf_op jit(solution)/shard_map/all_gather | solution.py:1041
  688.1 7.8 %convolution_bitcast_fusion.2 = f32[1,432,768]{2,1,0:T(8,128)} fusion(bf16[432,4096]{1,0:T(8,128)(2,1)} %get-tuple-element.87, bf16[4096,768]{1,0:T(8,128)(2,1)} %all-gather.12.cloned.1.call-done), kind=kOutput, calls=%fused_computation.6 | convolution fusion | flops 2717908992 | bytes 11157504 | tf_op jit(solution)/shard_map/dot_general | solution.py:46
  (178 shorter events, 18.8 us)
Async XLA Ops:
  7.2 18.7 %copy-start = (bf16[1,48,1536]{2,1,0:T(8,128)(2,1)S(1)}, bf16[1,48,1536]{2,1,0:T(8,128)(2,1)}, u32[]{:S(2)}) copy-start(bf16[1,48,1536]{2,1,0:T(8,128)(2,1)} %param.20) | copy-start | bytes 442372
  7.2 1.1 copy-start.12
  7.2 1.2 copy-start.25
  7.2 1.2 copy-start.29
  7.2 1.2 copy-start.28
  7.2 122.2 %all-gather.14.cloned.1.call-start = ((), (), s32[]{:S(2)}) async-start(), calls=%async_computation.6 | async-start | bytes 22560768 | tf_op jit(solution)/shard_map/all_gather | solution.py:870
  8.0 1.5 copy-start.34
  8.0 1.7 copy-start.35
  8.0 1.7 copy-start.33
  8.0 1.7 copy-start.37
  8.0 218.8 %all-gather.16.cloned.1.call-start = ((), (), s32[]{:S(2)}) async-start(), calls=%async_computation.7 | async-start | bytes 18800640 | tf_op jit(solution)/shard_map/all_gather | solution.py:872
  8.4 17.1 %copy-start.36 = (bf16[1000,48]{0,1:T(8,128)(2,1)S(1)}, bf16[1000,48]{0,1:T(8,128)(2,1)}, u32[]{:S(2)}) copy-start(bf16[1000,48]{0,1:T(8,128)(2,1)} %param.17) | copy-start | bytes 288004
  8.5 1.0 copy-start.3
  9.8 1.3 collective-permute-start.1
  10.4 23.3 %copy-start.26 = (bf16[4,1,32,768]{3,2,1,0:T(8,128)(2,1)S(1)}, bf16[4,1,32,768]{3,2,1,0:T(8,128)(2,1)}, u32[]{:S(2)}) copy-start(bf16[4,1,32,768]{3,2,1,0:T(8,128)(2,1)} %param.15) | copy-start | bytes 589828
  11.2 4.5 collective-permute-start.2
  15.7 3.9 collective-permute-start.3
  19.6 5.5 collective-permute-start.4
  27.0 25.3 %all-to-all-start = ((f32[16,4,1536]{2,1,0:T(4,128)}), f32[16,4,1536]{2,1,0:T(4,128)S(1)}, u32[]{:S(2)}, u32[]{:S(2)}) async-start(f32[16,4,1536]{2,1,0:T(4,128)} %copy.67), calls=%async_computation | async-start | bytes 786432 | tf_op jit(solution)/shard_map/all_to_all | solution.py:909
  33.6 426.8 %reduce-scatter.2.cloned.1.call-start = ((), (), s32[]{:S(2)}) async-start(), calls=%async_computation.5 | async-start | bytes 7520256 | tf_op jit(solution)/shard_map/reduce_scatter | solution.py:1057
  33.7 9.1 %collective-permute-start = (bf16[128,768]{1,0:T(8,128)(2,1)S(1)}, bf16[128,768]{1,0:T(8,128)(2,1)S(1)}, u32[]{:S(2)}, u32[]{:S(2)}) collective-permute-start(bf16[128,768]{1,0:T(8,128)(2,1)S(1)} %bitcast.105), channel_id=1, source_target_pairs={{16,0},{17,1},{18,2},{19,3},{20,4},{21,5},{22,6},{23,7},{24,8},{25... | collective-permute-start | bytes 589832 | tf_op jit(solution)/shard_map/ppermute | solution.py:813
  226.8 18.2 %copy-start.27 = (bf16[4,1,32,768]{3,2,1,0:T(8,128)(2,1)S(1)}, bf16[4,1,32,768]{3,2,1,0:T(8,128)(2,1)}, u32[]{:S(2)}) copy-start(bf16[4,1,32,768]{3,2,1,0:T(8,128)(2,1)} %param.16) | copy-start | bytes 589828
  241.5 17.4 %collective-permute-start.5 = (bf16[256,768]{1,0:T(8,128)(2,1)}, bf16[256,768]{1,0:T(8,128)(2,1)S(1)}, u32[]{:S(2)}, u32[]{:S(2)}) collective-permute-start(bf16[256,768]{1,0:T(8,128)(2,1)} %get-tuple-element.57), channel_id=1, source_target_pairs={{0,16},{1,17},{2,18},{3,19},{4,20},{5,21},{6,22},{7,23},{8,24},{9,... | collective-permute-start | bytes 1179656 | tf_op jit(solution)/shard_map/ppermute | solution.py:813
  245.0 13.2 %collective-permute-start.7 = (bf16[128,768]{1,0:T(8,128)(2,1)S(1)}, bf16[128,768]{1,0:T(8,128)(2,1)S(1)}, u32[]{:S(2)}, u32[]{:S(2)}) collective-permute-start(bf16[128,768]{1,0:T(8,128)(2,1)S(1)} %bitcast.108), channel_id=1, source_target_pairs={{0,16},{1,17},{2,18},{3,19},{4,20},{5,21},{6,22},{7,23},{8,24},{9,... | collective-permute-start | bytes 589832 | tf_op jit(solution)/shard_map/ppermute | solution.py:813
  258.9 0.7 copy-start.1
  326.5 12.5 %collective-permute-start.8 = (bf16[256,768]{1,0:T(8,128)(2,1)S(1)}, bf16[256,768]{1,0:T(8,128)(2,1)S(1)}, u32[]{:S(2)}, u32[]{:S(2)}) collective-permute-start(bf16[256,768]{1,0:T(8,128)(2,1)S(1)} %add_convert_fusion), channel_id=1, source_target_pairs={{16,0},{17,1},{18,2},{19,3},{20,4},{21,5},{22,6},{23,7},{24,8},{25... | collective-permute-start | bytes 1179656 | tf_op jit(solution)/shard_map/ppermute | solution.py:813
  339.0 0.7 copy-start.24
  339.7 21.1 %copy-start.5 = (bf16[256,768]{1,0:T(8,128)(2,1)S(1)}, bf16[256,768]{1,0:T(8,128)(2,1)}, u32[]{:S(2)}) copy-start(bf16[256,768]{1,0:T(8,128)(2,1)} %get-tuple-element.68.refs_6_) | copy-start | bytes 1179652
  339.7 22.2 %copy-start.2 = (bf16[256,768]{1,0:T(8,128)(2,1)S(1)}, bf16[256,768]{1,0:T(8,128)(2,1)}, u32[]{:S(2)}) copy-start(bf16[256,768]{1,0:T(8,128)(2,1)} %copy-done.1) | copy-start | bytes 1179652
  361.9 0.9 copy-start.6
  362.8 1.0 copy-start.19
  362.8 1.1 copy-start.20
  362.8 1.2 copy-start.21
  362.8 1.3 copy-start.22
  362.8 1.9 copy-start.11
  363.0 1.7 copy-start.8
  363.0 2.1 copy-start.9
  363.0 2.1 copy-start.10
  369.7 1.0 copy-start.14
  369.7 1.1 copy-start.15
  369.7 1.2 copy-start.16
  369.7 1.3 copy-start.17
  369.7 1.5 copy-start.18
  369.8 191.2 %all-gather.8.cloned.1.call-start = ((), (), s32[]{:S(2)}) async-start(), calls=%async_computation.2 | async-start | bytes 20054016 | tf_op jit(solution)/shard_map/all_gather | solution.py:965
  371.2 4.9 copy-start.4
  371.2 4.9 copy-start.7
  376.0 1.5 copy-start.23
  376.1 249.2 %all-gather.10.cloned.1.call-start = ((), (), s32[]{:S(2)}) async-start(), calls=%async_computation.3 | async-start | bytes 6684672 | tf_op jit(solution)/shard_map/all_gather | solution.py:1042
  376.9 311.2 %all-gather.12.cloned.1.call-start = ((), (), s32[]{:S(2)}) async-start(), calls=%async_computation.4 | async-start | bytes 6684672 | tf_op jit(solution)/shard_map/all_gather | solution.py:1041
  377.6 7.6 %collective-permute-start.6 = (bf16[128,768]{1,0:T(8,128)(2,1)S(1)}, bf16[128,768]{1,0:T(8,128)(2,1)S(1)}, u32[]{:S(2)}, u32[]{:S(2)}) collective-permute-start(bf16[128,768]{1,0:T(8,128)(2,1)S(1)} %slice.124), channel_id=1, source_target_pairs={{16,0},{17,1},{18,2},{19,3},{20,4},{21,5},{22,6},{23,7},{24,8},{25... | collective-permute-start | bytes 589832 | tf_op jit(solution)/shard_map/ppermute | solution.py:813
  385.8 9.7 %copy-start.30 = (f32[16,768]{1,0:T(8,128)S(1)}, f32[16,768]{1,0:T(8,128)}, u32[]{:S(2)}) copy-start(f32[16,768]{1,0:T(8,128)} %get-tuple-element.97) | copy-start | bytes 147460
  385.8 9.7 %copy-start.31 = (f32[16,768]{1,0:T(8,128)S(1)}, f32[16,768]{1,0:T(8,128)}, u32[]{:S(2)}) copy-start(f32[16,768]{1,0:T(8,128)} %get-tuple-element.98) | copy-start | bytes 147460
  385.8 9.7 %copy-start.32 = (f32[16,768]{1,0:T(8,128)S(1)}, f32[16,768]{1,0:T(8,128)}, u32[]{:S(2)}) copy-start(f32[16,768]{1,0:T(8,128)} %get-tuple-element.99) | copy-start | bytes 147460
  396.4 39.1 %copy-start.13 = (f32[256,768]{1,0:T(8,128)S(1)}, f32[256,768]{1,0:T(8,128)}, u32[]{:S(2)}) copy-start(f32[256,768]{1,0:T(8,128)} %get-tuple-element.78) | copy-start | bytes 2359300
  397.5 38.0 %collective-permute-start.9 = (bf16[128,768]{1,0:T(8,128)(2,1)S(1)}, bf16[128,768]{1,0:T(8,128)(2,1)S(1)}, u32[]{:S(2)}, u32[]{:S(2)}) collective-permute-start(bf16[128,768]{1,0:T(8,128)(2,1)S(1)} %slice.216), channel_id=1, source_target_pairs={{0,16},{1,17},{2,18},{3,19},{4,20},{5,21},{6,22},{7,23},{8,24},{9,... | collective-permute-start | bytes 589832 | tf_op jit(solution)/shard_map/ppermute | solution.py:813
  400.2 5.6 collective-permute-start.14
  402.6 4.4 collective-permute-start.10
  405.9 4.0 collective-permute-start.15
  407.0 4.4 collective-permute-start.11
  409.9 3.8 collective-permute-start.16
  411.5 5.1 collective-permute-start.12
  413.7 5.6 collective-permute-start.17
  416.7 9.4 %collective-permute-start.13 = (bf16[8,4,1536]{2,1,0:T(4,128)(2,1)S(1)}, bf16[8,4,1536]{2,1,0:T(4,128)(2,1)S(1)}, u32[]{:S(2)}, u32[]{:S(2)}) collective-permute-start(bf16[8,4,1536]{2,1,0:T(4,128)(2,1)S(1)} %maximum_select_fusion.4), channel_id=1, source_target_pairs={{0,8},{1,9},{2,10},{3,11},{4,12},{5,13},{6,14},{7,15},{8,0},{9,1},... | collective-permute-start | bytes 294920 | tf_op jit(solution)/shard_map/ppermute | solution.py:790
Sparse Core Ops, SparseCore 0:
  9.7 119.6 all-gather.13
  131.6 95.1 all-gather.15
  369.9 90.4 reduce-scatter.1
  462.5 98.4 all-gather.7
  563.4 61.8 all-gather.9
  627.6 60.4 all-gather.11

commit v2 on v1

v2 whole, which is shorter than its diff:
```python
import math
from functools import partial

import jax
import jax.numpy as jnp
import numpy as np
from jax import lax
from jax.experimental import pallas as pl
from jax.experimental.pallas import tpu as pltpu
from jax.sharding import PartitionSpec as P

WIDTH = 768
EMBED = 768
CLASSES = 1000
HEAD_DIM = 64
GROUPS = 32
SIDE = 8
LEVELS = 40
MICRO = 4
PIXELS = 64
TAPS = 9

EPS = 1e-05
SIGMA_LOW = 0.002
SIGMA_HIGH = 80.0

ACTIVE = "active"
ATTEND = "attend"
BEFORE = "before_"
BLOCK = "block_"
COLS_NAME = "cols"
COLS = "cols_"
COLUMNS_W = "columns_w"
CONV_IN = "conv_in"
CONV_ONE = "conv_one"
CONV_OUT = "conv_out"
DP = "dp"
FIELDS = "fields"
GRAD_HIDDEN = "grad_hidden"
GRAD_JOINED = "grad_joined"
GRAD_OUT = "grad_out"
GRAD_RESID = "grad_resid"
GRAD_RESID_B = "grad_resid_b"
GRAD_SKIPPED = "grad_skipped"
HELD = "held_"
HIDDEN = "hidden"
KEY = "key"
MIDDLE = "middle"
MIXED = "mixed"
MODULATION = "modulation"
OUT_NAME = "out"
OUT = "out_"
OUT_SEMS = "out_sems"
PAYLOAD = "payload"
PLANES = "planes"
PRIOR = "prior_"
PRODUCTS = "products"
PROJECT = "project"
QUERY = "query"
RESIDUAL = "residual"
RESULT = "result"
SECTION = "section"
SKIP = "skip"
SKIPPED = "skipped"
SOURCE = "source_"
STAT_C = "stat_c"
STAT_H = "stat_h"
STAT_R = "stat_r"
STAT_S = "stat_s"
SUMS = "sums"
TAKEN = "taken"
TOTAL = "total_"
VALUE = "value"

F32 = jnp.float32
BF16 = jnp.bfloat16
LANE = 128
CHUNKS = WIDTH // LANE
PER_GROUP = WIDTH // GROUPS
GROUP_SHARE = 1.0 / (PER_GROUP * PIXELS)
VMEM_LIMIT = 60 * 2**20

GAIN = 0
BIAS = 4

GROUP_OF = (np.arange(WIDTH)[:, None] // PER_GROUP == np.arange(LANE)[None, :]).astype(np.float32)


def lanes(chunk):
    return pl.ds(chunk * LANE, LANE)


def dot(left, right):
    return jnp.dot(left, right, preferred_element_type=F32)


def dot_nt(left, right):
    return lax.dot_general(left, right, (((1,), (1,)), ((), ())), preferred_element_type=F32)


def dot_tn(left, right):
    return lax.dot_general(left, right, (((0,), (0,)), ((), ())), preferred_element_type=F32)


def octet_sum(values, octets):
    width = values.shape[-1]
    partial_sums = values.reshape(SIDE, octets, width).sum(axis=0).reshape(octets // 8, 8, width)
    totals = jnp.sum(partial_sums, axis=1, keepdims=True)
    return jnp.broadcast_to(totals, partial_sums.shape).reshape(octets, width)


def over_rows(stat):
    octets, width = stat.shape
    return jnp.broadcast_to(stat[None], (SIDE, octets, width)).reshape(SIDE * octets, width)


def in_parts(values):
    first = values.astype(BF16)
    rest = values - first.astype(F32)
    second = rest.astype(BF16)
    third = (rest - second.astype(F32)).astype(BF16)
    return jnp.concatenate([first, second, third], axis=0)


def group_mean(sums, group_of, group_of_t):
    count = sums.shape[0]
    grouped = dot(in_parts(sums), group_of)
    grouped = (grouped[:count] + grouped[count : 2 * count] + grouped[2 * count :]) * GROUP_SHARE
    spread = dot(in_parts(grouped), group_of_t)
    return spread[:count] + spread[count : 2 * count] + spread[2 * count :]


def norm_stats(read, octets, group_of, group_of_t):
    sums = jnp.concatenate([octet_sum(read(c), octets) for c in range(CHUNKS)], axis=1)
    mean = group_mean(sums, group_of, group_of_t)
    squares = []
    for c in range(CHUNKS):
        centered = read(c) - over_rows(mean[:, c * LANE : (c + 1) * LANE])
        squares.append(octet_sum(centered * centered, octets))
    spread = group_mean(jnp.concatenate(squares, axis=1), group_of, group_of_t)
    return mean, lax.rsqrt(spread + EPS)


def normed_chunk(values, stat_ref, c):
    mean = stat_ref[0, :, lanes(c)]
    inv = stat_ref[1, :, lanes(c)]
    return (values - over_rows(mean)) * over_rows(inv)


def sigmoid(values):
    return 1.0 / (1.0 + jnp.exp(-values))


def silu_slope(values):
    gate = sigmoid(values)
    return gate * (1.0 + values * (1.0 - gate))


def put_shifted(planes, base, values, c, octets):
    rows = values.shape[0]
    column = lax.broadcasted_iota(jnp.int32, values.shape, 0) & 7
    before = jnp.where(column != 0, pltpu.roll(values, 1, 0), 0.0)
    after = jnp.where(column != 7, pltpu.roll(values, rows - 1, 0), 0.0)
    planes[base, pl.ds(octets, rows), lanes(c)] = before.astype(BF16)
    planes[base + 1, pl.ds(octets, rows), lanes(c)] = values.astype(BF16)
    planes[base + 2, pl.ds(octets, rows), lanes(c)] = after.astype(BF16)


def clear_edges(planes, octets):
    count, rows, width = planes.shape
    edge = jnp.zeros((count, octets, width), BF16)
    planes[:, pl.ds(0, octets), :] = edge
    planes[:, pl.ds(rows - octets, octets), :] = edge


def row_total(values):
    return jnp.sum(values, axis=0, keepdims=True)


def norm_back(read_grad, read_normed, gain_of, stat_ref, octets, tables, write, sums_out):
    group_of, group_of_t = tables
    first, second = [], []
    for c in range(CHUNKS):
        grad = read_grad(c)
        first.append(octet_sum(grad, octets))
        second.append(octet_sum(grad * read_normed(c), octets))
    first = jnp.concatenate(first, axis=1)
    second = jnp.concatenate(second, axis=1)
    sums_out(first, second)
    gain = gain_of(None)
    both = group_mean(jnp.concatenate([first * gain, second * gain], axis=0), group_of, group_of_t)
    for c in range(CHUNKS):
        part = slice(c * LANE, (c + 1) * LANE)
        inv = over_rows(stat_ref[1, :, lanes(c)])
        mean_one = over_rows(both[:octets, part])
        mean_two = over_rows(both[octets:, part])
        write(c, inv * (gain_of(c) * read_grad(c) - mean_one - read_normed(c) * mean_two))


class Weights:
    def __init__(self, sources, plan, sems):
        self.sources, self.plan, self.sems, self.waits, self.used = sources, plan, sems, {}, 0

    def fetch(self, name, held):
        self.waits[name] = []
        for source, piece, row, target, count in self.plan[name]:
            copy = pltpu.make_async_copy(
                self.sources[source].at[piece, pl.ds(row, count)],
                held.at[pl.ds(target, count)],
                self.sems.at[self.used],
            )
            copy.start()
            self.used += 1
            self.waits[name].append([target, copy])

    def need(self, name, stop):
        for entry in self.waits[name]:
            if entry[0] < stop and entry[1] is not None:
                entry[1].wait()
                entry[1] = None


def copies_of(plan, *names):
    return pltpu.SemaphoreType.DMA((sum(len(plan[name]) for name in names),))


SMALL = (QUERY, KEY, VALUE, OUT_NAME)


def held_at(r, name):
    if name in SMALL[:3]:
        return r.held_qkv.at[SMALL.index(name)]
    return getattr(r, HELD + name)


def held_scratch(decoder, names):
    sizes = {CONV_IN: (1 + decoder) * TAPS * WIDTH, CONV_OUT: TAPS * WIDTH, OUT_NAME: WIDTH, SKIP: 2 * WIDTH}
    scratch = {HELD + name: pltpu.VMEM((sizes[name], WIDTH), BF16) for name in names if name in sizes}
    if QUERY in names:
        scratch["held_qkv"] = pltpu.VMEM((3, WIDTH, WIDTH), BF16)
    return scratch


def head_pair(values, left):
    zero = jnp.zeros_like(values)
    return jnp.concatenate([jnp.where(left, values, zero), jnp.where(left, zero, values)], axis=0)


def attention_of(keys, queries):
    scores = [dot_nt(k, q) * (1.0 / math.sqrt(HEAD_DIM)) for k, q in zip(keys, queries)]
    tops = [jnp.max(part, axis=0, keepdims=True) for part in scores]
    weights = [jnp.exp(part - top) for part, top in zip(scores, tops)]
    totals = [1.0 / jnp.sum(part, axis=0, keepdims=True) for part in weights]
    return [part * total for part, total in zip(weights, totals)]


AT_ONCE = 4


def image_groups(images):
    every = [(image, pl.ds(image * PIXELS, PIXELS), pair) for image in range(images) for pair in range(CHUNKS)]
    return [every[start : start + AT_ONCE * CHUNKS] for start in range(0, len(every), AT_ONCE * CHUNKS)]


def by_image(scratch, image, chunk):
    part = scratch[:, image, :, lanes(chunk)]
    return part.reshape(PIXELS, LANE)


def put_image(scratch, image, chunk, values):
    scratch[:, image, :, lanes(chunk)] = values.reshape(SIDE, 8, LANE)


def conv_in_forward(r, decoder, shared, octets):
    rows = r.hidden.shape[0]
    tables = (r.group_of[...], r.group_of_t[...])
    sides = [(r.hidden, r.stat_h, 0)] + ([(r.skipped, r.stat_s, 1)] if decoder else [])
    span = WIDTH * len(sides)
    clear_edges(r.planes, octets)
    for source, stat, which in sides:
        mean, inv = norm_stats(lambda c: source[:, lanes(c)].astype(F32), octets, *tables)
        stat[0] = mean
        stat[1] = inv
        if shared and not which:
            for index, values in enumerate((mean, 1.0 / inv)):
                grouped = dot(values.astype(BF16), tables[0]) * (1.0 / PER_GROUP)
                r.turned[pl.ds(WIDTH + index * GROUPS, GROUPS), :] = over_rows(grouped).T[:GROUPS].astype(BF16)
        for c in range(CHUNKS):
            normed = normed_chunk(source[:, lanes(c)].astype(F32), stat, c)
            value = (
                normed * r.params[pl.ds(GAIN + which, 1), lanes(c)]
                + r.params[pl.ds(BIAS + which, 1), lanes(c)]
            )
            value = value * sigmoid(value)
            put_shifted(r.planes, 3 * which, value, c, octets)
            if not (shared and which):
                r.turned[pl.ds(which * WIDTH + c * LANE, LANE), :] = normed.T.astype(BF16)
    for tap in range(TAPS):
        r.weights.need(CONV_IN, (tap + 1) * span)
        for half in range(len(sides)):
            part = dot(
                r.planes[3 * half + tap % 3, pl.ds(octets * (tap // 3), rows), :],
                r.held_conv_in[pl.ds(tap * span + half * WIDTH, WIDTH), :],
            )
            if tap == 0 and half == 0:
                r.conv_one[...] = part + r.params[pl.ds(BIAS + 2, 1), :]
            else:
                r.conv_one[...] += part
    r.flush(CONV_ONE)
    mean, inv = norm_stats(lambda c: r.conv_one[:, lanes(c)], octets, *tables)
    r.stat_c[0] = mean
    r.stat_c[1] = inv
    for c in range(CHUNKS):
        normed = (
            normed_chunk(r.conv_one[:, lanes(c)], r.stat_c, c) * r.params[pl.ds(GAIN + 2, 1), lanes(c)]
            + r.params[pl.ds(BIAS + 5, 1), lanes(c)]
        )
        scale = over_rows(r.modulation[:, lanes(c)])
        shift = over_rows(r.modulation[:, lanes(CHUNKS + c)])
        value = normed * (1.0 + scale) + shift
        value = value * sigmoid(value)
        r.middle[:, lanes(c)] = value.astype(BF16)
        r.turned_w[lanes(c), :] = value.T.astype(BF16)
    r.flush(MIDDLE, STAT_C)
    r.leave(r.turned, r.fields, r.fields_sems.at[0])
    r.leave(r.turned_w, r.columns_w, r.fields_sems.at[1])


def block_forward(r, decoder, octets):
    rows = r.hidden.shape[0]
    images = octets // 8
    tables = (r.group_of[...], r.group_of_t[...])
    clear_edges(r.planes, octets)
    for c in range(CHUNKS):
        put_shifted(r.planes, 0, r.middle[:, lanes(c)].astype(F32), c, octets)
    for tap in range(TAPS):
        r.weights.need(CONV_OUT, (tap + 1) * WIDTH)
        part = dot(
            r.planes[tap % 3, pl.ds(octets * (tap // 3), rows), :], r.held_conv_out[pl.ds(tap * WIDTH, WIDTH), :]
        )
        if tap == 0:
            r.residual[...] = part + r.params[pl.ds(BIAS + 6, 1), :]
        else:
            r.residual[...] += part
    if decoder:
        r.weights.need(SKIP, 2 * WIDTH)
        r.residual[...] += (
            dot(r.hidden[...], r.held_skip[pl.ds(0, WIDTH), :])
            + dot(r.skipped[...], r.held_skip[pl.ds(WIDTH, WIDTH), :])
            + r.params[pl.ds(BIAS + 7, 1), :]
        )
    else:
        r.residual[...] += r.hidden[...].astype(F32)
    r.flush(RESIDUAL)
    mean, inv = norm_stats(lambda c: r.residual[:, lanes(c)], octets, *tables)
    r.stat_r[0] = mean
    r.stat_r[1] = inv
    for c in range(CHUNKS):
        r.attend[:, lanes(c)] = (
            normed_chunk(r.residual[:, lanes(c)], r.stat_r, c) * r.params[pl.ds(GAIN + 3, 1), lanes(c)]
            + r.params[pl.ds(BIAS + 8, 1), lanes(c)]
        ).astype(BF16)
    r.flush(ATTEND)
    for index, (name, bias) in enumerate(((QUERY, 9), (KEY, None), (VALUE, 10))):
        r.weights.need(name, WIDTH)
        part = dot(r.attend[...], r.held_qkv[index])
        if bias is not None:
            part = part + r.params[pl.ds(BIAS + bias, 1), :]
        part = part.reshape(SIDE, images, 8, WIDTH)
        for image in range(images):
            own = part[:, image].reshape(PIXELS, WIDTH).astype(BF16)
            r.project[pl.ds(image * PIXELS, PIXELS), pl.ds(index * WIDTH, WIDTH)] = own
    r.flush(PROJECT)
    left = lax.broadcasted_iota(jnp.int32, (PIXELS, LANE), 1) < HEAD_DIM
    for group in image_groups(images):
        queries = [head_pair(r.project[span, lanes(pair)], left) for _, span, pair in group]
        keys_h = [r.project[span, lanes(CHUNKS + pair)] for _, span, pair in group]
        values_h = [r.project[span, lanes(2 * CHUNKS + pair)] for _, span, pair in group]
        attention = [part.astype(BF16) for part in attention_of(keys_h, queries)]
        both = [dot_tn(part, values) for part, values in zip(attention, values_h)]
        for (image, _, pair), part in zip(group, both):
            put_image(r.grid, image, pair, jnp.where(left, part[:PIXELS], part[PIXELS:]))
    r.mixed[...] = r.grid[:, :, :, pl.ds(0, WIDTH)].reshape(rows, WIDTH).astype(BF16)
    r.flush(MIXED)
    r.weights.need(OUT_NAME, WIDTH)
    r.result[...] = (
        r.residual[...] + dot(r.mixed[...], r.held_out[...]) + r.params[pl.ds(BIAS + 11, 1), :]
    ).astype(BF16)


def attention_backward(r, decoder, octets, shards, with_skip):
    rows = r.residual.shape[0]
    images = octets // 8
    tables = (r.group_of[...], r.group_of_t[...])

    def put_sum(row, c, values):
        r.sums[pl.ds(row, 1), lanes(c)] = row_total(values)

    def leave(first, width):
        part = pl.ds(first * WIDTH, width * WIDTH)
        r.leave(r.built.at[:, part], r.products.at[:, part], r.built_sems.at[min(first, 2)])

    top = r.grad_out[...].astype(BF16)
    for c in range(CHUNKS):
        put_sum(BIAS + 11, c, r.grad_out[:, lanes(c)].astype(BF16).astype(F32))
    r.built[:, pl.ds(3 * WIDTH, WIDTH)] = dot_tn(r.mixed[...], top).astype(BF16)
    leave(3, 1)
    r.weights.need(OUT_NAME, WIDTH)
    r.grid[:, :, :, pl.ds(0, WIDTH)] = dot_nt(top, r.held_out[...]).reshape(SIDE, images, 8, WIDTH)
    left = lax.broadcasted_iota(jnp.int32, (PIXELS, LANE), 1) < HEAD_DIM
    root = 1.0 / math.sqrt(HEAD_DIM)
    for group in image_groups(images):
        queries = [head_pair(r.project[span, lanes(pair)], left) for _, span, pair in group]
        keys_h = [r.project[span, lanes(CHUNKS + pair)] for _, span, pair in group]
        values_h = [r.project[span, lanes(2 * CHUNKS + pair)] for _, span, pair in group]
        grads_h = [head_pair(by_image(r.grid, image, pair).astype(BF16), left) for image, _, pair in group]
        attention = attention_of(keys_h, queries)
        weighted = [dot_nt(v, g) * part for v, g, part in zip(values_h, grads_h, attention)]
        totals = [jnp.sum(part, axis=0, keepdims=True) for part in weighted]
        scores = [(w - part * total).astype(BF16) for w, part, total in zip(weighted, attention, totals)]
        both = [dot_tn(part, k) * root for part, k in zip(scores, keys_h)]
        grad_keys = [dot(part, q) * root for part, q in zip(scores, queries)]
        grad_values = [dot(part.astype(BF16), g) for part, g in zip(attention, grads_h)]
        for index, (image, _, pair) in enumerate(group):
            put_image(r.grid, image, pair, jnp.where(left, both[index][:PIXELS], both[index][PIXELS:]))
            put_image(r.grid, image, CHUNKS + pair, grad_keys[index])
            put_image(r.grid, image, 2 * CHUNKS + pair, grad_values[index])
    for index in range(3):
        for pair in range(CHUNKS):
            chunk = lanes(index * CHUNKS + pair)
            joined = r.grid[:, :, :, chunk].reshape(rows, LANE).astype(BF16)
            r.grad_project[:, chunk] = joined
            if index == 0:
                put_sum(BIAS + 9, pair, joined.astype(F32))
            if index == 2:
                put_sum(BIAS + 10, pair, joined.astype(F32))
    for index in range(3):
        columns = pl.ds(index * WIDTH, WIDTH)
        r.built[:, columns] = dot_tn(r.attend[...], r.grad_project[:, columns]).astype(BF16)
    leave(0, 3)
    for index, name in enumerate(SMALL[:3]):
        r.weights.need(name, WIDTH)
        part = dot_nt(r.grad_project[:, pl.ds(index * WIDTH, WIDTH)], r.held_qkv[index])
        if index == 0:
            r.work[...] = part
        else:
            r.work[...] += part

    def gain_attend(c):
        return r.params[pl.ds(GAIN + 3, 1), :] if c is None else r.params[pl.ds(GAIN + 3, 1), lanes(c)]

    def sums_attend(first, second):
        r.sums[pl.ds(BIAS + 8, 1), :] = row_total(first) * 0.125
        r.sums[pl.ds(GAIN + 3, 1), :] = row_total(second) * 0.125

    def write_resid(c, grad):
        total = r.grad_out[:, lanes(c)].astype(F32) + grad
        r.grad_resid[:, lanes(c)] = total
        rounded = total.astype(BF16)
        r.grad_resid_b[:, lanes(c)] = rounded
        rounded = rounded.astype(F32)
        put_sum(BIAS + 6, c, rounded)
        if decoder:
            put_sum(BIAS + 7, c, rounded)

    norm_back(
        lambda c: r.work[:, lanes(c)],
        lambda c: normed_chunk(r.residual[:, lanes(c)], r.stat_r, c),
        gain_attend,
        r.stat_r,
        octets,
        tables,
        write_resid,
        sums_attend,
    )
    r.flush(GRAD_RESID, GRAD_RESID_B)
    if with_skip:
        share = WIDTH // shards
        for side, source in enumerate((r.hidden, r.skipped)):
            first = side * shards // 2
            if decoder:
                part = dot_tn(source[...], r.grad_resid_b[...]).astype(BF16)
            else:
                part = jnp.zeros((WIDTH, WIDTH), BF16)
            for index in range(shards // 2):
                target = pl.ds((first + index) * share, share)
                for half in range(2):
                    r.built[target, pl.ds((4 + half) * WIDTH, WIDTH)] = part[
                        (2 * index + half) * share : (2 * index + half + 1) * share
                    ]
        part = pl.ds(4 * WIDTH, 2 * WIDTH)
        r.leave(r.built.at[:, part], r.products.at[:, part], r.built_sems.at[1])


def middle_backward(r, octets):
    rows = r.conv_one.shape[0]
    tables = (r.group_of[...], r.group_of_t[...])
    clear_edges(r.planes, octets)
    r.rows[pl.ds(0, rows), :] = r.grad_resid_b[...]
    for c in range(CHUNKS):
        put_shifted(r.planes, 0, r.grad_resid_b[:, lanes(c)].astype(F32), c, octets)
    for tap in range(TAPS):
        r.weights.need(CONV_OUT, (tap + 1) * WIDTH)
        part = dot_nt(
            r.planes[2 - tap % 3, pl.ds(octets * (2 - tap // 3), rows), :],
            r.held_conv_out[pl.ds(tap * WIDTH, WIDTH), :],
        )
        if tap == 0:
            r.work[...] = part
        else:
            r.work[...] += part
    for c in range(CHUNKS):
        normed = (
            normed_chunk(r.conv_one[:, lanes(c)], r.stat_c, c) * r.params[pl.ds(GAIN + 2, 1), lanes(c)]
            + r.params[pl.ds(BIAS + 5, 1), lanes(c)]
        )
        scale = over_rows(r.modulation[:, lanes(c)])
        shift = over_rows(r.modulation[:, lanes(CHUNKS + c)])
        r.work[:, lanes(c)] = r.work[:, lanes(c)] * silu_slope(normed * (1.0 + scale) + shift)

    def gain_middle(c):
        if c is None:
            return r.params[pl.ds(GAIN + 2, 1), :] * (1.0 + r.modulation[:, pl.ds(0, WIDTH)])
        return over_rows(r.params[pl.ds(GAIN + 2, 1), lanes(c)] * (1.0 + r.modulation[:, lanes(c)]))

    def sums_middle(first, second):
        scaled = 1.0 + r.modulation[:, pl.ds(0, WIDTH)]
        r.sums[pl.ds(BIAS + 5, 1), :] = row_total(first * scaled) * 0.125
        r.sums[pl.ds(GAIN + 2, 1), :] = row_total(second * scaled) * 0.125
        grad_scale = (
            r.params[pl.ds(GAIN + 2, 1), :] * second + r.params[pl.ds(BIAS + 5, 1), :] * first
        ).astype(BF16)
        grad_shift = first.astype(BF16)
        images = octets // 8
        row = lax.broadcasted_iota(jnp.int32, (16, octets), 0)
        column = lax.broadcasted_iota(jnp.int32, (16, octets), 1)
        for index, part in enumerate((grad_scale, grad_shift)):
            taken = ((row - index * images) * 8 == column) & (row >= index * images)
            chosen = dot(jnp.where(taken, 1.0, 0.0).astype(BF16), part)
            compact = chosen if index == 0 else compact + chosen
        r.rows[pl.ds(2 * rows, 16), :] = compact.astype(BF16)
        r.sums[pl.ds(BIAS + 3, 1), :] = row_total(grad_scale.astype(F32)) * 0.125
        r.sums[pl.ds(BIAS + 4, 1), :] = row_total(grad_shift.astype(F32)) * 0.125

    def write_conv(c, grad):
        rounded = grad.astype(BF16)
        r.grad_conv_b[:, lanes(c)] = rounded
        r.rows[pl.ds(rows, rows), lanes(c)] = rounded
        r.sums[pl.ds(BIAS + 2, 1), lanes(c)] = row_total(rounded.astype(F32))

    norm_back(
        lambda c: r.work[:, lanes(c)],
        lambda c: normed_chunk(r.conv_one[:, lanes(c)], r.stat_c, c),
        gain_middle,
        r.stat_c,
        octets,
        tables,
        write_conv,
        sums_middle,
    )
    r.leave(r.rows, r.payload, r.payload_sem)


def conv_in_backward(r, decoder, joined, octets):
    rows = r.hidden.shape[0]
    tables = (r.group_of[...], r.group_of_t[...])
    sides = [(r.hidden, r.stat_h, r.total if joined else r.grad_hidden, 0)]
    if decoder:
        sides.append((r.skipped, r.stat_s, r.total if joined else r.grad_skipped, 1))
    span = WIDTH * len(sides)
    clear_edges(r.planes, octets)
    for c in range(CHUNKS):
        put_shifted(r.planes, 0, r.grad_conv_b[:, lanes(c)].astype(F32), c, octets)
    for tap in range(TAPS):
        r.weights.need(CONV_IN, (tap + 1) * span)
        for _, _, _, half in sides:
            part = dot_nt(
                r.planes[2 - tap % 3, pl.ds(octets * (2 - tap // 3), rows), :],
                r.held_conv_in[pl.ds(tap * span + half * WIDTH, WIDTH), :],
            )
            if tap == 0:
                r.sides[half] = part
            else:
                r.sides[half] += part
    if decoder:
        r.weights.need(SKIP, 2 * WIDTH)
    for source, stat, target, which in sides:

        def normed_of(c, source=source, stat=stat):
            return normed_chunk(source[:, lanes(c)].astype(F32), stat, c)

        def gain_input(c, which=which):
            row = pl.ds(GAIN + which, 1)
            return r.params[row, :] if c is None else r.params[row, lanes(c)]

        for c in range(CHUNKS):
            value = normed_of(c) * gain_input(c) + r.params[pl.ds(BIAS + which, 1), lanes(c)]
            r.sides[which, :, lanes(c)] = r.sides[which, :, lanes(c)] * silu_slope(value)

        def sums_input(first, second, which=which):
            r.sums[pl.ds(BIAS + which, 1), :] = row_total(first) * 0.125
            r.sums[pl.ds(GAIN + which, 1), :] = row_total(second) * 0.125

        if decoder:
            part = dot_nt(r.grad_resid_b[...], r.held_skip[pl.ds(which * WIDTH, WIDTH), :])
            if joined and which:
                target[...] += part
            else:
                target[...] = part

        def write_input(c, grad, target=target):
            if decoder:
                target[:, lanes(c)] += grad
            else:
                target[:, lanes(c)] = grad + r.grad_resid[:, lanes(c)]

        norm_back(
            lambda c, which=which: r.sides[which, :, lanes(c)],
            normed_of,
            gain_input,
            stat,
            octets,
            tables,
            write_input,
            sums_input,
        )
    if joined:
        r.grad_joined[...] = r.total[...].astype(BF16)


def shape(dims, kind):
    return jax.ShapeDtypeStruct(dims, kind)


IN_VMEM = pl.BlockSpec(memory_space=pltpu.VMEM)
IN_HBM = pl.BlockSpec(memory_space=pl.ANY)
IN_SMEM = pl.BlockSpec(memory_space=pltpu.SMEM)


class Refs:
    def __init__(self, refs, targets):
        self.__dict__.update(refs)
        self._targets, self._leaving = targets, []

    def leave(self, source, target, sem):
        self._leaving.append(pltpu.make_async_copy(source, target, sem))
        self._leaving[-1].start()

    def flush(self, *names):
        for name in names:
            if name in self._targets:
                self.leave(getattr(self, name), *self._targets.pop(name))

    def finish(self):
        self.flush(*list(self._targets))
        for copy in self._leaving:
            copy.wait()


def call(body, name, operands, outputs, scratch, weights=None, order=(), active=None, far=(), flops=0, always=False, light=False):
    sources, plan = weights if weights is not None else ([], {})
    scratch = dict(scratch)
    if order:
        scratch["fetched"] = pltpu.SemaphoreType.DMA((sum(len(plan[part]) for part in order),))
    ins = [key for key in operands if key not in far and not key.startswith(BEFORE)]
    outs = [key for key in outputs if key not in far]
    for key in outs:
        scratch[OUT + key] = pltpu.VMEM(outputs[key].shape, outputs[key].dtype)
    scratch[OUT_SEMS] = pltpu.SemaphoreType.DMA((max(len(outs), 1),))
    names = [*operands, *(SOURCE + str(index) for index in range(len(sources)))]
    names += ([ACTIVE] if active is not None else []) + [*outputs, *scratch]
    moved = sum(int(np.prod(v.shape)) * v.dtype.itemsize for v in (*operands.values(), *outputs.values()))

    def kernel(*refs):
        refs = dict(zip(names, refs))

        def run():
            targets = {}
            for index, key in enumerate(outs):
                targets[key] = (refs[key], refs[OUT_SEMS].at[index])
                refs[key] = refs[OUT + key]
            r = Refs(refs, targets)
            if order:
                r.weights = Weights([getattr(r, SOURCE + str(index)) for index in range(len(sources))], plan, r.fetched)
                for part in order:
                    r.weights.fetch(part, held_at(r, part))
            if SUMS in outputs:
                r.sums[...] = jnp.zeros(r.sums.shape, F32)
            body(r)
            r.finish()

        if active is None or always:
            run()
        else:
            pl.when(refs[ACTIVE][0] == 1)(run)

    keys = list(operands)
    results = pl.pallas_call(
        kernel,
        out_shape=list(outputs.values()),
        in_specs=[IN_VMEM if key in ins else IN_HBM for key in keys] + [IN_HBM] * len(sources) + ([IN_SMEM] if active is not None else []),
        out_specs=[IN_HBM] * len(outputs),
        scratch_shapes=list(scratch.values()),
        input_output_aliases={
            index: list(outputs).index(key[len(BEFORE) :])
            for index, key in enumerate(keys)
            if key.startswith(BEFORE)
        },
        compiler_params=pltpu.CompilerParams(vmem_limit_bytes=VMEM_LIMIT),
        cost_estimate=pl.CostEstimate(
            flops=flops // 4 if light else flops, bytes_accessed=moved // 4 if light else moved, transcendentals=0
        ),
        name=name,
    )(*operands.values(), *sources, *([active] if active is not None else []))
    return dict(zip(outputs, results))


def field(rows, kind=BF16, width=WIDTH):
    return shape((rows, width), kind)


def planes_scratch(sides, rows):
    return pltpu.VMEM((3 * sides, rows + 2 * rows // SIDE, WIDTH), BF16)


def run_forward(decoder, shared, hidden, skipped, weights_for, modulation, common, before, active):
    rows = hidden.shape[0]
    octets = rows // SIDE
    inputs = {HIDDEN: hidden, **({SKIPPED: skipped} if decoder else {}), **common}
    inputs.update(before)
    stat = shape((2, octets, WIDTH), F32)
    first_out = {
        CONV_ONE: field(rows, F32),
        STAT_C: stat,
        FIELDS: field(WIDTH + (2 * GROUPS if shared else WIDTH), width=rows),
        COLUMNS_W: field(WIDTH, width=rows),
        STAT_H: stat,
        **({STAT_S: stat} if decoder else {}),
    }
    first_scratch = {
        "turned": pltpu.VMEM(first_out[FIELDS].shape, BF16),
        "turned_w": pltpu.VMEM((WIDTH, rows), BF16),
        "fields_sems": pltpu.SemaphoreType.DMA((2,)),
        PLANES: planes_scratch(1 + decoder, rows),
        **held_scratch(decoder, (CONV_IN,)),
    }
    second_names = (CONV_OUT, *((SKIP,) if decoder else ()), *SMALL)
    second_out = {
        RESULT: field(rows),
        RESIDUAL: field(rows, F32),
        STAT_R: stat,
        ATTEND: field(rows),
        PROJECT: field(rows, width=3 * WIDTH),
        MIXED: field(rows),
    }
    second_scratch = {
        "grid": pltpu.VMEM((SIDE, octets // 8, 8, WIDTH), F32),
        PLANES: planes_scratch(1, rows),
        **held_scratch(decoder, second_names),
    }
    first_flops = 2 * rows * (1 + decoder) * TAPS * WIDTH * WIDTH
    second_flops = 2 * rows * (TAPS + 6) * WIDTH * WIDTH

    def first_body(r):
        conv_in_forward(r, decoder, shared, octets)

    def second_body(r):
        block_forward(r, decoder, octets)

    def both(r):
        first_body(r)
        second_body(r)

    if not decoder:
        names = (CONV_IN, *second_names)
        return call(
            both,
            "encoder_forward",
            {**inputs, MODULATION: modulation},
            {**first_out, **second_out},
            {**second_scratch, **first_scratch, MIDDLE: pltpu.VMEM((rows, WIDTH), BF16)},
            weights_for(decoder, *names),
            names,
            active,
            (FIELDS, COLUMNS_W),
            first_flops + second_flops,
        )
    first = call(
        first_body,
        "conv_in_forward",
        {**inputs, MODULATION: modulation},
        {**first_out, MIDDLE: field(rows)},
        first_scratch,
        weights_for(decoder, CONV_IN),
        (CONV_IN,),
        active,
        (FIELDS, COLUMNS_W),
        first_flops,
    )
    second = call(
        second_body,
        "block_forward",
        {HIDDEN: hidden, SKIPPED: skipped, MIDDLE: first[MIDDLE], **common},
        second_out,
        second_scratch,
        weights_for(decoder, *second_names),
        second_names,
        active,
        (),
        second_flops,
    )
    return {**first, **second}


def run_backward(decoder, joined, shards, with_skip, part, entry, weights_for, modulation, common, before, active):
    rows = entry[HIDDEN].shape[0]
    octets = rows // SIDE
    first, second = part in (0, None), part in (1, None)
    inputs, names = {}, ()
    if first:
        names += (OUT_NAME, *SMALL[:3], CONV_OUT)
        used = [GRAD_OUT, PROJECT, RESIDUAL, STAT_R, ATTEND, MIXED, CONV_ONE, STAT_C]
        inputs.update({name: entry[name] for name in used}, modulation=modulation, **before)
    if second:
        names += (CONV_IN, *((SKIP,) if decoder else ()))
    if second or with_skip:
        inputs[HIDDEN] = entry[HIDDEN]
        if decoder or with_skip:
            inputs[SKIPPED] = entry[SKIPPED]
    if second:
        inputs[STAT_H] = entry[STAT_H]
        if decoder:
            inputs[STAT_S] = entry[STAT_S]
    between = {GRAD_RESID: field(rows, F32), GRAD_RESID_B: field(rows), "grad_conv_b": field(rows)}
    outputs = {SUMS: field(16, F32)}
    scratch = {PLANES: planes_scratch(1, rows), **held_scratch(decoder, names)}
    if first:
        outputs[PRODUCTS] = field(WIDTH, width=(6 if with_skip else 4) * WIDTH)
        outputs[PAYLOAD] = field(2 * rows + 16)
        scratch.update(
            grid=pltpu.VMEM((SIDE, octets // 8, 8, 3 * WIDTH), F32),
            grad_project=pltpu.VMEM((rows, 3 * WIDTH), BF16),
            built=pltpu.VMEM(outputs[PRODUCTS].shape, BF16),
            built_sems=pltpu.SemaphoreType.DMA((3,)),
            rows=pltpu.VMEM(outputs[PAYLOAD].shape, BF16),
            payload_sem=pltpu.SemaphoreType.DMA,
        )
    if part == 0:
        outputs.update(between)
    elif part == 1:
        inputs.update({name: entry[name] for name in between if decoder or name != GRAD_RESID_B})
    else:
        scratch.update({name: pltpu.VMEM(value.shape, value.dtype) for name, value in between.items()})
    scratch["sides"] = pltpu.VMEM((1 + (decoder and second), rows, WIDTH), F32)
    if second:
        if joined:
            outputs[GRAD_JOINED] = field(rows)
            scratch["total"] = pltpu.VMEM((rows, WIDTH), F32)
        else:
            outputs[GRAD_HIDDEN] = field(rows, F32)
            if decoder:
                outputs[GRAD_SKIPPED] = field(rows, F32)

    def body(r):
        r.work = r.sides.at[0]
        if first:
            attention_backward(r, decoder, octets, shards, with_skip)
            middle_backward(r, octets)
        if second:
            conv_in_backward(r, decoder, joined, octets)

    return call(
        body,
        "section_backward" if part is None else ("block_backward", "conv_in_backward")[part],
        {**inputs, **common},
        outputs,
        scratch,
        weights_for(decoder, *names),
        names,
        active,
        (PRODUCTS, PAYLOAD),
        2 * rows * (first * (TAPS + 14) + second * (1 + decoder) * TAPS) * WIDTH * WIDTH,
    )


def tap_at(place, index, rows, channels):
    block = rows // TAPS
    per_tap = channels // block
    position = place * TAPS + index
    tap = lax.div(position, per_tap)
    start = pl.multiple_of(lax.rem(position, per_tap) * block, 16)
    return lax.div(tap, 3) - 1, lax.rem(tap, 3) - 1, start, block


def shifted_field(values, down, across, octets, also=None):
    width = values.shape[1]
    lane = lax.broadcasted_iota(jnp.int32, (1, width), 1)
    row, column = lax.div(lane, octets) + down, (lane & 7) + across
    inside = (row >= 0) & (row < SIDE) & (column >= 0) & (column < 8)
    if also is not None:
        inside = inside & also(lane)
    back = lax.rem(width - (octets * down + across), width)
    return jnp.where(inside, pltpu.roll(values, back, 1), 0.0).astype(BF16)


def columns_in_kernel(octets, shared, place, order, fields, affine, cols_in, *cols_skip):
    width = fields.shape[2]
    rows = cols_in.shape[0]
    for index in range(TAPS):
        down, across, start, block = tap_at(place[0], index, rows, 2 * WIDTH)
        side = lax.div(start, WIDTH)
        spot = pl.multiple_of(start - side * WIDTH if shared else start, 16)
        values = fields[0, pl.ds(spot, block), :].astype(F32)
        values = values * affine[pl.ds(start, block), 0:1] + affine[pl.ds(start, block), 1:2]
        values = values * sigmoid(values)
        kept = lax.mul(side, 1 - place[1]) * width
        cols_in[pl.ds(index * block, block), :] = shifted_field(
            values, down, across, octets, lambda lane: lane >= kept
        )
    if shared:
        rows = cols_skip[0].shape[0]
        start = pl.multiple_of(lax.rem(place[0] * rows, WIDTH), 16)
        channel = lax.broadcasted_iota(jnp.int32, (rows, GROUPS), 0) + start
        group = lax.broadcasted_iota(jnp.int32, (rows, GROUPS), 1) * PER_GROUP
        member = jnp.where((channel >= group) & (channel < group + PER_GROUP), 1.0, 0.0).astype(BF16)
        mean = dot(member, fields[0, pl.ds(WIDTH, GROUPS), :])
        deviation = dot(member, fields[0, pl.ds(WIDTH + GROUPS, GROUPS), :])
        values = fields[0, pl.ds(start, rows), :].astype(F32) * deviation + mean
        lane = lax.broadcasted_iota(jnp.int32, (1, width), 1)
        cols_skip[0][...] = jnp.where(lane < place[1] * width, values, 0.0).astype(BF16)


def tap_slices_plain(fields, rows, channels, place, octets):
    pieces, _, width = fields.shape
    spots = place * rows + jnp.arange(rows)
    taps = spots // channels
    values = jnp.take(fields, spots % channels, axis=1)
    lane = jnp.arange(width)
    total = jnp.zeros_like(values)
    for tap in range(TAPS):
        down, across = tap // 3 - 1, tap % 3 - 1
        row, column = lane // octets + down, lane % 8 + across
        inside = (row >= 0) & (row < SIDE) & (column >= 0) & (column < 8)
        moved = jnp.roll(values, -(octets * down + across), axis=2)
        total = jnp.where((taps == tap)[None, :, None] & inside, moved, total)
    return total.transpose(1, 0, 2).reshape(rows, pieces * width)


def columns_in(fields, order, affine, rows_in, rows_skip, place, decoder, octets, shared):
    _, height, width = fields.shape
    pieces = order.shape[0]
    if not shared and rows_in % (TAPS * 16):
        fields = jnp.take(fields, order, axis=0)
        sides = fields.astype(F32) * affine[:, :1] + affine[:, 1:]
        keep = (jnp.arange(2 * WIDTH)[:, None] < WIDTH) | decoder
        sides = jnp.where(keep, jax.nn.silu(sides), 0.0).astype(BF16)
        return [tap_slices_plain(sides, rows_in, 2 * WIDTH, place, octets)]
    heights = (rows_in, rows_skip) if shared else (rows_in,)
    return pl.pallas_call(
        partial(columns_in_kernel, octets, shared),
        grid_spec=pltpu.PrefetchScalarGridSpec(
            num_scalar_prefetch=2,
            grid=(pieces,),
            in_specs=[
                pl.BlockSpec((1, height, width), lambda piece, place, order: (order[piece], 0, 0)),
                pl.BlockSpec((2 * WIDTH, 2), lambda piece, place, order: (0, 0)),
            ],
            out_specs=[pl.BlockSpec((rows, width), lambda piece, place, order: (0, piece)) for rows in heights],
        ),
        out_shape=[shape((rows, pieces * width), BF16) for rows in heights],
        compiler_params=pltpu.CompilerParams(vmem_limit_bytes=VMEM_LIMIT),
        cost_estimate=pl.CostEstimate(
            flops=0, bytes_accessed=pieces * height * width, transcendentals=0
        ),
        name="columns_in",
    )(jnp.stack([place, decoder.astype(jnp.int32)]).astype(jnp.int32), order, fields, affine)


def columns_out(blocks, rows, place, octets):
    fields = [
        (number, first) for number, block in enumerate(blocks) for first in range(0, block.shape[0], WIDTH)
    ]
    if rows % (TAPS * 16):
        taken = jnp.stack([blocks[number][first : first + WIDTH] for number, first in fields])
        return tap_slices_plain(taken, rows, WIDTH, place, octets)
    width = blocks[0].shape[1]

    def body(r):
        for index in range(TAPS):
            down, across, start, block = tap_at(r.active[0], index, rows, WIDTH)
            for column, (number, first) in enumerate(fields):
                values = getattr(r, BLOCK + str(number))[pl.ds(start + first, block), :].astype(F32)
                r.cols[pl.ds(index * block, block), pl.ds(column * width, width)] = shifted_field(
                    values, down, across, octets
                )

    operands = {BLOCK + str(number): block for number, block in enumerate(blocks)}
    return call(
        body,
        "columns_out",
        operands,
        {COLS_NAME: field(rows, width=len(fields) * width)},
        {},
        active=place.reshape(1).astype(jnp.int32),
        always=True,
        light=True,
    )[COLS_NAME]


def grad_step(cols, blocks, totals):
    sides = len(cols[0])
    count = len(blocks) // len(cols)
    depth = cols[0][0].shape[1] // count

    def body(r):
        for side, part in enumerate(cols[0]):
            target = getattr(r, TOTAL + str(side))
            rows = part.shape[0]
            tile = rows // 3 if rows % 48 == 0 and rows > 128 else rows
            for start in range(0, rows, tile):
                total = getattr(r, PRIOR + str(side))[pl.ds(start, tile), :] if totals else None
                for number in range(len(blocks)):
                    factor = getattr(r, COLS + str(number // count * sides + side))
                    product = dot(
                        factor[pl.ds(start, tile), pl.ds(number % count * depth, depth)],
                        getattr(r, BLOCK + str(number))[pl.ds(depth if side == 1 else 0, depth), :],
                    )
                    total = product if total is None else total + product
                target[pl.ds(start, tile), :] = total
            r.flush(TOTAL + str(side))

    every = [part for step in cols for part in step]
    operands = {COLS + str(index): part for index, part in enumerate(every)}
    operands.update({BLOCK + str(number): block for number, block in enumerate(blocks)})
    if totals:
        operands.update({PRIOR + str(side): total for side, total in enumerate(totals)})
    outputs = {TOTAL + str(side): field(part.shape[0], F32) for side, part in enumerate(cols[0])}
    flops = 2 * sum(part.shape[0] * part.shape[1] for part in every) * WIDTH
    return list(call(body, "grad_step", operands, outputs, {}, flops=flops, light=True).values())


def last_rows(blocks, first):
    def body(r):
        copies = [
            pltpu.make_async_copy(
                getattr(r, BLOCK + str(index)).at[pl.ds(first, r.taken.shape[1])], r.landed.at[index], r.sems.at[index]
            )
            for index in range(len(blocks))
        ]
        for copy in copies:
            copy.start()
        for copy in copies:
            copy.wait()
        r.taken[...] = r.landed[...]

    operands = {BLOCK + str(index): block for index, block in enumerate(blocks)}
    taken = shape((len(blocks), blocks[0].shape[0] - first, blocks[0].shape[1]), blocks[0].dtype)
    scratch = {"sems": pltpu.SemaphoreType.DMA((len(blocks),)), "landed": pltpu.VMEM(taken.shape, taken.dtype)}
    return call(body, "last_rows", operands, {TAKEN: taken}, scratch, far=operands)[TAKEN]


class Doubling:
    def __init__(self, value, axis):
        self.axis, self.value, self.distance = axis, value[None], 1

    def step(self):
        count, index = lax.axis_size(self.axis), lax.axis_index(self.axis)
        if self.distance < count:
            pairs = [(i, i ^ self.distance) for i in range(count)]
            other = lax.ppermute(self.value, self.axis, pairs)
            self.value = jnp.where(
                (index // self.distance) % 2 == 0,
                jnp.concatenate([self.value, other], axis=0),
                jnp.concatenate([other, self.value], axis=0),
            )
            self.distance *= 2

    def finish(self):
        while self.distance < lax.axis_size(self.axis):
            self.step()
        return self.value


class Ring:
    def __init__(self, value, axis):
        self.axis = axis
        self.count = lax.axis_size(axis)
        self.stride = self.count // 4
        self.values, self.rows, self.steps = [value], [], []

    def send(self, value, target):
        return lax.ppermute(value, self.axis, [(i, target(i)) for i in range(self.count)])

    def around(self, value, steps=1):
        return self.send(value, lambda i: (i + steps * self.stride) % self.count)

    def besides(self, value):
        row, stride = [value], self.stride
        for _ in range(stride // 2 - 1):
            row.append(self.send(row[-1], lambda i: i // stride * stride + (i + 2) % stride))
        return row

    def with_core(self, row):
        return row + [self.send(part, lambda i: i ^ 1) for part in row]

    def turn(self):
        self.values.append(self.around(self.values[-1]))

    def spread(self):
        self.rows.append(self.besides(self.values[len(self.rows)]))

    def spread_last(self):
        stride, half = self.stride, self.values[3].shape[0] // 32 * 16
        row = [self.values[3]]
        for index in range(1, stride // 2):
            beside = self.send(row[-1][:half], lambda i: i // stride * stride + (i + 2) % stride)
            turned = self.around(self.rows[2][index][half:])
            row.append(jnp.concatenate([beside, turned], axis=0))
        self.rows.append(row)

    def share(self, step):
        self.steps.append(self.with_core(self.rows[step]))


def ring_order(axis, step):
    index, stride = lax.axis_index(axis), lax.axis_size(axis) // 4
    quarter = (index // stride + 4 - step) % 4 * stride
    sources = []
    for core in range(2):
        for beside in range(stride // 2):
            sources.append(quarter + (index % stride + stride - 2 * beside) % stride // 2 * 2 + (index + core) % 2)
    return jnp.stack(sources).astype(jnp.int32)


def together(*values):
    return lax.optimization_barrier(values)


def moved(value, source, target):
    return lax.ppermute(value, SECTION, [(source, target)])


def to_rows(value):
    micro, images, pixels, channels = value.shape
    count = micro * images
    return (
        value.reshape(count, pixels // 8, 8, channels).transpose(1, 0, 2, 3).reshape(-1, channels)
    )


def from_rows(value, images):
    count = MICRO * images
    channels = value.shape[-1]
    grid_rows = value.shape[0] // (8 * count)
    planes = value.reshape(grid_rows, count, 8, channels).transpose(1, 0, 2, 3)
    return planes.reshape(MICRO, images, grid_rows * 8, channels)


def noise_columns(pair_ids, columns):
    fraction = pair_ids.astype(F32) / (LEVELS - 1)
    top_root = SIGMA_HIGH ** (1.0 / 7.0)
    bottom_root = SIGMA_LOW ** (1.0 / 7.0)
    sigmas = (top_root + fraction * (bottom_root - top_root)) ** 7
    log_scale = 250.0 * jnp.log(sigmas)
    quarter = EMBED // 4
    kind = columns // quarter
    frequency = jnp.exp(-math.log(10000.0) * (columns % quarter).astype(F32) / quarter)
    angles = jnp.where(kind < 2, log_scale[:, :1], log_scale[:, 1:]) * frequency
    return jnp.where(kind % 2 == 0, jnp.cos(angles), jnp.sin(angles))


def block_homes(shards, rows_in):
    block = rows_in // TAPS
    per_tap = 2 * WIDTH // block
    mine = [[i for i in range(TAPS) if (TAPS * d + i) % per_tap < per_tap // 2] for d in range(shards)]
    slots = max(-(-(len(mine[d]) + len(mine[d ^ 1])) // 2) for d in range(shards))
    sent = [mine[d][slots:] for d in range(shards)]
    most = max(1, max(len(part) for part in sent))
    offers, names = [], []
    for d in range(shards):
        kept = mine[d][:slots]
        offer = kept + [TAPS + i for i in range(len(sent[d ^ 1]))]
        names.append([TAPS * d + i for i in kept] + [TAPS * (d ^ 1) + i for i in sent[d ^ 1]])
        offers.append(offer + [0] * (slots - len(offer)))
    sends = [part + [0] * (most - len(part)) for part in sent]
    return np.array(sends, np.int32), np.array(offers, np.int32), names, slots


def spans(name_rows, cuts):
    found, start = {}, 0
    for name, count in name_rows:
        found[name], first, base = [], 0, 0
        for array, height in enumerate(cuts):
            low, high = max(start, base), min(start + count, base + height)
            if low < high:
                found[name].append((array, low - base, low - start, high - low))
            base += height
        start += count
    return found


def section_weights(conv_in, conv_out, skip_proj, qkv_proj, out_proj, is_decoder):
    shards, me = lax.axis_size(DP), lax.axis_index(DP)
    qkv_parts = [qkv_proj[:, part * WIDTH : (part + 1) * WIDTH] for part in range(3)]
    small = dict(zip(SMALL, (*qkv_parts, out_proj)))
    shares = {CONV_IN: conv_in, CONV_OUT: conv_out, **small, SKIP: skip_proj}
    heights = [(name, part.shape[0]) for name, part in shares.items()]
    if any(height % 16 for _, height in heights) or conv_in.shape[0] % (TAPS * 16):
        whole = {name: lax.all_gather(part, DP, axis=0, tiled=True)[None] for name, part in shares.items()}
        sources = list(whole.values())
        plan = {name: [(index, 0, 0, 0, part.shape[1])] for index, (name, part) in enumerate(whole.items())}
        encoder_plan = dict(plan)
        encoder_plan[CONV_IN] = [(0, 0, tap * 2 * WIDTH, tap * WIDTH, WIDTH) for tap in range(TAPS)]
        return sources, encoder_plan, plan
    sends, offers, names, slots = block_homes(shards, conv_in.shape[0])
    blocks = conv_in.reshape(TAPS, -1, WIDTH)
    block = blocks.shape[1]
    other = lax.ppermute(
        jnp.take(blocks, jnp.asarray(sends)[me], axis=0), DP, [(i, i ^ 1) for i in range(shards)]
    )
    chosen = jnp.take(jnp.concatenate([blocks, other], axis=0), jnp.asarray(offers)[me], axis=0)
    encoder_parts = [chosen.reshape(slots * block, WIDTH), conv_out, *small.values()]
    encoder_rows = sum(part.shape[0] for part in encoder_parts)
    first_rows = max(encoder_rows, sum(height for name, height in heights if name not in (OUT_NAME, SKIP)))
    everything = jnp.concatenate(list(shares.values()), axis=0)
    encoder_parts.append(jnp.zeros((first_rows - encoder_rows, WIDTH), BF16))
    first = lax.all_gather(
        jnp.where(is_decoder, everything[:first_rows], jnp.concatenate(encoder_parts, axis=0)), DP, axis=0
    )
    second = lax.all_gather(everything[first_rows:], DP, axis=0)

    def plan_of(found):
        return {
            name: [
                (array, piece, row, piece * height + start, count)
                for piece in range(shards)
                for array, row, start, count in found[name]
            ]
            for name, height in heights
            if name in found
        }

    decoder_plan = plan_of(spans(heights, (first_rows, everything.shape[0] - first_rows)))
    encoder_plan = plan_of(
        spans([("blocks", slots * block)] + [item for item in heights if item[0] in (CONV_OUT, *SMALL)], (encoder_rows,))
    )
    per_tap = 2 * WIDTH // block
    encoder_plan[CONV_IN] = sorted(
        (
            (0, piece, slot * block, name // per_tap * WIDTH + name % per_tap * block, block)
            for piece in range(shards)
            for slot, name in enumerate(names[piece])
        ),
        key=lambda entry: entry[3],
    )
    return [first, second], encoder_plan, decoder_plan


def on_device(
    level_input,
    cotangent,
    class_table,
    conv_in,
    conv_out,
    embed_proj,
    skip_proj,
    qkv_proj,
    out_proj,
    gains,
    biases,
    noise_pairs,
    classes,
):
    sections = lax.axis_size(SECTION)
    section_id = lax.axis_index(SECTION)
    shards = lax.axis_size(DP)
    shard_id = lax.axis_index(DP)
    images = level_input.shape[1]
    count = MICRO * images
    octets = 8 * count
    rows = SIDE * octets

    is_decoder = section_id >= sections // 2
    skip_by_columns = sections == 2
    sources, encoder_plan, decoder_plan = section_weights(
        conv_in[0], conv_out[0], skip_proj[0], qkv_proj[0], out_proj[0], is_decoder
    )

    gain_share, bias_share = gains.shape[1], biases.shape[1]
    small = jnp.concatenate(
        [
            gains[0].astype(F32),
            biases[0].astype(F32),
            noise_pairs.reshape(-1).astype(F32),
            classes.reshape(-1).astype(F32),
        ]
    )
    spare = -small.shape[0] % LANE
    every = Doubling(jnp.pad(small, (0, spare))[None], DP).finish()[:, 0]
    cut = gain_share + bias_share
    params = jnp.concatenate(
        [every[:, :gain_share].reshape(4, WIDTH), every[:, gain_share:cut].reshape(12, WIDTH)],
        axis=0,
    )
    all_images = shards * count
    pair_ids = every[:, cut : cut + 2 * count].reshape(all_images, 2)
    class_ids = every[:, cut + 2 * count : cut + 3 * count].reshape(all_images).astype(jnp.int32)

    slice_width = class_table.shape[1]
    columns = shard_id * slice_width + jnp.arange(slice_width)[None, :]
    onehot = (class_ids[:, None] == jnp.arange(CLASSES)[None, :]).astype(BF16)
    pre = noise_columns(pair_ids, columns) + dot(onehot, class_table)
    embed_b = jax.nn.silu(pre).astype(BF16)
    shares = dot(embed_b, embed_proj[0]).astype(BF16).reshape(shards, count, 2 * WIDTH)
    modulation = lax.all_to_all(shares, DP, 0, 0).astype(F32).sum(axis=0)
    modulation = modulation + params[BIAS + 3 : BIAS + 5].reshape(1, 2 * WIDTH)
    modulation = jnp.repeat(modulation, 8, axis=0)

    level_own, top_own = to_rows(level_input), to_rows(cotangent)
    level_rows = jnp.concatenate(
        [level_own] + [moved(level_own, source, 0) for source in range(1, sections)], axis=0
    )
    top_rows = jnp.concatenate(
        [moved(top_own, source, sections - 1) for source in range(sections - 1)] + [top_own], axis=0
    )

    orders = [ring_order(DP, step) for step in range(4)]
    order = jnp.concatenate(orders)

    def in_order(values):
        return jnp.take(values.reshape(shards, count, -1), order, axis=0).reshape(all_images, -1)

    common = {
        "params": params,
        "group_of": jnp.asarray(GROUP_OF, BF16),
        "group_of_t": jnp.asarray(GROUP_OF.T, BF16),
    }
    level_rows, top_rows, modulation, embed_late, pre_late, onehot_late = together(
        level_rows, top_rows, modulation, in_order(embed_b), in_order(pre), in_order(onehot)
    )

    def weights_for(decoder, *names):
        plan = decoder_plan if decoder else encoder_plan
        used = sorted({entry[0] for name in names for entry in plan[name]})
        return [sources[index] for index in used], {
            name: [(used.index(entry[0]), *entry[1:]) for entry in plan[name]] for name in names
        }

    kept = []
    skips = {}
    hidden = level_rows
    result = None
    before = {}
    for tick in range(sections):
        decoder = tick >= sections // 2
        mirror = sections - 1 - tick
        active = (section_id == tick).astype(jnp.int32).reshape(1)
        skipped = skips[tick] if decoder else hidden
        outs = run_forward(
            decoder, sections == 2, hidden, skipped, weights_for, modulation, common, before, active
        )
        before = {"before_fields": outs[FIELDS], "before_columns_w": outs[COLUMNS_W]}
        result = outs[RESULT]
        entry = {HIDDEN: hidden, SKIPPED: skipped, STAT_S: outs[STAT_H], **outs}
        for name in (FIELDS, COLUMNS_W, RESULT, MIDDLE):
            entry.pop(name, None)
        if sections > 2 and kept:
            entry = {name: jnp.where(section_id == tick, value, kept[-1][name]) for name, value in entry.items()}
            kept = [entry] * (tick + 1)
        else:
            kept.append(entry)
        if tick < sections - 1:
            hidden = moved(result, tick, tick + 1)
            if not decoder:
                skips[mirror] = hidden if mirror == tick + 1 else moved(result, tick, mirror)

    def own(values):
        if sections > 2 and values[0] is values[-1]:
            return values[0]
        chosen = values[0]
        for tick in range(1, sections):
            chosen = jnp.where(section_id == tick, values[tick], chosen)
        return chosen

    fields = lax.all_gather(outs[FIELDS], DP, axis=0)
    circle = Ring(outs[COLUMNS_W], DP)
    turned = {0: outs[COLUMNS_W]}
    w_rows, w_steps = {}, {}

    def beside(stage, *values):
        if stage == 0:
            turned.update({step % 4: circle.around(turned[0], step) for step in (1, -1)})
            w_rows[0] = circle.besides(turned[0])
        if stage == 1:
            turned[2] = circle.around(turned[1])
            w_rows.update({step: circle.besides(turned[step]) for step in (1, 3)})
        if stage == 2:
            w_rows[2] = circle.besides(turned[2])
        for step in ((), (0,), (1, 3), (2,))[stage]:
            other = circle.send(jnp.concatenate(w_rows[step], axis=0), lambda i: i ^ 1)
            w_steps[step] = [*w_rows[step], other]
        state, *values = together((turned, w_rows, w_steps), *values)
        for old, new in zip((turned, w_rows, w_steps), state):
            old.update(new)
        return values

    def to_owners(value, source):
        share = rows // sections
        pieces = [value[index * share : (index + 1) * share] for index in range(sections)]
        total = jnp.where(section_id == source, pieces[source], jnp.zeros_like(pieces[source]))
        for target in range(sections):
            if target != source:
                total = total + moved(pieces[target].astype(BF16), source, target).astype(value.dtype)
        return from_rows(total, images)


    sums_of = [None] * sections
    skip_grads = {}
    grad_out = top_rows
    before = {}
    for tick in reversed(range(sections)):
        decoder = tick >= sections // 2
        mirror = sections - 1 - tick
        entry = kept[tick]
        if not decoder and tick in skip_grads:
            grad_out = grad_out.astype(F32) + skip_grads[tick].astype(F32)
        joined = decoder and mirror == tick - 1
        active = (section_id == tick).astype(jnp.int32).reshape(1)

        def backward(part, entry, decoder=decoder, joined=joined, active=active):
            return run_backward(
                decoder, joined, shards, not skip_by_columns, part, entry, weights_for, modulation, common, before, active
            )

        outs = backward(0 if tick == 0 else None, {**entry, GRAD_OUT: grad_out})
        if tick == sections - 1:
            level_output = to_owners(result, sections - 1)
            outs, level_output = beside(0, outs, level_output)
        if tick == 0:
            (outs,) = beside(1, outs)
        before = {"before_products": outs[PRODUCTS], "before_payload": outs[PAYLOAD]}
        sums_of[tick] = outs[SUMS]
        if joined:
            grad_out = moved(outs[GRAD_JOINED], tick, mirror)
        elif tick:
            if decoder:
                skip_grads[mirror] = moved(outs[GRAD_SKIPPED].astype(BF16), tick, mirror)
            grad_out = moved(outs[GRAD_HIDDEN].astype(BF16), tick, tick - 1)
    products, payload = outs[PRODUCTS], outs[PAYLOAD]

    affine = jnp.stack([params[GAIN : GAIN + 2].reshape(-1), params[BIAS : BIAS + 2].reshape(-1)], axis=1)

    def cols_in_of(step):
        return columns_in(
            fields,
            orders[step],
            affine,
            conv_in.shape[1],
            skip_proj.shape[1],
            shard_id,
            is_decoder,
            octets,
            sections == 2,
        )

    def with_out(step, others):
        return [columns_out(w_steps[step], conv_out.shape[1], shard_id, octets), *others]

    ring = Ring(payload, DP)
    cols = []

    small_grads = lax.psum_scatter(products, DP, scatter_dimension=0, tiled=True)
    ring.turn()
    ring.spread()
    last = backward(1, {**entry, **outs})
    cols.append(cols_in_of(0))
    ring.values, ring.rows, fields, cols, sums_of[0], input_rows = beside(
        2, ring.values, ring.rows, fields, cols, sums_of[0] + last[SUMS], last[GRAD_HIDDEN]
    )
    sums = own(sums_of)
    shares = jnp.concatenate([sums[:4].reshape(shards, gain_share), sums[4:].reshape(shards, bias_share)], axis=1)
    summed = lax.all_to_all(shares, DP, 0, 0, tiled=True).sum(axis=0)
    ring.turn()
    ring.spread()
    ring.share(0)
    cols = [with_out(0, cols[0]), with_out(1, cols_in_of(1))]
    ring.values, ring.rows, ring.steps, cols, fields, input_rows, summed = beside(
        3, ring.values, ring.rows, ring.steps, cols, fields, input_rows, summed
    )
    ring.turn()
    ring.spread()
    ring.share(1)
    cols += [with_out(step, cols_in_of(step)) for step in (2, 3)]
    ring.values, ring.rows, ring.steps, cols, input_rows, small_grads = together(
        ring.values, ring.rows, ring.steps, cols, input_rows, small_grads
    )
    ring.spread_last()
    ring.share(2)
    input_grad = to_owners(input_rows, 0)
    totals = grad_step(cols[:2], ring.steps[0] + ring.steps[1], None)
    small_grads = small_grads.astype(F32)
    qkv_grad = small_grads[:, : 3 * WIDTH]
    out_grad = small_grads[:, 3 * WIDTH : 4 * WIDTH]
    ring.rows, ring.steps, cols, totals, input_grad, qkv_grad, out_grad = together(
        ring.rows, ring.steps, cols, totals, input_grad, qkv_grad, out_grad
    )
    ring.share(3)
    totals = grad_step(cols[2:], ring.steps[2] + ring.steps[3], totals)
    conv_out_grad, conv_in_grad = totals[:2]
    gains_grad, biases_grad = summed[:gain_share], summed[gain_share:]

    mods = last_rows([block for step in ring.steps for block in step], 2 * rows)
    mods = jnp.concatenate(
        [mods[:, start : start + count].reshape(all_images, WIDTH) for start in (0, count)], axis=1
    )
    embed_grad = dot_tn(embed_late, mods)
    grad_embed = dot_nt(mods, embed_proj[0])
    if sections == 2:
        grad_embed = grad_embed + lax.ppermute(grad_embed, SECTION, [(0, 1), (1, 0)])
    else:
        grad_embed = lax.psum(grad_embed, SECTION)
    grad_pre = jax.vjp(jax.nn.silu, pre_late)[1](grad_embed)[0]
    table_grad = lax.dot_general(
        onehot_late.astype(F32),
        grad_pre,
        (((0,), (0,)), ((), ())),
        precision=lax.Precision.HIGHEST,
        preferred_element_type=F32,
    )

    if skip_by_columns:
        skip_grad = totals[2]
    else:
        skip_grad = jnp.concatenate(
            [small_grads[:, 4 * WIDTH : 5 * WIDTH], small_grads[:, 5 * WIDTH :]], axis=0
        )
    return (
        level_output,
        input_grad,
        table_grad,
        conv_in_grad[None],
        conv_out_grad[None],
        embed_grad[None],
        skip_grad[None],
        qkv_grad[None],
        out_grad[None],
        gains_grad[None],
        biases_grad[None],
    )


def solution(mesh):
    placed = (
        P(None, DP, SECTION, None),
        P(None, DP, SECTION, None),
        P(None, DP),
        P(SECTION, DP, None),
        P(SECTION, DP, None),
        P(SECTION, DP, None),
        P(SECTION, DP, None),
        P(SECTION, DP, None),
        P(SECTION, DP, None),
        P(SECTION, DP),
        P(SECTION, DP),
        P(None, DP, None),
        P(None, DP),
    )
    return jax.shard_map(
        on_device,
        mesh=mesh,
        in_specs=placed,
        out_specs=(
            P(None, DP, SECTION, None),
            P(None, DP, SECTION, None),
            P(None, DP),
            P(SECTION, DP, None),
            P(SECTION, DP, None),
            P(SECTION, DP, None),
            P(SECTION, DP, None),
            P(SECTION, DP, None),
            P(SECTION, DP, None),
            P(SECTION, DP),
            P(SECTION, DP),
        ),
        check_vma=False,
    )
```

time: 714 us -> 501 us (0.70)
  waiting for transfers between devices: 450 us -> 237 us
  matrix products: 23.6 us -> 2.47 us
  local copies, waits for them, and re-layouts: 16.8 us -> 34.5 us
  starting transfers between devices: 36.2 us -> 47 us
  other arithmetic: 17.5 us -> 25.2 us
    all_gather x5 -> x3, waiting for transfers between devices: 361 us -> 159 us  [the longest x1 138 us: section_weights(): lax.all_gather(jnp.where(is_decoder, everything[:first_rows], jnp.concate...]
    reduce_scatter x1, waiting for transfers between devices: 24 us -> 5.1 us  [on_device(): lax.psum_scatter(products, DP, scatter_dimension=0, tiled=True)]
    dot_general x4 -> x2, matrix products: 19 us -> 0.5 us  [dot(): return jnp.dot(left, right, preferred_element_type=F32)]
    all_to_all x1 -> x2, waiting for transfers between devices: 8.81 us -> 16.5 us  [the longest x1 9.41 us: on_device(): modulation = lax.all_to_all(shares, DP, 0, 0).astype(F32).sum(axis=0)]
    select_n x5 -> x1, other arithmetic: 7.54 us -> 0.01 us  [own(): chosen = jnp.where(section_id == tick, values[tick], chosen)]
    ppermute x18 -> x39, starting transfers between devices: 29.4 us -> 35 us  [the longest x27 16.6 us: send(): lax.ppermute(value, self.axis, [(i, target(i)) for i in range(self.count)])]
    pallas_call x9 -> x17, Pallas kernels: 136 us -> 134 us  [the longest x13 105 us: call(): pl.pallas_call(kernel, out_shape=list(outputs.values()), in_specs=[IN_VME...]
    ppermute x18 -> x39, waiting for transfers between devices: 55.2 us -> 56.7 us  [the longest x6 44.6 us: moved(): return lax.ppermute(value, SECTION, [(source, target)])]
  transfers between devices with their start and end apart: 25 -> 45, of which waited for: 20 -> 13; matrix products, arithmetic and copies ran while one was open for 5% -> 8% of each run, Pallas kernels for 5% -> 27%
where the time goes in v2:
time: 501 us; the launch traced here: 496 us
  waiting for transfers between devices  237 us (47%)
  Pallas kernels  134 us (27%)
  starting transfers between devices  47 us (9%)
  local copies, waits for them, and re-layouts  34.5 us (7%)
  other arithmetic  25.2 us (5%)
  between operations  15.1 us (3%)
    all_gather x1, waiting for transfers between devices, section_weights(): lax.all_gather(jnp.where(is_decoder, everything[:first_rows], jnp.concate...  138 us
    pallas_call x13, Pallas kernels, call(): pl.pallas_call(kernel, out_shape=list(outputs.values()), in_specs=[IN_VME...  105 us
    ppermute x6, waiting for transfers between devices, moved(): return lax.ppermute(value, SECTION, [(source, target)])  44.6 us
    pallas_call x4, Pallas kernels, columns_in(): pl.pallas_call(partial(columns_in_kernel, octets, shared), grid_spec=pltp...  29.6 us
    all_gather x1, waiting for transfers between devices, section_weights(): second = lax.all_gather(everything[first_rows:], DP, axis=0)  20.9 us
    ppermute x27, starting transfers between devices, send(): lax.ppermute(value, self.axis, [(i, target(i)) for i in range(self.count)])  16.6 us
    ppermute x6, starting transfers between devices, moved(): return lax.ppermute(value, SECTION, [(source, target)])  11.9 us
  transfers between devices with their start and end apart: 45, of which 13 were waited for; matrix products, arithmetic and copies ran while one was open for 8% of the time, Pallas kernels for 27%

profile of v2, /device:TPU:0, one launch (start us, length us, event | category | flops | bytes accessed | tf_op | source)
XLA Modules:
  0.0 496.0 jit_solution(8122814340129229611)
XLA Ops:
  8.8 1.9 gather_fusion.3
  13.0 1.1 constant_dynamic-update-slice_fusion.1
  14.2 1.4 pad_maximum_fusion
  15.5 2.2 gather_fusion.4
  18.0 1.2 constant_dynamic-update-slice_fusion.3
  19.3 1.6 broadcast_select_fusion
  22.1 4.7 collective-permute-start.1
  26.9 1.3 collective-permute-start
  29.4 1.6 collective-permute-start.3
  31.0 2.1 collective-permute-done.3
  33.1 1.6 collective-permute-start.4
  34.8 2.4 collective-permute-done.4
  37.2 2.7 collective-permute-start.5
  39.9 2.7 collective-permute-done.5
  46.8 6.2 %all-to-all-start = ((bf16[16,4,1536]{2,1,0:T(4,128)(2,1)}), bf16[16,4,1536]{2,1,0:T(4,128)(2,1)S(1)}, u32[]{:S(2)}, u32[]{:S(2)}) async-start(bf16[16,4,1536]{2,1,0:T(4,128)(2,1)} %reshape.1406), calls=%async_computation | async-start | bytes 393216 | tf_op jit(solution)/shard_map/all_to_all | solution.py:1315
  56.2 9.4 %all-to-all-done = bf16[16,4,1536]{2,1,0:T(4,128)(2,1)S(1)} async-done(((bf16[16,4,1536]{2,1,0:T(4,128)(2,1)}), bf16[16,4,1536]{2,1,0:T(4,128)(2,1)S(1)}, u32[]{:S(2)}, u32[]{:S(2)}) %all-to-all-start) | async-done | bytes 196640 | tf_op jit(solution)/shard_map/all_to_all | solution.py:1315
  66.4 138.1 %all-gather.6.cloned.1.call-done.refs_5_.refs_8_.refs_6_.refs_16_.refs_14_.refs_7_ = bf16[16,1440,768]{2,1,0:T(8,128)(2,1)} async-done(((bf16[1,1440,768]{2,1,0:T(8,128)(2,1)}), bf16[16,1440,768]{2,1,0:T(8,128)(2,1)}) %all-gather.6.cloned.1.call-update) | async-done | bytes 35389456 | tf_op jit(solution)/shard_map/all_gather | solution.py:1227
  204.4 22.0 %encoder_forward.1 = (f32[256,768]{1,0:T(8,128)}, f32[2,32,768]{2,1,0:T(8,128)}, bf16[832,256]{1,0:T(8,128)(2,1)}, bf16[768,256]{1,0:T(8,128)(2,1)}, f32[2,32,76...) custom-call(bf16[256,768]{1,0:T(8,128)(2,1)} %pad_maximum_fusion.6.r, ...), custom_call_target="tpu_custom_call" | custom-call | flops 7247757312 | bytes 6373376 | tf_op jit(solution)/shard_map/encoder_forward/pallas_call | solution.py:698
  226.4 1.3 collective-permute-start.7
  227.7 9.3 %collective-permute-done.7.refs_0_.refs_1_.refs_9_.refs_10_ = bf16[256,768]{1,0:T(8,128)(2,1)S(1)} collective-permute-done((bf16[256,768]{1,0:T(8,128)(2,1)}, bf16[256,768]{1,0:T(8,128)(2,1)S(1)}, u32[]{:S(2)}, u32[]{:S(2)}) %collective-permute-start.7) | collective-permute-done | bytes 393248 | tf_op jit(solution)/shard_map/ppermute | solution.py:1140
  237.8 1.7 conv_in_forward.1
  239.6 1.2 collective-permute-start.10
  240.8 2.8 collective-permute-start.8
  243.7 1.0 collective-permute-start.9
  244.7 20.9 %all-gather.8.cloned.1.call-done = bf16[2304,768]{1,0:T(8,128)(2,1)} async-done(((bf16[144,768]{1,0:T(8,128)(2,1)}), bf16[2304,768]{1,0:T(8,128)(2,1)}) %all-gather.8.cloned.1.call-update) | async-done | bytes 3538960 | tf_op jit(solution)/shard_map/all_gather | solution.py:1230
  265.6 2.7 block_forward.1
  269.2 1.3 collective-permute-start.11
  270.5 14.3 %section_backward.1 = (f32[16,768]{1,0:T(8,128)}, bf16[768,3072]{1,0:T(8,128)(2,1)}, bf16[528,768]{1,0:T(8,128)(2,1)}, bf16[256,768]{1,0:T(8,128)(2,1)}) custom-call(bf16[256,768]{1,0:T(8,128)(2,1)} %pad_maximum_fusion.7.refs_0_, bf16[256,2304]{1,0:T(8,128)(2,1)} %get-tuple-element.188.refs_1_, f32[256,768]{1,0:T(8,128)} %get-tuple-element.189.refs_2_, ...), custom_call_target="tpu_custom_call" | custom-call | flops 12381585408 | bytes 12115968 | tf_op jit(solution)/shard_map/section_backward/pallas_call | solution.py:698
  285.6 1.3 collective-permute-start.16
  288.2 1.5 collective-permute-start.14
  289.7 35.2 %collective-permute-done.16.refs_0_ = bf16[256,768]{1,0:T(8,128)(2,1)S(1)} collective-permute-done((bf16[256,768]{1,0:T(8,128)(2,1)}, bf16[256,768]{1,0:T(8,128)(2,1)S(1)}, u32[]{:S(2)}, u32[]{:S(2)}) %collective-permute-start.16) | collective-permute-done | bytes 393248 | tf_op jit(solution)/shard_map/ppermute | solution.py:1140
  325.6 17.7 %block_backward.1 = (f32[16,768]{1,0:T(8,128)}, bf16[768,3072]{1,0:T(8,128)(2,1)}, bf16[528,768]{1,0:T(8,128)(2,1)}, f32[256,768]{1,0:T(8,128)}, bf16[256,768]{1,0:T(8,128)(2,1)}, /*index=5*/bf16[256,768]{1,0:T(8,128)(2,1)}) custom-call(bf16[256,768]{1,0:T(8,128)(2,1)} %copy-done.24, ...), custom_call_target="tpu_custom_call", output_to_operand_aliasing={{1}: (9, {}), {2}: (10, {})} | custom-call | flops 6945767424 | bytes 17645568 | tf_op jit(solution)/shard_map/block_backward/pallas_call | solution.py:698
  344.3 1.1 copy-done.2
  345.5 1.1 collective-permute-start.20
  347.4 1.9 pad_maximum_fusion.4
  349.4 2.1 pad_maximum_fusion.3
  354.6 1.1 collective-permute-start.17
  356.4 1.2 copy.72.affine
  357.6 10.8 %conv_in_backward.1 = (f32[16,768]{1,0:T(8,128)}, f32[256,768]{1,0:T(8,128)}) custom-call(bf16[256,768]{1,0:T(8,128)(2,1)} %pad_maximum_fusion.6.refs_0_, f32[2,32,768]{2,1,0:T(8,128)} %get-tuple-element.235.refs_1_, f32[256,768]{1,0:T(8,128)} %get-tuple-element.236.refs_2_, bf16[256,768]{1,0:T(8,128)(2,1)} %get-tuple-element.237.refs_3_, ...), custom_call_target="tpu_custom_call" | custom-call | flops 2717908992 | bytes 3047424 | tf_op jit(solution)/shard_map/conv_in_backward/pallas_call | solution.py:698
  368.5 1.4 add.417
  369.9 7.6 %columns_in.4 = (bf16[864,1024]{1,0:T(8,128)(2,1)}, bf16[96,1024]{1,0:T(8,128)(2,1)}) custom-call(s32[2]{0:T(128)} %pad_add_fusion.place, s32[4]{0:T(128)} %pad_add_fusion.1.order, bf16[16,832,256]{2,1,0:T(8,128)(2,1)} %bitcast.144, f32[1536,2]{1,0:T(8,128)} %copy.72.affine), custom_call_target="tpu_custom_call" | custom-call | bytes 851968 | tf_op jit(solution)/shard_map/columns_in/pallas_call | solution.py:959
  380.3 1.9 pad_maximum_fusion.5
  383.5 1.5 reshape.1419
  385.0 1.4 reshape.1418
  387.9 5.6 %all-to-all-start.1 = ((f32[16,1,768]{2,1,0:T(1,128)}), f32[16,1,768]{2,1,0:T(1,128)}, u32[]{:S(2)}, u32[]{:S(2)}) async-start(f32[16,1,768]{2,1,0:T(1,128)} %all_to_all.10), calls=%async_computation.1 | async-start | bytes 98304 | tf_op jit(solution)/shard_map/all_to_all | solution.py:1482
  394.1 7.3 %columns_in.5 = (bf16[864,1024]{1,0:T(8,128)(2,1)}, bf16[96,1024]{1,0:T(8,128)(2,1)}) custom-call(s32[2]{0:T(128)} %pad_add_fusion.place, s32[4]{0:T(128)} %pad_add_fusion.2.order, bf16[16,832,256]{2,1,0:T(8,128)(2,1)} %bitcast.145, f32[1536,2]{1,0:T(8,128)} %copy.72.affine), custom_call_target="tpu_custom_call" | custom-call | bytes 851968 | tf_op jit(solution)/shard_map/columns_in/pallas_call | solution.py:959
  401.4 2.7 columns_out.5.refs_3_
  404.1 2.7 columns_out.4.refs_0_
  406.8 7.1 %all-to-all-done.1 = f32[16,1,768]{2,1,0:T(1,128)} async-done(((f32[16,1,768]{2,1,0:T(1,128)}), f32[16,1,768]{2,1,0:T(1,128)}, u32[]{:S(2)}, u32[]{:S(2)}) %all-to-all-start.1) | async-done | bytes 49184 | tf_op jit(solution)/shard_map/all_to_all | solution.py:1482
  417.3 7.4 %columns_in.7 = (bf16[864,1024]{1,0:T(8,128)(2,1)}, bf16[96,1024]{1,0:T(8,128)(2,1)}) custom-call(s32[2]{0:T(128)} %pad_add_fusion.place, s32[4]{0:T(128)} %pad_add_fusion.4.order, bf16[16,832,256]{2,1,0:T(8,128)(2,1)} %bitcast.146, f32[1536,2]{1,0:T(8,128)} %copy.72.affine), custom_call_target="tpu_custom_call" | custom-call | bytes 851968 | tf_op jit(solution)/shard_map/columns_in/pallas_call | solution.py:959
  424.8 7.3 %columns_in.6 = (bf16[864,1024]{1,0:T(8,128)(2,1)}, bf16[96,1024]{1,0:T(8,128)(2,1)}) custom-call(s32[2]{0:T(128)} %pad_add_fusion.place, s32[4]{0:T(128)} %pad_add_fusion.3.order, bf16[16,832,256]{2,1,0:T(8,128)(2,1)} %bitcast.147, f32[1536,2]{1,0:T(8,128)} %copy.72.affine), custom_call_target="tpu_custom_call" | custom-call | bytes 851968 | tf_op jit(solution)/shard_map/columns_in/pallas_call | solution.py:959
  432.1 2.7 columns_out.7.refs_3_
  434.8 2.8 columns_out.6.refs_0_
  437.6 5.1 %reduce-scatter.2.cloned.1.call-done = bf16[48,3072]{1,0:T(8,128)(2,1)} async-done(((bf16[768,3072]{1,0:T(8,128)(2,1)}), bf16[48,3072]{1,0:T(8,128)(2,1)}) %reduce-scatter.2.cloned.1.call-update) | async-done | bytes 294928 | tf_op jit(solution)/shard_map/reduce_scatter | solution.py:1472
  442.7 3.1 collective-permute-done.27.refs_12_.refs_10_
  446.4 1.7 slice.163
  448.1 2.0 collective-permute-start.35
  454.0 10.9 %grad_step.2 = (f32[432,768]{1,0:T(8,128)}, f32[864,768]{1,0:T(8,128)}, f32[96,768]{1,0:T(8,128)}) custom-call(bf16[432,1024]{1,0:T(8,128)(2,1)} %columns_out.4.refs_0_, bf16[864,1024]{1,0:T(8,128)(2,1)} %get-tuple-element.300.refs_1_, bf16[96,1024]{1,0:T(8,128)(2,1)} %get-tuple-element.301.refs_2_, bf16[432,1024]{1,0:T(8,128)(2,1)} %columns_out.5.refs_3_, ...), custom_call_target="tpu_custom_call" | custom-call | flops 1094713344 | bytes 4116480 | tf_op jit(solution)/shard_map/grad_step/pallas_call | solution.py:698
  464.9 1.0 convert_add_fusion
  466.6 1.1 pad_maximum_fusion.1.refs_13_.refs_11_
  470.1 1.2 collective-permute-done.37.refs_15_.refs_13_
  472.2 1.9 last_rows.1
  474.1 1.1 fusion.37
  476.3 12.0 %grad_step.3 = (f32[432,768]{1,0:T(8,128)}, f32[864,768]{1,0:T(8,128)}, f32[96,768]{1,0:T(8,128)}) custom-call(bf16[432,1024]{1,0:T(8,128)(2,1)} %columns_out.6.refs_0_, bf16[864,1024]{1,0:T(8,128)(2,1)} %get-tuple-element.334.refs_1_, bf16[96,1024]{1,0:T(8,128)(2,1)} %get-tuple-element.335.refs_2_, bf16[432,1024]{1,0:T(8,128)(2,1)} %columns_out.7.refs_3_, ...), custom_call_target="tpu_custom_call" | custom-call | flops 1094713344 | bytes 5185536 | tf_op jit(solution)/shard_map/grad_step/pallas_call | solution.py:698
  (257 shorter events, 44.8 us)
Async XLA Ops:
  7.2 38.7 %copy-start = (bf16[1,48,1536]{2,1,0:T(8,128)(2,1)S(1)}, bf16[1,48,1536]{2,1,0:T(8,128)(2,1)}, u32[]{:S(2)}) copy-start(bf16[1,48,1536]{2,1,0:T(8,128)(2,1)} %param.22) | copy-start | bytes 442372
  7.2 197.2 %all-gather.6.cloned.1.call-start = ((), (), s32[]{:S(2)}) async-start(), calls=%async_computation.3 | async-start | bytes 37601280 | tf_op jit(solution)/shard_map/all_gather | solution.py:1227
  10.8 3.4 collective-permute-start.6
  20.9 23.1 %copy-start.39 = (bf16[1000,48]{0,1:T(8,128)(2,1)S(1)}, bf16[1000,48]{0,1:T(8,128)(2,1)}, u32[]{:S(2)}) copy-start(bf16[1000,48]{0,1:T(8,128)(2,1)} %param.19) | copy-start | bytes 288004
  21.0 244.6 %all-gather.8.cloned.1.call-start = ((), (), s32[]{:S(2)}) async-start(), calls=%async_computation.5 | async-start | bytes 3760128 | tf_op jit(solution)/shard_map/all_gather | solution.py:1230
  21.9 7.5 %collective-permute-start.2 = (f32[1,1,896]{2,0,1:T(1,128)S(1)}, f32[1,1,896]{2,0,1:T(1,128)S(1)}, u32[]{:S(2)}, u32[]{:S(2)}) collective-permute-start(f32[1,1,896]{2,0,1:T(1,128)S(1)} %broadcast_in_dim_broadcast_in_dim.3), channel_id=1, source_target_pairs={{0,1},{1,0},{2,3},{3,2},{4,5},{5,4},{6,7},{7,6},{8,9},{9,8},{10,11... | collective-permute-start | bytes 10760 | tf_op jit(solution)/shard_map/ppermute | solution.py:1070
  22.1 32.4 %collective-permute-start.1 = (bf16[128,768]{1,0:T(8,128)(2,1)S(1)}, bf16[128,768]{1,0:T(8,128)(2,1)S(1)}, u32[]{:S(2)}, u32[]{:S(2)}) collective-permute-start(bf16[128,768]{1,0:T(8,128)(2,1)S(1)} %bitcast.155), channel_id=1, source_target_pairs={{0,16},{1,17},{2,18},{3,19},{4,20},{5,21},{6,22},{7,23},{8,24},{9,... | collective-permute-start | bytes 589832 | tf_op jit(solution)/shard_map/ppermute | solution.py:1140
  26.9 28.5 %collective-permute-start = (bf16[128,768]{1,0:T(8,128)(2,1)S(1)}, bf16[128,768]{1,0:T(8,128)(2,1)S(1)}, u32[]{:S(2)}, u32[]{:S(2)}) collective-permute-start(bf16[128,768]{1,0:T(8,128)(2,1)S(1)} %bitcast.153), channel_id=1, source_target_pairs={{16,0},{17,1},{18,2},{19,3},{20,4},{21,5},{22,6},{23,7},{24,8},{25... | collective-permute-start | bytes 589832 | tf_op jit(solution)/shard_map/ppermute | solution.py:1140
  29.4 3.7 collective-permute-start.3
  33.1 4.1 collective-permute-start.4
  37.2 5.4 %collective-permute-start.5 = (f32[8,1,896]{2,0,1:T(8,128)S(1)}, f32[8,1,896]{2,0,1:T(8,128)S(1)}, u32[]{:S(2)}, u32[]{:S(2)}) collective-permute-start(f32[8,1,896]{2,0,1:T(8,128)S(1)} %maximum_select_fusion.2), channel_id=1, source_target_pairs={{0,8},{1,9},{2,10},{3,11},{4,12},{5,13},{6,14},{7,15},{8,0},{9,1},... | collective-permute-start | bytes 86024 | tf_op jit(solution)/shard_map/ppermute | solution.py:1070
  42.7 13.5 %copy-start.26 = (f32[16,896]{1,0:T(8,128)}, f32[16,896]{1,0:T(8,128)S(1)}, u32[]{:S(2)}) copy-start(f32[16,896]{1,0:T(8,128)S(1)} %maximum_select_fusion) | copy-start | bytes 172036
  46.8 18.7 %all-to-all-start = ((bf16[16,4,1536]{2,1,0:T(4,128)(2,1)}), bf16[16,4,1536]{2,1,0:T(4,128)(2,1)S(1)}, u32[]{:S(2)}, u32[]{:S(2)}) async-start(bf16[16,4,1536]{2,1,0:T(4,128)(2,1)} %reshape.1406), calls=%async_computation | async-start | bytes 393216 | tf_op jit(solution)/shard_map/all_to_all | solution.py:1315
  53.1 316.8 %all-gather.10.cloned.1.call-start = ((), (), s32[]{:S(2)}) async-start(), calls=%async_computation.6 | async-start | bytes 7241728 | tf_op jit(solution)/shard_map/all_gather | solution.py:1385
  226.4 10.7 %collective-permute-start.7 = (bf16[256,768]{1,0:T(8,128)(2,1)}, bf16[256,768]{1,0:T(8,128)(2,1)S(1)}, u32[]{:S(2)}, u32[]{:S(2)}) collective-permute-start(bf16[256,768]{1,0:T(8,128)(2,1)} %get-tuple-element.182), channel_id=1, source_target_pairs={{0,16},{1,17},{2,18},{3,19},{4,20},{5,21},{6,22},{7,23},{8,24},{9,... | collective-permute-start | bytes 1179656 | tf_op jit(solution)/shard_map/ppermute | solution.py:1140
  239.6 203.1 %reduce-scatter.2.cloned.1.call-start = ((), (), s32[]{:S(2)}) async-start(), calls=%async_computation.4 | async-start | bytes 5013504 | tf_op jit(solution)/shard_map/reduce_scatter | solution.py:1472
  239.6 46.0 %collective-permute-start.10 = (bf16[768,256]{1,0:T(8,128)(2,1)}, bf16[768,256]{1,0:T(8,128)(2,1)S(1)}, u32[]{:S(2)}, u32[]{:S(2)}) collective-permute-start(bf16[768,256]{1,0:T(8,128)(2,1)} %get-tuple-element.242.refs_0_), channel_id=1, source_target_pairs={{0,2},{1,3},{2,0},{3,1},{4,6},{5,7},{6,4},{7,5},{8,10},{9,11},{10,... | collective-permute-start | bytes 1179656 | tf_op jit(solution)/shard_map/ppermute | solution.py:1092
  240.8 44.7 %collective-permute-start.8 = (bf16[768,256]{1,0:T(8,128)(2,1)}, bf16[768,256]{1,0:T(8,128)(2,1)S(1)}, u32[]{:S(2)}, u32[]{:S(2)}) collective-permute-start(bf16[768,256]{1,0:T(8,128)(2,1)} %get-tuple-element.242.refs_0_), channel_id=1, source_target_pairs={{0,4},{1,5},{2,6},{3,7},{4,8},{5,9},{6,10},{7,11},{8,12},{9,13},{1... | collective-permute-start | bytes 1179656 | tf_op jit(solution)/shard_map/ppermute | solution.py:1092
  243.7 42.0 %collective-permute-start.9 = (bf16[768,256]{1,0:T(8,128)(2,1)}, bf16[768,256]{1,0:T(8,128)(2,1)S(1)}, u32[]{:S(2)}, u32[]{:S(2)}) collective-permute-start(bf16[768,256]{1,0:T(8,128)(2,1)} %get-tuple-element.242.refs_0_), channel_id=1, source_target_pairs={{0,12},{1,13},{2,14},{3,15},{4,0},{5,1},{6,2},{7,3},{8,4},{9,5},{1... | collective-permute-start | bytes 1179656 | tf_op jit(solution)/shard_map/ppermute | solution.py:1092
  269.2 15.7 %collective-permute-start.11 = (bf16[128,768]{1,0:T(8,128)(2,1)S(1)}, bf16[128,768]{1,0:T(8,128)(2,1)S(1)}, u32[]{:S(2)}, u32[]{:S(2)}) collective-permute-start(bf16[128,768]{1,0:T(8,128)(2,1)S(1)} %slice.96), channel_id=1, source_target_pairs={{16,0},{17,1},{18,2},{19,3},{20,4},{21,5},{22,6},{23,7},{24,8},{25... | collective-permute-start | bytes 589832 | tf_op jit(solution)/shard_map/ppermute | solution.py:1140
  270.5 14.4 %copy-start.25 = (bf16[256,768]{1,0:T(8,128)(2,1)S(1)}, bf16[256,768]{1,0:T(8,128)(2,1)}, u32[]{:S(2)}) copy-start(bf16[256,768]{1,0:T(8,128)(2,1)} %get-tuple-element.201) | copy-start | bytes 1179652
  270.5 16.4 %copy-start.8 = (bf16[768,256]{1,0:T(8,128)(2,1)S(1)}, bf16[768,256]{1,0:T(8,128)(2,1)}, u32[]{:S(2)}) copy-start(bf16[768,256]{1,0:T(8,128)(2,1)} %get-tuple-element.242.refs_0_) | copy-start | bytes 1179652
  285.6 57.8 %copy-start.15 = (bf16[768,256]{1,0:T(8,128)(2,1)}, bf16[768,256]{1,0:T(8,128)(2,1)S(1)}, u32[]{:S(2)}) copy-start(bf16[768,256]{1,0:T(8,128)(2,1)S(1)} %collective-permute-done.10.refs_1_) | copy-start | bytes 1179652
  285.6 57.8 %copy-start.18 = (bf16[768,256]{1,0:T(8,128)(2,1)}, bf16[768,256]{1,0:T(8,128)(2,1)S(1)}, u32[]{:S(2)}) copy-start(bf16[768,256]{1,0:T(8,128)(2,1)S(1)} %collective-permute-done.8.refs_0_) | copy-start | bytes 1179652
  285.6 61.8 %copy-start.14 = (bf16[768,256]{1,0:T(8,128)(2,1)}, bf16[768,256]{1,0:T(8,128)(2,1)S(1)}, u32[]{:S(2)}) copy-start(bf16[768,256]{1,0:T(8,128)(2,1)S(1)} %collective-permute-done.9.refs_0_) | copy-start | bytes 1179652
  285.6 39.3 %collective-permute-start.16 = (bf16[256,768]{1,0:T(8,128)(2,1)}, bf16[256,768]{1,0:T(8,128)(2,1)S(1)}, u32[]{:S(2)}, u32[]{:S(2)}) collective-permute-start(bf16[256,768]{1,0:T(8,128)(2,1)} %get-tuple-element.207), channel_id=1, source_target_pairs={{16,0},{17,1},{18,2},{19,3},{20,4},{21,5},{22,6},{23,7},{24,8},{25... | collective-permute-start | bytes 1179656 | tf_op jit(solution)/shard_map/ppermute | solution.py:1140
  287.0 57.2 %collective-permute-start.15 = (bf16[1536,256]{1,0:T(8,128)(2,1)S(1)}, bf16[1536,256]{1,0:T(8,128)(2,1)}, u32[]{:S(2)}, u32[]{:S(2)}) collective-permute-start(bf16[1536,256]{1,0:T(8,128)(2,1)S(1)} %pad_maximum_fusion.2), channel_id=1, source_target_pairs={{0,1},{1,0},{2,3},{3,2},{4,5},{5,4},{6,7},{7,6},{8,9},{9,8},{10,11... | collective-permute-start | bytes 2359304 | tf_op jit(solution)/shard_map/ppermute | solution.py:1092
  287.3 56.1 %collective-permute-start.12 = (bf16[768,256]{1,0:T(8,128)(2,1)S(1)}, bf16[768,256]{1,0:T(8,128)(2,1)S(1)}, u32[]{:S(2)}, u32[]{:S(2)}) collective-permute-start(bf16[768,256]{1,0:T(8,128)(2,1)S(1)} %collective-permute-done.8.refs_0_), channel_id=1, source_target_pairs={{0,4},{1,5},{2,6},{3,7},{4,8},{5,9},{6,10},{7,11},{8,12},{9,13},{1... | collective-permute-start | bytes 1179656 | tf_op jit(solution)/shard_map/ppermute | solution.py:1092
  287.6 55.7 %collective-permute-start.13 = (bf16[768,256]{1,0:T(8,128)(2,1)S(1)}, bf16[768,256]{1,0:T(8,128)(2,1)S(1)}, u32[]{:S(2)}, u32[]{:S(2)}) collective-permute-start(bf16[768,256]{1,0:T(8,128)(2,1)S(1)} %collective-permute-done.8.refs_0_), channel_id=1, source_target_pairs={{0,2},{1,3},{2,0},{3,1},{4,6},{5,7},{6,4},{7,5},{8,10},{9,11},{10,... | collective-permute-start | bytes 1179656 | tf_op jit(solution)/shard_map/ppermute | solution.py:1092
  288.2 55.2 %collective-permute-start.14 = (bf16[768,256]{1,0:T(8,128)(2,1)S(1)}, bf16[768,256]{1,0:T(8,128)(2,1)S(1)}, u32[]{:S(2)}, u32[]{:S(2)}) collective-permute-start(bf16[768,256]{1,0:T(8,128)(2,1)S(1)} %collective-permute-done.9.refs_0_), channel_id=1, source_target_pairs={{0,2},{1,3},{2,0},{3,1},{4,6},{5,7},{6,4},{7,5},{8,10},{9,11},{10,... | collective-permute-start | bytes 1179656 | tf_op jit(solution)/shard_map/ppermute | solution.py:1092
  343.4 11.2 %copy-start.16 = (bf16[768,256]{1,0:T(8,128)(2,1)}, bf16[768,256]{1,0:T(8,128)(2,1)S(1)}, u32[]{:S(2)}) copy-start(bf16[768,256]{1,0:T(8,128)(2,1)S(1)} %collective-permute-done.12.refs_0_) | copy-start | bytes 1179652
  345.5 32.1 %collective-permute-start.20 = (bf16[528,768]{1,0:T(8,128)(2,1)S(1)}, bf16[528,768]{1,0:T(8,128)(2,1)S(1)}, u32[]{:S(2)}, u32[]{:S(2)}) collective-permute-start(bf16[528,768]{1,0:T(8,128)(2,1)S(1)} %copy-done.2), channel_id=1, source_target_pairs={{0,4},{1,5},{2,6},{3,7},{4,8},{5,9},{6,10},{7,11},{8,12},{9,13},{1... | collective-permute-start | bytes 2433032 | tf_op jit(solution)/shard_map/ppermute | solution.py:1092
  346.5 31.0 %collective-permute-start.21 = (bf16[528,768]{1,0:T(8,128)(2,1)S(1)}, bf16[528,768]{1,0:T(8,128)(2,1)S(1)}, u32[]{:S(2)}, u32[]{:S(2)}) collective-permute-start(bf16[528,768]{1,0:T(8,128)(2,1)S(1)} %copy-done.2), channel_id=1, source_target_pairs={{0,2},{1,3},{2,0},{3,1},{4,6},{5,7},{6,4},{7,5},{8,10},{9,11},{10,... | collective-permute-start | bytes 2433032 | tf_op jit(solution)/shard_map/ppermute | solution.py:1092
  349.4 28.1 %collective-permute-start.19 = (bf16[1536,256]{1,0:T(8,128)(2,1)}, bf16[1536,256]{1,0:T(8,128)(2,1)}, u32[]{:S(2)}, u32[]{:S(2)}) collective-permute-start(bf16[1536,256]{1,0:T(8,128)(2,1)} %pad_maximum_fusion.4), channel_id=1, source_target_pairs={{0,1},{1,0},{2,3},{3,2},{4,5},{5,4},{6,7},{7,6},{8,9},{9,8},{10,11... | collective-permute-start | bytes 2359304 | tf_op jit(solution)/shard_map/ppermute | solution.py:1092
  351.5 26.0 %collective-permute-start.18 = (bf16[1536,256]{1,0:T(8,128)(2,1)}, bf16[1536,256]{1,0:T(8,128)(2,1)}, u32[]{:S(2)}, u32[]{:S(2)}) collective-permute-start(bf16[1536,256]{1,0:T(8,128)(2,1)} %pad_maximum_fusion.3), channel_id=1, source_target_pairs={{0,1},{1,0},{2,3},{3,2},{4,5},{5,4},{6,7},{7,6},{8,9},{9,8},{10,11... | collective-permute-start | bytes 2359304 | tf_op jit(solution)/shard_map/ppermute | solution.py:1092
  354.6 22.9 %collective-permute-start.17 = (bf16[768,256]{1,0:T(8,128)(2,1)S(1)}, bf16[768,256]{1,0:T(8,128)(2,1)S(1)}, u32[]{:S(2)}, u32[]{:S(2)}) collective-permute-start(bf16[768,256]{1,0:T(8,128)(2,1)S(1)} %collective-permute-done.12.refs_0_), channel_id=1, source_target_pairs={{0,2},{1,3},{2,0},{3,1},{4,6},{5,7},{6,4},{7,5},{8,10},{9,11},{10,... | collective-permute-start | bytes 1179656 | tf_op jit(solution)/shard_map/ppermute | solution.py:1092
  357.6 10.8 %copy-start.34 = (f32[16,768]{1,0:T(8,128)S(1)}, f32[16,768]{1,0:T(8,128)}, u32[]{:S(2)}) copy-start(f32[16,768]{1,0:T(8,128)} %get-tuple-element.234) | copy-start | bytes 147460
  369.9 10.4 %copy-start.17 = (bf16[768,256]{1,0:T(8,128)(2,1)S(1)}, bf16[768,256]{1,0:T(8,128)(2,1)}, u32[]{:S(2)}) copy-start(bf16[768,256]{1,0:T(8,128)(2,1)} %copy-done.16) | copy-start | bytes 1179652
  369.9 12.3 %copy-start.31 = (f32[16,768]{1,0:T(8,128)S(1)}, f32[16,768]{1,0:T(8,128)}, u32[]{:S(2)}) copy-start(f32[16,768]{1,0:T(8,128)} %add.417) | copy-start | bytes 147460
  369.9 12.3 %copy-start.33 = (f32[16,768]{1,0:T(8,128)S(1)}, f32[16,768]{1,0:T(8,128)}, u32[]{:S(2)}) copy-start(f32[16,768]{1,0:T(8,128)} %get-tuple-element.260) | copy-start | bytes 147460
  377.5 38.1 %copy-start.12 = (bf16[528,768]{1,0:T(8,128)(2,1)}, bf16[528,768]{1,0:T(8,128)(2,1)S(1)}, u32[]{:S(2)}) copy-start(bf16[528,768]{1,0:T(8,128)(2,1)S(1)} %collective-permute-done.20.refs_10_.refs_4_) | copy-start | bytes 2433028
  377.6 23.8 %copy-start.13 = (bf16[528,768]{1,0:T(8,128)(2,1)}, bf16[528,768]{1,0:T(8,128)(2,1)S(1)}, u32[]{:S(2)}) copy-start(bf16[528,768]{1,0:T(8,128)(2,1)S(1)} %collective-permute-done.21.refs_7_.refs_1_) | copy-start | bytes 2433028
  378.5 36.2 %collective-permute-start.23 = (bf16[528,768]{1,0:T(8,128)(2,1)S(1)}, bf16[528,768]{1,0:T(8,128)(2,1)S(1)}, u32[]{:S(2)}, u32[]{:S(2)}) collective-permute-start(bf16[528,768]{1,0:T(8,128)(2,1)S(1)} %collective-permute-done.20.refs_10_.refs_4_), channel_id=1, source_target_pairs={{0,4},{1,5},{2,6},{3,7},{4,8},{5,9},{6,10},{7,11},{8,12},{9,13},{1... | collective-permute-start | bytes 2433032 | tf_op jit(solution)/shard_map/ppermute | solution.py:1092
  379.2 35.5 %collective-permute-start.24 = (bf16[528,768]{1,0:T(8,128)(2,1)S(1)}, bf16[528,768]{1,0:T(8,128)(2,1)}, u32[]{:S(2)}, u32[]{:S(2)}) collective-permute-start(bf16[528,768]{1,0:T(8,128)(2,1)S(1)} %collective-permute-done.20.refs_10_.refs_4_), channel_id=1, source_target_pairs={{0,2},{1,3},{2,0},{3,1},{4,6},{5,7},{6,4},{7,5},{8,10},{9,11},{10,... | collective-permute-start | bytes 2433032 | tf_op jit(solution)/shard_map/ppermute | solution.py:1092
  379.8 35.0 %collective-permute-start.25 = (bf16[528,768]{1,0:T(8,128)(2,1)S(1)}, bf16[528,768]{1,0:T(8,128)(2,1)}, u32[]{:S(2)}, u32[]{:S(2)}) collective-permute-start(bf16[528,768]{1,0:T(8,128)(2,1)S(1)} %copy-done.2), channel_id=1, source_target_pairs={{0,1},{1,0},{2,3},{3,2},{4,5},{5,4},{6,7},{7,6},{8,9},{9,8},{10,11... | collective-permute-start | bytes 2433032 | tf_op jit(solution)/shard_map/ppermute | solution.py:1092
  379.8 35.0 %collective-permute-start.26 = (bf16[528,768]{1,0:T(8,128)(2,1)S(1)}, bf16[528,768]{1,0:T(8,128)(2,1)}, u32[]{:S(2)}, u32[]{:S(2)}) collective-permute-start(bf16[528,768]{1,0:T(8,128)(2,1)S(1)} %collective-permute-done.21.refs_7_.refs_1_), channel_id=1, source_target_pairs={{0,1},{1,0},{2,3},{3,2},{4,5},{5,4},{6,7},{7,6},{8,9},{9,8},{10,11... | collective-permute-start | bytes 2433032 | tf_op jit(solution)/shard_map/ppermute | solution.py:1092
  382.2 32.4 %collective-permute-start.22 = (bf16[1536,256]{1,0:T(8,128)(2,1)}, bf16[1536,256]{1,0:T(8,128)(2,1)}, u32[]{:S(2)}, u32[]{:S(2)}) collective-permute-start(bf16[1536,256]{1,0:T(8,128)(2,1)} %pad_maximum_fusion.5), channel_id=1, source_target_pairs={{0,1},{1,0},{2,3},{3,2},{4,5},{5,4},{6,7},{7,6},{8,9},{9,8},{10,11... | collective-permute-start | bytes 2359304 | tf_op jit(solution)/shard_map/ppermute | solution.py:1092
  387.9 25.9 %all-to-all-start.1 = ((f32[16,1,768]{2,1,0:T(1,128)}), f32[16,1,768]{2,1,0:T(1,128)}, u32[]{:S(2)}, u32[]{:S(2)}) async-start(f32[16,1,768]{2,1,0:T(1,128)} %all_to_all.10), calls=%async_computation.1 | async-start | bytes 98304 | tf_op jit(solution)/shard_map/all_to_all | solution.py:1482
  414.7 31.1 %copy-start.9 = (bf16[528,768]{1,0:T(8,128)(2,1)}, bf16[528,768]{1,0:T(8,128)(2,1)S(1)}, u32[]{:S(2)}) copy-start(bf16[528,768]{1,0:T(8,128)(2,1)S(1)} %collective-permute-done.23.refs_8_.refs_6_) | copy-start | bytes 2433028
  414.7 31.0 %collective-permute-start.27 = (bf16[528,768]{1,0:T(8,128)(2,1)S(1)}, bf16[528,768]{1,0:T(8,128)(2,1)S(1)}, u32[]{:S(2)}, u32[]{:S(2)}) collective-permute-start(bf16[528,768]{1,0:T(8,128)(2,1)S(1)} %collective-permute-done.23.refs_8_.refs_6_), channel_id=1, source_target_pairs={{0,4},{1,5},{2,6},{3,7},{4,8},{5,9},{6,10},{7,11},{8,12},{9,13},{1... | collective-permute-start | bytes 2433032 | tf_op jit(solution)/shard_map/ppermute | solution.py:1092
  415.0 30.7 %collective-permute-start.28 = (bf16[528,768]{1,0:T(8,128)(2,1)S(1)}, bf16[528,768]{1,0:T(8,128)(2,1)S(1)}, u32[]{:S(2)}, u32[]{:S(2)}) collective-permute-start(bf16[528,768]{1,0:T(8,128)(2,1)S(1)} %collective-permute-done.23.refs_8_.refs_6_), channel_id=1, source_target_pairs={{0,2},{1,3},{2,0},{3,1},{4,6},{5,7},{6,4},{7,5},{8,10},{9,11},{10,... | collective-permute-start | bytes 2433032 | tf_op jit(solution)/shard_map/ppermute | solution.py:1092
  415.7 30.1 %collective-permute-start.29 = (bf16[528,768]{1,0:T(8,128)(2,1)S(1)}, bf16[528,768]{1,0:T(8,128)(2,1)}, u32[]{:S(2)}, u32[]{:S(2)}) collective-permute-start(bf16[528,768]{1,0:T(8,128)(2,1)S(1)} %collective-permute-done.20.refs_10_.refs_4_), channel_id=1, source_target_pairs={{0,1},{1,0},{2,3},{3,2},{4,5},{5,4},{6,7},{7,6},{8,9},{9,8},{10,11... | collective-permute-start | bytes 2433032 | tf_op jit(solution)/shard_map/ppermute | solution.py:1092
  415.7 30.1 %collective-permute-start.30 = (bf16[528,768]{1,0:T(8,128)(2,1)}, bf16[528,768]{1,0:T(8,128)(2,1)}, u32[]{:S(2)}, u32[]{:S(2)}) collective-permute-start(bf16[528,768]{1,0:T(8,128)(2,1)} %collective-permute-done.24.refs_11_.refs_5_), channel_id=1, source_target_pairs={{0,1},{1,0},{2,3},{3,2},{4,5},{5,4},{6,7},{7,6},{8,9},{9,8},{10,11... | collective-permute-start | bytes 2433032 | tf_op jit(solution)/shard_map/ppermute | solution.py:1092
  445.7 22.0 %copy-start.7 = (bf16[528,768]{1,0:T(8,128)(2,1)}, bf16[528,768]{1,0:T(8,128)(2,1)S(1)}, u32[]{:S(2)}) copy-start(bf16[528,768]{1,0:T(8,128)(2,1)S(1)} %collective-permute-done.27.refs_12_.refs_10_) | copy-start | bytes 2433028
  445.8 19.1 %copy-start.6 = (bf16[528,768]{1,0:T(8,128)(2,1)}, bf16[528,768]{1,0:T(8,128)(2,1)S(1)}, u32[]{:S(2)}) copy-start(bf16[528,768]{1,0:T(8,128)(2,1)S(1)} %collective-permute-done.28.refs_9_.refs_7_) | copy-start | bytes 2433028
  445.8 21.9 %collective-permute-start.33 = (bf16[528,768]{1,0:T(8,128)(2,1)S(1)}, bf16[528,768]{1,0:T(8,128)(2,1)}, u32[]{:S(2)}, u32[]{:S(2)}) collective-permute-start(bf16[528,768]{1,0:T(8,128)(2,1)S(1)} %collective-permute-done.23.refs_8_.refs_6_), channel_id=1, source_target_pairs={{0,1},{1,0},{2,3},{3,2},{4,5},{5,4},{6,7},{7,6},{8,9},{9,8},{10,11... | collective-permute-start | bytes 2433032 | tf_op jit(solution)/shard_map/ppermute | solution.py:1092
  445.9 21.8 %collective-permute-start.34 = (bf16[528,768]{1,0:T(8,128)(2,1)S(1)}, bf16[528,768]{1,0:T(8,128)(2,1)}, u32[]{:S(2)}, u32[]{:S(2)}) collective-permute-start(bf16[528,768]{1,0:T(8,128)(2,1)S(1)} %collective-permute-done.28.refs_9_.refs_7_), channel_id=1, source_target_pairs={{0,1},{1,0},{2,3},{3,2},{4,5},{5,4},{6,7},{7,6},{8,9},{9,8},{10,11... | collective-permute-start | bytes 2433032 | tf_op jit(solution)/shard_map/ppermute | solution.py:1092
  448.1 16.8 %collective-permute-start.35 = (bf16[128,768]{1,0:T(8,128)(2,1)}, bf16[128,768]{1,0:T(8,128)(2,1)}, u32[]{:S(2)}, u32[]{:S(2)}) collective-permute-start(bf16[128,768]{1,0:T(8,128)(2,1)} %slice.163), channel_id=1, source_target_pairs={{0,16},{1,17},{2,18},{3,19},{4,20},{5,21},{6,22},{7,23},{8,24},{9,... | collective-permute-start | bytes 589832 | tf_op jit(solution)/shard_map/ppermute | solution.py:1140
  450.8 15.8 %collective-permute-start.32 = (bf16[272,768]{1,0:T(8,128)(2,1)}, bf16[272,768]{1,0:T(8,128)(2,1)S(1)}, u32[]{:S(2)}, u32[]{:S(2)}) collective-permute-start(bf16[272,768]{1,0:T(8,128)(2,1)} %slice.102), channel_id=1, source_target_pairs={{0,4},{1,5},{2,6},{3,7},{4,8},{5,9},{6,10},{7,11},{8,12},{9,13},{1... | collective-permute-start | bytes 1253384 | tf_op jit(solution)/shard_map/ppermute | solution.py:1092
  451.8 14.9 %collective-permute-start.31 = (bf16[256,768]{1,0:T(8,128)(2,1)}, bf16[256,768]{1,0:T(8,128)(2,1)}, u32[]{:S(2)}, u32[]{:S(2)}) collective-permute-start(bf16[256,768]{1,0:T(8,128)(2,1)} %slice.101), channel_id=1, source_target_pairs={{0,2},{1,3},{2,0},{3,1},{4,6},{5,7},{6,4},{7,5},{8,10},{9,11},{10,... | collective-permute-start | bytes 1179656 | tf_op jit(solution)/shard_map/ppermute | solution.py:1092
  454.0 10.9 %copy-start.23 = (f32[256,768]{1,0:T(8,128)S(1)}, f32[256,768]{1,0:T(8,128)}, u32[]{:S(2)}) copy-start(f32[256,768]{1,0:T(8,128)} %get-tuple-element.314) | copy-start | bytes 2359300
  467.7 2.4 collective-permute-start.36
  467.8 3.5 collective-permute-start.37
  476.3 12.1 %collective-permute-start.38 = (f32[64,48]{0,1:T(8,128)S(1)}, f32[64,48]{0,1:T(8,128)S(1)}, u32[]{:S(2)}, u32[]{:S(2)}) collective-permute-start(f32[64,48]{0,1:T(8,128)S(1)} %fusion.1), channel_id=1, source_target_pairs={{0,16},{16,0},{1,17},{17,1},{2,18},{18,2},{3,19},{19,3},{4,20},{20... | collective-permute-start | bytes 36872 | tf_op jit(solution)/shard_map/ppermute | solution.py:1519
  (22 other events, 58.0 us)
Sparse Core Ops, SparseCore 0:
  21.1 183.2 all-gather.5
  207.3 58.2 all-gather.7
  268.4 70.4 all-gather.9
  344.5 98.1 reduce-scatter.1

commit v3 on v2

--- a/solution.py
+++ b/solution.py
@@ -241,6 +241,18 @@
     return scratch
 
 
+def tap_loop(body):
+    def one(tap, carry):
+        body(tap, lax.div(tap, 3), lax.rem(tap, 3))
+        return carry
+
+    lax.fori_loop(0, TAPS, one, 0)
+
+
+def plane_rows(planes, plane, down, octets, rows):
+    return planes[plane, pl.ds(pl.multiple_of(octets * down, 16), rows), :]
+
+
 def head_pair(values, left):
     zero = jnp.zeros_like(values)
     return jnp.concatenate([jnp.where(left, values, zero), jnp.where(left, zero, values)], axis=0)
@@ -295,7 +307,20 @@
             put_shifted(r.planes, 3 * which, value, c, octets)
             if not (shared and which):
                 r.turned[pl.ds(which * WIDTH + c * LANE, LANE), :] = normed.T.astype(BF16)
-    for tap in range(TAPS):
+    if decoder:
+        r.conv_one[...] = jnp.broadcast_to(r.params[pl.ds(BIAS + 2, 1), :], r.conv_one.shape)
+    for down in range(3 if decoder else 0):
+        r.weights.need(CONV_IN, 3 * (down + 1) * span)
+
+        def one_tap(across, carry, down=down):
+            for half in range(len(sides)):
+                first = pl.multiple_of((3 * down + across) * span + half * WIDTH, WIDTH)
+                values = r.planes[3 * half + across, pl.ds(octets * down, rows), :]
+                r.conv_one[...] += dot(values, r.held_conv_in[pl.ds(first, WIDTH), :])
+            return carry
+
+        lax.fori_loop(0, 3, one_tap, 0)
+    for tap in range(0 if decoder else TAPS):
         r.weights.need(CONV_IN, (tap + 1) * span)
         for half in range(len(sides)):
             part = dot(
@@ -333,7 +358,16 @@
     clear_edges(r.planes, octets)
     for c in range(CHUNKS):
         put_shifted(r.planes, 0, r.middle[:, lanes(c)].astype(F32), c, octets)
-    for tap in range(TAPS):
+    if not decoder:
+        r.weights.need(CONV_OUT, TAPS * WIDTH)
+        r.residual[...] = jnp.broadcast_to(r.params[pl.ds(BIAS + 6, 1), :], r.residual.shape)
+
+        def one_tap(tap, down, across):
+            weights = r.held_conv_out[pl.ds(pl.multiple_of(tap * WIDTH, WIDTH), WIDTH), :]
+            r.residual[...] += dot(plane_rows(r.planes, across, down, octets, rows), weights)
+
+        tap_loop(one_tap)
+    for tap in range(TAPS if decoder else 0):
         r.weights.need(CONV_OUT, (tap + 1) * WIDTH)
         part = dot(
             r.planes[tap % 3, pl.ds(octets * (tap // 3), rows), :], r.held_conv_out[pl.ds(tap * WIDTH, WIDTH), :]
@@ -499,16 +533,14 @@
     r.rows[pl.ds(0, rows), :] = r.grad_resid_b[...]
     for c in range(CHUNKS):
         put_shifted(r.planes, 0, r.grad_resid_b[:, lanes(c)].astype(F32), c, octets)
-    for tap in range(TAPS):
-        r.weights.need(CONV_OUT, (tap + 1) * WIDTH)
-        part = dot_nt(
-            r.planes[2 - tap % 3, pl.ds(octets * (2 - tap // 3), rows), :],
-            r.held_conv_out[pl.ds(tap * WIDTH, WIDTH), :],
-        )
-        if tap == 0:
-            r.work[...] = part
-        else:
-            r.work[...] += part
+    r.weights.need(CONV_OUT, TAPS * WIDTH)
+    r.work[...] = jnp.zeros(r.work.shape, F32)
+
+    def one_tap(tap, down, across):
+        weights = r.held_conv_out[pl.ds(pl.multiple_of(tap * WIDTH, WIDTH), WIDTH), :]
+        r.work[...] += dot_nt(plane_rows(r.planes, 2 - across, 2 - down, octets, rows), weights)
+
+    tap_loop(one_tap)
     for c in range(CHUNKS):
         normed = (
             normed_chunk(r.conv_one[:, lanes(c)], r.stat_c, c) * r.params[pl.ds(GAIN + 2, 1), lanes(c)]
@@ -561,7 +593,7 @@
     r.leave(r.rows, r.payload, r.payload_sem)
 
 
-def conv_in_backward(r, decoder, joined, octets):
+def conv_in_backward(r, decoder, joined, octets, prefetched):
     rows = r.hidden.shape[0]
     tables = (r.group_of[...], r.group_of_t[...])
     sides = [(r.hidden, r.stat_h, r.total if joined else r.grad_hidden, 0)]
@@ -571,7 +603,18 @@
     clear_edges(r.planes, octets)
     for c in range(CHUNKS):
         put_shifted(r.planes, 0, r.grad_conv_b[:, lanes(c)].astype(F32), c, octets)
-    for tap in range(TAPS):
+    if prefetched:
+        r.weights.need(CONV_IN, TAPS * span)
+        r.sides[...] = jnp.zeros(r.sides.shape, F32)
+
+        def one_tap(tap, down, across):
+            values = plane_rows(r.planes, 2 - across, 2 - down, octets, rows)
+            for half in range(len(sides)):
+                first = pl.multiple_of(tap * span + half * WIDTH, WIDTH)
+                r.sides[half] += dot_nt(values, r.held_conv_in[pl.ds(first, WIDTH), :])
+
+        tap_loop(one_tap)
+    for tap in range(0 if prefetched else TAPS):
         r.weights.need(CONV_IN, (tap + 1) * span)
         for _, _, _, half in sides:
             part = dot_nt(
@@ -867,7 +910,7 @@
             attention_backward(r, decoder, octets, shards, with_skip)
             middle_backward(r, octets)
         if second:
-            conv_in_backward(r, decoder, joined, octets)
+            conv_in_backward(r, decoder, joined, octets, first)
 
     return call(
         body,
@@ -1384,7 +1427,8 @@
 
     fields = lax.all_gather(outs[FIELDS], DP, axis=0)
     circle = Ring(outs[COLUMNS_W], DP)
-    turned = {0: outs[COLUMNS_W]}
+    columns_w, kept[-1] = together(outs[COLUMNS_W], kept[-1])
+    turned = {0: columns_w}
     w_rows, w_steps = {}, {}
 
     def beside(stage, *values):
@@ -1491,19 +1535,19 @@
     ring.spread()
     ring.share(1)
     cols += [with_out(step, cols_in_of(step)) for step in (2, 3)]
-    ring.values, ring.rows, ring.steps, cols, input_rows, small_grads = together(
-        ring.values, ring.rows, ring.steps, cols, input_rows, small_grads
+    ring.values, ring.rows, ring.steps, cols, input_rows = together(
+        ring.values, ring.rows, ring.steps, cols, input_rows
     )
     ring.spread_last()
     ring.share(2)
     input_grad = to_owners(input_rows, 0)
     totals = grad_step(cols[:2], ring.steps[0] + ring.steps[1], None)
+    ring.rows, ring.steps, cols, totals, input_grad, small_grads = together(
+        ring.rows, ring.steps, cols, totals, input_grad, small_grads
+    )
     small_grads = small_grads.astype(F32)
     qkv_grad = small_grads[:, : 3 * WIDTH]
     out_grad = small_grads[:, 3 * WIDTH : 4 * WIDTH]
-    ring.rows, ring.steps, cols, totals, input_grad, qkv_grad, out_grad = together(
-        ring.rows, ring.steps, cols, totals, input_grad, qkv_grad, out_grad
-    )
     ring.share(3)
     totals = grad_step(cols[2:], ring.steps[2] + ring.steps[3], totals)
     conv_out_grad, conv_in_grad = totals[:2]

time: 501 us -> 498 us (level)
  Pallas kernels: 134 us -> 122 us
  starting transfers between devices: 47 us -> 55.1 us
    ppermute x27, waiting for transfers between devices: 4.88 us -> 23.4 us  [send(): lax.ppermute(value, self.axis, [(i, target(i)) for i in range(self.count)])]
    pallas_call x13, Pallas kernels: 105 us -> 92.3 us  [call(): pl.pallas_call(kernel, out_shape=list(outputs.values()), in_specs=[IN_VME...]
    all_to_all x1, waiting for transfers between devices: 7.06 us -> 0.01 us  [on_device(): summed = lax.all_to_all(shares, DP, 0, 0, tiled=True).sum(axis=0)]
    reduce_scatter x1, waiting for transfers between devices: 5.1 us -> 0.02 us  [on_device(): lax.psum_scatter(products, DP, scatter_dimension=0, tiled=True)]
  transfers between devices with their start and end apart: 45 -> 45, of which waited for: 13 -> 13; matrix products, arithmetic and copies ran while one was open for 8% -> 9% of each run, Pallas kernels for 27% -> 24%
where the time goes in v3:
time: 498 us; the launch traced here: 492 us
  waiting for transfers between devices  238 us (48%)
  Pallas kernels  122 us (24%)
  starting transfers between devices  55.1 us (11%)
  local copies, waits for them, and re-layouts  34.2 us (7%)
  other arithmetic  26.3 us (5%)
  between operations  15.1 us (3%)
    all_gather x1, waiting for transfers between devices, section_weights(): lax.all_gather(jnp.where(is_decoder, everything[:first_rows], jnp.concate...  138 us
    pallas_call x13, Pallas kernels, call(): pl.pallas_call(kernel, out_shape=list(outputs.values()), in_specs=[IN_VME...  92.3 us
    ppermute x6, waiting for transfers between devices, moved(): return lax.ppermute(value, SECTION, [(source, target)])  42.1 us
    pallas_call x4, Pallas kernels, columns_in(): pl.pallas_call(partial(columns_in_kernel, octets, shared), grid_spec=pltp...  29.3 us
    ppermute x27, waiting for transfers between devices, send(): lax.ppermute(value, self.axis, [(i, target(i)) for i in range(self.count)])  23.4 us
    ppermute x27, starting transfers between devices, send(): lax.ppermute(value, self.axis, [(i, target(i)) for i in range(self.count)])  19.7 us
    all_gather x1, waiting for transfers between devices, section_weights(): second = lax.all_gather(everything[first_rows:], DP, axis=0)  17.2 us
    ppermute x6, starting transfers between devices, moved(): return lax.ppermute(value, SECTION, [(source, target)])  16 us
  transfers between devices with their start and end apart: 45, of which 13 were waited for; matrix products, arithmetic and copies ran while one was open for 9% of the time, Pallas kernels for 24%

profile of v3, /device:TPU:0, one launch (start us, length us, event | category | flops | bytes accessed | tf_op | source)
XLA Modules:
  0.0 492.3 jit_solution(2697647478158530477)
XLA Ops:
  8.8 1.9 gather_fusion.3
  13.0 1.1 constant_dynamic-update-slice_fusion.1
  14.2 1.3 pad_maximum_fusion
  15.5 2.2 gather_fusion.4
  18.0 1.2 constant_dynamic-update-slice_fusion.3
  19.3 1.6 broadcast_select_fusion
  22.1 4.7 collective-permute-start.1
  26.9 1.3 collective-permute-start
  29.4 1.6 collective-permute-start.3
  31.0 2.1 collective-permute-done.3
  33.1 1.6 collective-permute-start.4
  34.8 2.4 collective-permute-done.4
  37.2 2.7 collective-permute-start.5
  39.9 2.7 collective-permute-done.5
  46.8 6.2 %all-to-all-start = ((bf16[16,4,1536]{2,1,0:T(4,128)(2,1)}), bf16[16,4,1536]{2,1,0:T(4,128)(2,1)S(1)}, u32[]{:S(2)}, u32[]{:S(2)}) async-start(bf16[16,4,1536]{2,1,0:T(4,128)(2,1)} %reshape.1406), calls=%async_computation | async-start | bytes 393216 | tf_op jit(solution)/shard_map/all_to_all | solution.py:1358
  56.1 9.4 %all-to-all-done = bf16[16,4,1536]{2,1,0:T(4,128)(2,1)S(1)} async-done(((bf16[16,4,1536]{2,1,0:T(4,128)(2,1)}), bf16[16,4,1536]{2,1,0:T(4,128)(2,1)S(1)}, u32[]{:S(2)}, u32[]{:S(2)}) %all-to-all-start) | async-done | bytes 196640 | tf_op jit(solution)/shard_map/all_to_all | solution.py:1358
  66.3 138.0 %all-gather.6.cloned.1.call-done.refs_5_.refs_8_.refs_6_.refs_16_.refs_14_.refs_7_ = bf16[16,1440,768]{2,1,0:T(8,128)(2,1)} async-done(((bf16[1,1440,768]{2,1,0:T(8,128)(2,1)}), bf16[16,1440,768]{2,1,0:T(8,128)(2,1)}) %all-gather.6.cloned.1.call-update) | async-done | bytes 35389456 | tf_op jit(solution)/shard_map/all_gather | solution.py:1270
  204.4 19.8 %encoder_forward.1 = (f32[256,768]{1,0:T(8,128)}, f32[2,32,768]{2,1,0:T(8,128)}, bf16[832,256]{1,0:T(8,128)(2,1)}, bf16[768,256]{1,0:T(8,128)(2,1)}, f32[2,32,76...) custom-call(bf16[256,768]{1,0:T(8,128)(2,1)} %pad_maximum_fusion.6.r, ...), custom_call_target="tpu_custom_call" | custom-call | flops 7247757312 | bytes 6373376 | tf_op jit(solution)/shard_map/encoder_forward/pallas_call | solution.py:741
  224.2 1.3 collective-permute-start.7
  225.5 9.3 %collective-permute-done.7.refs_0_.refs_1_.refs_9_.refs_10_ = bf16[256,768]{1,0:T(8,128)(2,1)S(1)} collective-permute-done((bf16[256,768]{1,0:T(8,128)(2,1)}, bf16[256,768]{1,0:T(8,128)(2,1)S(1)}, u32[]{:S(2)}, u32[]{:S(2)}) %collective-permute-start.7) | collective-permute-done | bytes 393248 | tf_op jit(solution)/shard_map/ppermute | solution.py:1183
  235.6 2.0 conv_in_forward.1
  237.7 17.2 %all-gather.8.cloned.1.call-done = bf16[2304,768]{1,0:T(8,128)(2,1)} async-done(((bf16[144,768]{1,0:T(8,128)(2,1)}), bf16[2304,768]{1,0:T(8,128)(2,1)}) %all-gather.8.cloned.1.call-update) | async-done | bytes 3538960 | tf_op jit(solution)/shard_map/all_gather | solution.py:1273
  254.9 2.3 block_forward.1
  257.9 2.1 collective-permute-start.8
  259.9 1.8 collective-permute-start.9
  262.6 1.4 collective-permute-start.11
  264.1 4.2 section_backward.1
  268.2 13.2 %collective-permute-done.11 = bf16[128,768]{1,0:T(8,128)(2,1)S(1)} collective-permute-done((bf16[128,768]{1,0:T(8,128)(2,1)S(1)}, bf16[128,768]{1,0:T(8,128)(2,1)S(1)}, u32[]{:S(2)}, u32[]{:S(2)}) %collective-permute-start.11) | collective-permute-done | bytes 196640 | tf_op jit(solution)/shard_map/ppermute | solution.py:1183
  282.2 10.5 %collective-permute-done.9.refs_0_ = bf16[768,256]{1,0:T(8,128)(2,1)S(1)} collective-permute-done((bf16[768,256]{1,0:T(8,128)(2,1)S(1)}, bf16[768,256]{1,0:T(8,128)(2,1)S(1)}, u32[]{:S(2)}, u32[]{:S(2)}) %collective-permute-start.9) | collective-permute-done | bytes 393248 | tf_op jit(solution)/shard_map/ppermute | solution.py:1135
  292.8 1.3 collective-permute-start.16
  294.8 1.5 collective-permute-start.13
  296.8 19.6 %collective-permute-done.16.refs_0_ = bf16[256,768]{1,0:T(8,128)(2,1)S(1)} collective-permute-done((bf16[256,768]{1,0:T(8,128)(2,1)}, bf16[256,768]{1,0:T(8,128)(2,1)S(1)}, u32[]{:S(2)}, u32[]{:S(2)}) %collective-permute-start.16) | collective-permute-done | bytes 393248 | tf_op jit(solution)/shard_map/ppermute | solution.py:1183
  317.2 17.7 %block_backward.1 = (f32[16,768]{1,0:T(8,128)}, bf16[768,3072]{1,0:T(8,128)(2,1)}, bf16[528,768]{1,0:T(8,128)(2,1)}, f32[256,768]{1,0:T(8,128)}, bf16[256,768]{1,0:T(8,128)(2,1)}, /*index=5*/bf16[256,768]{1,0:T(8,128)(2,1)}) custom-call(bf16[256,768]{1,0:T(8,128)(2,1)} %copy-done.23, ...), custom_call_target="tpu_custom_call", output_to_operand_aliasing={{1}: (9, {}), {2}: (10, {})} | custom-call | flops 6945767424 | bytes 17645568 | tf_op jit(solution)/shard_map/block_backward/pallas_call | solution.py:741
  337.2 1.5 collective-permute-start.21
  338.7 1.9 pad_maximum_fusion.4
  340.6 2.1 pad_maximum_fusion.3
  347.0 1.2 copy.72.affine
  348.3 10.6 %conv_in_backward.1 = (f32[16,768]{1,0:T(8,128)}, f32[256,768]{1,0:T(8,128)}) custom-call(bf16[256,768]{1,0:T(8,128)(2,1)} %pad_maximum_fusion.6.refs_0_, f32[2,32,768]{2,1,0:T(8,128)} %get-tuple-element.257.refs_1_, f32[256,768]{1,0:T(8,128)} %get-tuple-element.258.refs_2_, bf16[256,768]{1,0:T(8,128)(2,1)} %get-tuple-element.259.refs_3_, ...), custom_call_target="tpu_custom_call" | custom-call | flops 2717908992 | bytes 3047424 | tf_op jit(solution)/shard_map/conv_in_backward/pallas_call | solution.py:741
  358.9 1.4 add.417
  360.3 7.4 %columns_in.4 = (bf16[864,1024]{1,0:T(8,128)(2,1)}, bf16[96,1024]{1,0:T(8,128)(2,1)}) custom-call(s32[2]{0:T(128)} %pad_add_fusion.place, s32[4]{0:T(128)} %pad_add_fusion.1.order, bf16[16,832,256]{2,1,0:T(8,128)(2,1)} %bitcast.146, f32[1536,2]{1,0:T(8,128)} %copy.72.affine), custom_call_target="tpu_custom_call" | custom-call | bytes 851968 | tf_op jit(solution)/shard_map/columns_in/pallas_call | solution.py:1002
  369.5 1.5 collective-permute-start.24
  371.5 2.0 pad_maximum_fusion.5
  374.7 1.5 reshape.1419
  376.2 1.4 reshape.1418
  379.1 4.9 all-to-all-start.1
  384.6 7.3 %columns_in.5 = (bf16[864,1024]{1,0:T(8,128)(2,1)}, bf16[96,1024]{1,0:T(8,128)(2,1)}) custom-call(s32[2]{0:T(128)} %pad_add_fusion.place, s32[4]{0:T(128)} %pad_add_fusion.2.order, bf16[16,832,256]{2,1,0:T(8,128)(2,1)} %bitcast.147, f32[1536,2]{1,0:T(8,128)} %copy.72.affine), custom_call_target="tpu_custom_call" | custom-call | bytes 851968 | tf_op jit(solution)/shard_map/columns_in/pallas_call | solution.py:1002
  391.9 2.7 columns_out.5.refs_3_
  394.7 2.7 columns_out.4.refs_0_
  398.3 1.9 collective-permute-start.27
  400.2 1.5 collective-permute-start.28
  403.4 7.3 %columns_in.7 = (bf16[864,1024]{1,0:T(8,128)(2,1)}, bf16[96,1024]{1,0:T(8,128)(2,1)}) custom-call(s32[2]{0:T(128)} %pad_add_fusion.place, s32[4]{0:T(128)} %pad_add_fusion.4.order, bf16[16,832,256]{2,1,0:T(8,128)(2,1)} %bitcast.148, f32[1536,2]{1,0:T(8,128)} %copy.72.affine), custom_call_target="tpu_custom_call" | custom-call | bytes 851968 | tf_op jit(solution)/shard_map/columns_in/pallas_call | solution.py:1002
  410.7 7.3 %columns_in.6 = (bf16[864,1024]{1,0:T(8,128)(2,1)}, bf16[96,1024]{1,0:T(8,128)(2,1)}) custom-call(s32[2]{0:T(128)} %pad_add_fusion.place, s32[4]{0:T(128)} %pad_add_fusion.3.order, bf16[16,832,256]{2,1,0:T(8,128)(2,1)} %bitcast.149, f32[1536,2]{1,0:T(8,128)} %copy.72.affine), custom_call_target="tpu_custom_call" | custom-call | bytes 851968 | tf_op jit(solution)/shard_map/columns_in/pallas_call | solution.py:1002
  418.0 2.7 columns_out.7.refs_3_
  420.7 2.8 columns_out.6.refs_0_
  423.5 9.0 %collective-permute-done.27.refs_12_.refs_10_ = bf16[528,768]{1,0:T(8,128)(2,1)S(1)} collective-permute-done((bf16[528,768]{1,0:T(8,128)(2,1)S(1)}, bf16[528,768]{1,0:T(8,128)(2,1)S(1)}, u32[]{:S(2)}, u32[]{:S(2)}) %collective-permute-start.27) | collective-permute-done | bytes 811040 | tf_op jit(solution)/shard_map/ppermute | solution.py:1135
  433.1 1.7 slice.165
  434.8 5.9 %collective-permute-start.35 = (bf16[128,768]{1,0:T(8,128)(2,1)}, bf16[128,768]{1,0:T(8,128)(2,1)}, u32[]{:S(2)}, u32[]{:S(2)}) collective-permute-start(bf16[128,768]{1,0:T(8,128)(2,1)} %slice.165), channel_id=1, source_target_pairs={{0,16},{1,17},{2,18},{3,19},{4,20},{5,21},{6,22},{7,23},{8,24},{9,... | collective-permute-start | bytes 589832 | tf_op jit(solution)/shard_map/ppermute | solution.py:1183
  441.7 1.7 collective-permute-start.31
  444.7 10.9 %grad_step.2 = (f32[432,768]{1,0:T(8,128)}, f32[864,768]{1,0:T(8,128)}, f32[96,768]{1,0:T(8,128)}) custom-call(bf16[432,1024]{1,0:T(8,128)(2,1)} %columns_out.4.refs_0_, bf16[864,1024]{1,0:T(8,128)(2,1)} %get-tuple-element.321.refs_1_, bf16[96,1024]{1,0:T(8,128)(2,1)} %get-tuple-element.322.refs_2_, bf16[432,1024]{1,0:T(8,128)(2,1)} %columns_out.5.refs_3_, ...), custom_call_target="tpu_custom_call" | custom-call | flops 1094713344 | bytes 4116480 | tf_op jit(solution)/shard_map/grad_step/pallas_call | solution.py:741
  457.4 3.3 collective-permute-done.32
  460.7 1.2 pad_maximum_fusion.1.refs_13_.refs_11_
  467.0 1.9 last_rows.1
  471.1 1.5 collective-permute-start.38
  472.6 12.0 %grad_step.3 = (f32[432,768]{1,0:T(8,128)}, f32[864,768]{1,0:T(8,128)}, f32[96,768]{1,0:T(8,128)}) custom-call(bf16[432,1024]{1,0:T(8,128)(2,1)} %columns_out.6.refs_0_, bf16[864,1024]{1,0:T(8,128)(2,1)} %get-tuple-element.355.refs_1_, bf16[96,1024]{1,0:T(8,128)(2,1)} %get-tuple-element.356.refs_2_, bf16[432,1024]{1,0:T(8,128)(2,1)} %columns_out.7.refs_3_, ...), custom_call_target="tpu_custom_call" | custom-call | flops 1094713344 | bytes 5185536 | tf_op jit(solution)/shard_map/grad_step/pallas_call | solution.py:741
  (256 shorter events, 47.2 us)
Async XLA Ops:
  7.2 38.7 %copy-start = (bf16[1,48,1536]{2,1,0:T(8,128)(2,1)S(1)}, bf16[1,48,1536]{2,1,0:T(8,128)(2,1)}, u32[]{:S(2)}) copy-start(bf16[1,48,1536]{2,1,0:T(8,128)(2,1)} %param.22) | copy-start | bytes 442372
  7.2 197.2 %all-gather.6.cloned.1.call-start = ((), (), s32[]{:S(2)}) async-start(), calls=%async_computation.3 | async-start | bytes 37601280 | tf_op jit(solution)/shard_map/all_gather | solution.py:1270
  10.8 3.4 collective-permute-start.6
  20.9 7.3 %copy-start.31 = (bf16[1,96,768]{2,1,0:T(8,128)(2,1)S(1)}, bf16[1,96,768]{2,1,0:T(8,128)(2,1)}, u32[]{:S(2)}) copy-start(bf16[1,96,768]{2,1,0:T(8,128)(2,1)} %param.23) | copy-start | bytes 442372
  20.9 23.1 %copy-start.38 = (bf16[1000,48]{0,1:T(8,128)(2,1)S(1)}, bf16[1000,48]{0,1:T(8,128)(2,1)}, u32[]{:S(2)}) copy-start(bf16[1000,48]{0,1:T(8,128)(2,1)} %param.19) | copy-start | bytes 288004
  21.0 233.9 %all-gather.8.cloned.1.call-start = ((), (), s32[]{:S(2)}) async-start(), calls=%async_computation.5 | async-start | bytes 3760128 | tf_op jit(solution)/shard_map/all_gather | solution.py:1273
  21.9 7.5 %collective-permute-start.2 = (f32[1,1,896]{2,0,1:T(1,128)S(1)}, f32[1,1,896]{2,0,1:T(1,128)S(1)}, u32[]{:S(2)}, u32[]{:S(2)}) collective-permute-start(f32[1,1,896]{2,0,1:T(1,128)S(1)} %broadcast_in_dim_broadcast_in_dim.3), channel_id=1, source_target_pairs={{0,1},{1,0},{2,3},{3,2},{4,5},{5,4},{6,7},{7,6},{8,9},{9,8},{10,11... | collective-permute-start | bytes 10760 | tf_op jit(solution)/shard_map/ppermute | solution.py:1113
  22.1 32.4 %collective-permute-start.1 = (bf16[128,768]{1,0:T(8,128)(2,1)S(1)}, bf16[128,768]{1,0:T(8,128)(2,1)S(1)}, u32[]{:S(2)}, u32[]{:S(2)}) collective-permute-start(bf16[128,768]{1,0:T(8,128)(2,1)S(1)} %bitcast.157), channel_id=1, source_target_pairs={{0,16},{1,17},{2,18},{3,19},{4,20},{5,21},{6,22},{7,23},{8,24},{9,... | collective-permute-start | bytes 589832 | tf_op jit(solution)/shard_map/ppermute | solution.py:1183
  26.9 28.5 %collective-permute-start = (bf16[128,768]{1,0:T(8,128)(2,1)S(1)}, bf16[128,768]{1,0:T(8,128)(2,1)S(1)}, u32[]{:S(2)}, u32[]{:S(2)}) collective-permute-start(bf16[128,768]{1,0:T(8,128)(2,1)S(1)} %bitcast.155), channel_id=1, source_target_pairs={{16,0},{17,1},{18,2},{19,3},{20,4},{21,5},{22,6},{23,7},{24,8},{25... | collective-permute-start | bytes 589832 | tf_op jit(solution)/shard_map/ppermute | solution.py:1183
  29.4 3.7 collective-permute-start.3
  33.1 4.1 collective-permute-start.4
  37.2 5.4 %collective-permute-start.5 = (f32[8,1,896]{2,0,1:T(8,128)S(1)}, f32[8,1,896]{2,0,1:T(8,128)S(1)}, u32[]{:S(2)}, u32[]{:S(2)}) collective-permute-start(f32[8,1,896]{2,0,1:T(8,128)S(1)} %maximum_select_fusion.2), channel_id=1, source_target_pairs={{0,8},{1,9},{2,10},{3,11},{4,12},{5,13},{6,14},{7,15},{8,0},{9,1},... | collective-permute-start | bytes 86024 | tf_op jit(solution)/shard_map/ppermute | solution.py:1113
  42.6 13.5 %copy-start.25 = (f32[16,896]{1,0:T(8,128)}, f32[16,896]{1,0:T(8,128)S(1)}, u32[]{:S(2)}) copy-start(f32[16,896]{1,0:T(8,128)S(1)} %maximum_select_fusion) | copy-start | bytes 172036
  46.8 18.7 %all-to-all-start = ((bf16[16,4,1536]{2,1,0:T(4,128)(2,1)}), bf16[16,4,1536]{2,1,0:T(4,128)(2,1)S(1)}, u32[]{:S(2)}, u32[]{:S(2)}) async-start(bf16[16,4,1536]{2,1,0:T(4,128)(2,1)} %reshape.1406), calls=%async_computation | async-start | bytes 393216 | tf_op jit(solution)/shard_map/all_to_all | solution.py:1358
  53.1 307.2 %all-gather.10.cloned.1.call-start = ((), (), s32[]{:S(2)}) async-start(), calls=%async_computation.6 | async-start | bytes 7241728 | tf_op jit(solution)/shard_map/all_gather | solution.py:1428
  224.2 10.7 %collective-permute-start.7 = (bf16[256,768]{1,0:T(8,128)(2,1)}, bf16[256,768]{1,0:T(8,128)(2,1)S(1)}, u32[]{:S(2)}, u32[]{:S(2)}) collective-permute-start(bf16[256,768]{1,0:T(8,128)(2,1)} %get-tuple-element.192), channel_id=1, source_target_pairs={{0,16},{1,17},{2,18},{3,19},{4,20},{5,21},{6,22},{7,23},{8,24},{9,... | collective-permute-start | bytes 1179656 | tf_op jit(solution)/shard_map/ppermute | solution.py:1183
  237.7 224.3 %reduce-scatter.2.cloned.1.call-start = ((), (), s32[]{:S(2)}) async-start(), calls=%async_computation.4 | async-start | bytes 5013504 | tf_op jit(solution)/shard_map/reduce_scatter | solution.py:1516
  257.2 25.0 %collective-permute-start.10 = (bf16[768,256]{1,0:T(8,128)(2,1)S(1)}, bf16[768,256]{1,0:T(8,128)(2,1)S(1)}, u32[]{:S(2)}, u32[]{:S(2)}) collective-permute-start(bf16[768,256]{1,0:T(8,128)(2,1)S(1)} %copy-done.8), channel_id=1, source_target_pairs={{0,2},{1,3},{2,0},{3,1},{4,6},{5,7},{6,4},{7,5},{8,10},{9,11},{10,... | collective-permute-start | bytes 1179656 | tf_op jit(solution)/shard_map/ppermute | solution.py:1135
  257.9 24.3 %collective-permute-start.8 = (bf16[768,256]{1,0:T(8,128)(2,1)S(1)}, bf16[768,256]{1,0:T(8,128)(2,1)S(1)}, u32[]{:S(2)}, u32[]{:S(2)}) collective-permute-start(bf16[768,256]{1,0:T(8,128)(2,1)S(1)} %copy-done.8), channel_id=1, source_target_pairs={{0,4},{1,5},{2,6},{3,7},{4,8},{5,9},{6,10},{7,11},{8,12},{9,13},{1... | collective-permute-start | bytes 1179656 | tf_op jit(solution)/shard_map/ppermute | solution.py:1135
  259.9 32.8 %collective-permute-start.9 = (bf16[768,256]{1,0:T(8,128)(2,1)S(1)}, bf16[768,256]{1,0:T(8,128)(2,1)S(1)}, u32[]{:S(2)}, u32[]{:S(2)}) collective-permute-start(bf16[768,256]{1,0:T(8,128)(2,1)S(1)} %copy-done.8), channel_id=1, source_target_pairs={{0,12},{1,13},{2,14},{3,15},{4,0},{5,1},{6,2},{7,3},{8,4},{9,5},{1... | collective-permute-start | bytes 1179656 | tf_op jit(solution)/shard_map/ppermute | solution.py:1135
  262.6 18.9 %copy-start.24 = (bf16[256,768]{1,0:T(8,128)(2,1)S(1)}, bf16[256,768]{1,0:T(8,128)(2,1)}, u32[]{:S(2)}) copy-start(bf16[256,768]{1,0:T(8,128)(2,1)} %get-tuple-element.223) | copy-start | bytes 1179652
  262.6 18.8 %collective-permute-start.11 = (bf16[128,768]{1,0:T(8,128)(2,1)S(1)}, bf16[128,768]{1,0:T(8,128)(2,1)S(1)}, u32[]{:S(2)}, u32[]{:S(2)}) collective-permute-start(bf16[128,768]{1,0:T(8,128)(2,1)S(1)} %slice.96), channel_id=1, source_target_pairs={{16,0},{17,1},{18,2},{19,3},{20,4},{21,5},{22,6},{23,7},{24,8},{25... | collective-permute-start | bytes 589832 | tf_op jit(solution)/shard_map/ppermute | solution.py:1183
  282.2 52.7 %copy-start.17 = (bf16[768,256]{1,0:T(8,128)(2,1)}, bf16[768,256]{1,0:T(8,128)(2,1)S(1)}, u32[]{:S(2)}) copy-start(bf16[768,256]{1,0:T(8,128)(2,1)S(1)} %collective-permute-done.10.refs_1_) | copy-start | bytes 1179652
  282.2 52.7 %copy-start.19 = (bf16[768,256]{1,0:T(8,128)(2,1)}, bf16[768,256]{1,0:T(8,128)(2,1)S(1)}, u32[]{:S(2)}) copy-start(bf16[768,256]{1,0:T(8,128)(2,1)S(1)} %collective-permute-done.8.refs_0_) | copy-start | bytes 1179652
  292.7 45.9 %copy-start.14 = (bf16[768,256]{1,0:T(8,128)(2,1)}, bf16[768,256]{1,0:T(8,128)(2,1)S(1)}, u32[]{:S(2)}) copy-start(bf16[768,256]{1,0:T(8,128)(2,1)S(1)} %collective-permute-done.9.refs_0_) | copy-start | bytes 1179652
  292.8 23.6 %collective-permute-start.16 = (bf16[256,768]{1,0:T(8,128)(2,1)}, bf16[256,768]{1,0:T(8,128)(2,1)S(1)}, u32[]{:S(2)}, u32[]{:S(2)}) collective-permute-start(bf16[256,768]{1,0:T(8,128)(2,1)} %get-tuple-element.229), channel_id=1, source_target_pairs={{16,0},{17,1},{18,2},{19,3},{20,4},{21,5},{22,6},{23,7},{24,8},{25... | collective-permute-start | bytes 1179656 | tf_op jit(solution)/shard_map/ppermute | solution.py:1183
  294.1 41.6 %collective-permute-start.15 = (bf16[1536,256]{1,0:T(8,128)(2,1)S(1)}, bf16[1536,256]{1,0:T(8,128)(2,1)}, u32[]{:S(2)}, u32[]{:S(2)}) collective-permute-start(bf16[1536,256]{1,0:T(8,128)(2,1)S(1)} %pad_maximum_fusion.2), channel_id=1, source_target_pairs={{0,1},{1,0},{2,3},{3,2},{4,5},{5,4},{6,7},{7,6},{8,9},{9,8},{10,11... | collective-permute-start | bytes 2359304 | tf_op jit(solution)/shard_map/ppermute | solution.py:1135
  294.2 40.7 %collective-permute-start.12 = (bf16[768,256]{1,0:T(8,128)(2,1)S(1)}, bf16[768,256]{1,0:T(8,128)(2,1)S(1)}, u32[]{:S(2)}, u32[]{:S(2)}) collective-permute-start(bf16[768,256]{1,0:T(8,128)(2,1)S(1)} %collective-permute-done.8.refs_0_), channel_id=1, source_target_pairs={{0,4},{1,5},{2,6},{3,7},{4,8},{5,9},{6,10},{7,11},{8,12},{9,13},{1... | collective-permute-start | bytes 1179656 | tf_op jit(solution)/shard_map/ppermute | solution.py:1135
  294.8 40.1 %collective-permute-start.13 = (bf16[768,256]{1,0:T(8,128)(2,1)S(1)}, bf16[768,256]{1,0:T(8,128)(2,1)S(1)}, u32[]{:S(2)}, u32[]{:S(2)}) collective-permute-start(bf16[768,256]{1,0:T(8,128)(2,1)S(1)} %collective-permute-done.8.refs_0_), channel_id=1, source_target_pairs={{0,2},{1,3},{2,0},{3,1},{4,6},{5,7},{6,4},{7,5},{8,10},{9,11},{10,... | collective-permute-start | bytes 1179656 | tf_op jit(solution)/shard_map/ppermute | solution.py:1135
  296.3 38.6 %collective-permute-start.14 = (bf16[768,256]{1,0:T(8,128)(2,1)S(1)}, bf16[768,256]{1,0:T(8,128)(2,1)S(1)}, u32[]{:S(2)}, u32[]{:S(2)}) collective-permute-start(bf16[768,256]{1,0:T(8,128)(2,1)S(1)} %collective-permute-done.9.refs_0_), channel_id=1, source_target_pairs={{0,2},{1,3},{2,0},{3,1},{4,6},{5,7},{6,4},{7,5},{8,10},{9,11},{10,... | collective-permute-start | bytes 1179656 | tf_op jit(solution)/shard_map/ppermute | solution.py:1135
  334.9 10.9 %copy-start.15 = (bf16[768,256]{1,0:T(8,128)(2,1)}, bf16[768,256]{1,0:T(8,128)(2,1)S(1)}, u32[]{:S(2)}) copy-start(bf16[768,256]{1,0:T(8,128)(2,1)S(1)} %collective-permute-done.12.refs_0_) | copy-start | bytes 1179652
  337.0 30.8 %collective-permute-start.20 = (bf16[528,768]{1,0:T(8,128)(2,1)S(1)}, bf16[528,768]{1,0:T(8,128)(2,1)S(1)}, u32[]{:S(2)}, u32[]{:S(2)}) collective-permute-start(bf16[528,768]{1,0:T(8,128)(2,1)S(1)} %copy-done.2), channel_id=1, source_target_pairs={{0,4},{1,5},{2,6},{3,7},{4,8},{5,9},{6,10},{7,11},{8,12},{9,13},{1... | collective-permute-start | bytes 2433032 | tf_op jit(solution)/shard_map/ppermute | solution.py:1135
  337.2 30.5 %collective-permute-start.21 = (bf16[528,768]{1,0:T(8,128)(2,1)S(1)}, bf16[528,768]{1,0:T(8,128)(2,1)S(1)}, u32[]{:S(2)}, u32[]{:S(2)}) collective-permute-start(bf16[528,768]{1,0:T(8,128)(2,1)S(1)} %copy-done.2), channel_id=1, source_target_pairs={{0,2},{1,3},{2,0},{3,1},{4,6},{5,7},{6,4},{7,5},{8,10},{9,11},{10,... | collective-permute-start | bytes 2433032 | tf_op jit(solution)/shard_map/ppermute | solution.py:1135
  340.6 27.1 %collective-permute-start.19 = (bf16[1536,256]{1,0:T(8,128)(2,1)}, bf16[1536,256]{1,0:T(8,128)(2,1)}, u32[]{:S(2)}, u32[]{:S(2)}) collective-permute-start(bf16[1536,256]{1,0:T(8,128)(2,1)} %pad_maximum_fusion.4), channel_id=1, source_target_pairs={{0,1},{1,0},{2,3},{3,2},{4,5},{5,4},{6,7},{7,6},{8,9},{9,8},{10,11... | collective-permute-start | bytes 2359304 | tf_op jit(solution)/shard_map/ppermute | solution.py:1135
  342.7 25.0 %collective-permute-start.18 = (bf16[1536,256]{1,0:T(8,128)(2,1)}, bf16[1536,256]{1,0:T(8,128)(2,1)}, u32[]{:S(2)}, u32[]{:S(2)}) collective-permute-start(bf16[1536,256]{1,0:T(8,128)(2,1)} %pad_maximum_fusion.3), channel_id=1, source_target_pairs={{0,1},{1,0},{2,3},{3,2},{4,5},{5,4},{6,7},{7,6},{8,9},{9,8},{10,11... | collective-permute-start | bytes 2359304 | tf_op jit(solution)/shard_map/ppermute | solution.py:1135
  345.8 21.9 %collective-permute-start.17 = (bf16[768,256]{1,0:T(8,128)(2,1)S(1)}, bf16[768,256]{1,0:T(8,128)(2,1)S(1)}, u32[]{:S(2)}, u32[]{:S(2)}) collective-permute-start(bf16[768,256]{1,0:T(8,128)(2,1)S(1)} %collective-permute-done.12.refs_0_), channel_id=1, source_target_pairs={{0,2},{1,3},{2,0},{3,1},{4,6},{5,7},{6,4},{7,5},{8,10},{9,11},{10,... | collective-permute-start | bytes 1179656 | tf_op jit(solution)/shard_map/ppermute | solution.py:1135
  348.3 10.6 %copy-start.33 = (f32[16,768]{1,0:T(8,128)S(1)}, f32[16,768]{1,0:T(8,128)}, u32[]{:S(2)}) copy-start(f32[16,768]{1,0:T(8,128)} %get-tuple-element.256) | copy-start | bytes 147460
  360.3 11.2 %copy-start.16 = (bf16[768,256]{1,0:T(8,128)(2,1)S(1)}, bf16[768,256]{1,0:T(8,128)(2,1)}, u32[]{:S(2)}) copy-start(bf16[768,256]{1,0:T(8,128)(2,1)} %copy-done.15) | copy-start | bytes 1179652
  360.3 13.2 %copy-start.30 = (f32[16,768]{1,0:T(8,128)S(1)}, f32[16,768]{1,0:T(8,128)}, u32[]{:S(2)}) copy-start(f32[16,768]{1,0:T(8,128)} %add.417) | copy-start | bytes 147460
  360.3 13.2 %copy-start.32 = (f32[16,768]{1,0:T(8,128)S(1)}, f32[16,768]{1,0:T(8,128)}, u32[]{:S(2)}) copy-start(f32[16,768]{1,0:T(8,128)} %get-tuple-element.282) | copy-start | bytes 147460
  367.7 34.0 %copy-start.12 = (bf16[528,768]{1,0:T(8,128)(2,1)}, bf16[528,768]{1,0:T(8,128)(2,1)S(1)}, u32[]{:S(2)}) copy-start(bf16[528,768]{1,0:T(8,128)(2,1)S(1)} %collective-permute-done.20.refs_10_.refs_4_) | copy-start | bytes 2433028
  367.7 24.2 %copy-start.13 = (bf16[528,768]{1,0:T(8,128)(2,1)}, bf16[528,768]{1,0:T(8,128)(2,1)S(1)}, u32[]{:S(2)}) copy-start(bf16[528,768]{1,0:T(8,128)(2,1)S(1)} %collective-permute-done.21.refs_7_.refs_1_) | copy-start | bytes 2433028
  368.7 29.5 %collective-permute-start.23 = (bf16[528,768]{1,0:T(8,128)(2,1)S(1)}, bf16[528,768]{1,0:T(8,128)(2,1)S(1)}, u32[]{:S(2)}, u32[]{:S(2)}) collective-permute-start(bf16[528,768]{1,0:T(8,128)(2,1)S(1)} %collective-permute-done.20.refs_10_.refs_4_), channel_id=1, source_target_pairs={{0,4},{1,5},{2,6},{3,7},{4,8},{5,9},{6,10},{7,11},{8,12},{9,13},{1... | collective-permute-start | bytes 2433032 | tf_op jit(solution)/shard_map/ppermute | solution.py:1135
  369.5 28.8 %collective-permute-start.24 = (bf16[528,768]{1,0:T(8,128)(2,1)S(1)}, bf16[528,768]{1,0:T(8,128)(2,1)}, u32[]{:S(2)}, u32[]{:S(2)}) collective-permute-start(bf16[528,768]{1,0:T(8,128)(2,1)S(1)} %collective-permute-done.20.refs_10_.refs_4_), channel_id=1, source_target_pairs={{0,2},{1,3},{2,0},{3,1},{4,6},{5,7},{6,4},{7,5},{8,10},{9,11},{10,... | collective-permute-start | bytes 2433032 | tf_op jit(solution)/shard_map/ppermute | solution.py:1135
  371.0 27.3 %collective-permute-start.25 = (bf16[528,768]{1,0:T(8,128)(2,1)S(1)}, bf16[528,768]{1,0:T(8,128)(2,1)}, u32[]{:S(2)}, u32[]{:S(2)}) collective-permute-start(bf16[528,768]{1,0:T(8,128)(2,1)S(1)} %copy-done.2), channel_id=1, source_target_pairs={{0,1},{1,0},{2,3},{3,2},{4,5},{5,4},{6,7},{7,6},{8,9},{9,8},{10,11... | collective-permute-start | bytes 2433032 | tf_op jit(solution)/shard_map/ppermute | solution.py:1135
  371.0 27.3 %collective-permute-start.26 = (bf16[528,768]{1,0:T(8,128)(2,1)S(1)}, bf16[528,768]{1,0:T(8,128)(2,1)}, u32[]{:S(2)}, u32[]{:S(2)}) collective-permute-start(bf16[528,768]{1,0:T(8,128)(2,1)S(1)} %collective-permute-done.21.refs_7_.refs_1_), channel_id=1, source_target_pairs={{0,1},{1,0},{2,3},{3,2},{4,5},{5,4},{6,7},{7,6},{8,9},{9,8},{10,11... | collective-permute-start | bytes 2433032 | tf_op jit(solution)/shard_map/ppermute | solution.py:1135
  373.5 24.8 %collective-permute-start.22 = (bf16[1536,256]{1,0:T(8,128)(2,1)}, bf16[1536,256]{1,0:T(8,128)(2,1)}, u32[]{:S(2)}, u32[]{:S(2)}) collective-permute-start(bf16[1536,256]{1,0:T(8,128)(2,1)} %pad_maximum_fusion.5), channel_id=1, source_target_pairs={{0,1},{1,0},{2,3},{3,2},{4,5},{5,4},{6,7},{7,6},{8,9},{9,8},{10,11... | collective-permute-start | bytes 2359304 | tf_op jit(solution)/shard_map/ppermute | solution.py:1135
  379.1 18.2 %all-to-all-start.1 = ((f32[16,1,768]{2,1,0:T(1,128)}), f32[16,1,768]{2,1,0:T(1,128)}, u32[]{:S(2)}, u32[]{:S(2)}) async-start(f32[16,1,768]{2,1,0:T(1,128)} %all_to_all.10), calls=%async_computation.1 | async-start | bytes 98304 | tf_op jit(solution)/shard_map/all_to_all | solution.py:1526
  398.2 34.2 %copy-start.9 = (bf16[528,768]{1,0:T(8,128)(2,1)}, bf16[528,768]{1,0:T(8,128)(2,1)S(1)}, u32[]{:S(2)}) copy-start(bf16[528,768]{1,0:T(8,128)(2,1)S(1)} %collective-permute-done.23.refs_8_.refs_6_) | copy-start | bytes 2433028
  398.3 34.2 %collective-permute-start.27 = (bf16[528,768]{1,0:T(8,128)(2,1)S(1)}, bf16[528,768]{1,0:T(8,128)(2,1)S(1)}, u32[]{:S(2)}, u32[]{:S(2)}) collective-permute-start(bf16[528,768]{1,0:T(8,128)(2,1)S(1)} %collective-permute-done.23.refs_8_.refs_6_), channel_id=1, source_target_pairs={{0,4},{1,5},{2,6},{3,7},{4,8},{5,9},{6,10},{7,11},{8,12},{9,13},{1... | collective-permute-start | bytes 2433032 | tf_op jit(solution)/shard_map/ppermute | solution.py:1135
  400.2 32.2 %collective-permute-start.28 = (bf16[528,768]{1,0:T(8,128)(2,1)S(1)}, bf16[528,768]{1,0:T(8,128)(2,1)S(1)}, u32[]{:S(2)}, u32[]{:S(2)}) collective-permute-start(bf16[528,768]{1,0:T(8,128)(2,1)S(1)} %collective-permute-done.23.refs_8_.refs_6_), channel_id=1, source_target_pairs={{0,2},{1,3},{2,0},{3,1},{4,6},{5,7},{6,4},{7,5},{8,10},{9,11},{10,... | collective-permute-start | bytes 2433032 | tf_op jit(solution)/shard_map/ppermute | solution.py:1135
  401.7 30.8 %collective-permute-start.29 = (bf16[528,768]{1,0:T(8,128)(2,1)S(1)}, bf16[528,768]{1,0:T(8,128)(2,1)}, u32[]{:S(2)}, u32[]{:S(2)}) collective-permute-start(bf16[528,768]{1,0:T(8,128)(2,1)S(1)} %collective-permute-done.20.refs_10_.refs_4_), channel_id=1, source_target_pairs={{0,1},{1,0},{2,3},{3,2},{4,5},{5,4},{6,7},{7,6},{8,9},{9,8},{10,11... | collective-permute-start | bytes 2433032 | tf_op jit(solution)/shard_map/ppermute | solution.py:1135
  401.7 30.8 %collective-permute-start.30 = (bf16[528,768]{1,0:T(8,128)(2,1)}, bf16[528,768]{1,0:T(8,128)(2,1)}, u32[]{:S(2)}, u32[]{:S(2)}) collective-permute-start(bf16[528,768]{1,0:T(8,128)(2,1)} %collective-permute-done.24.refs_11_.refs_5_), channel_id=1, source_target_pairs={{0,1},{1,0},{2,3},{3,2},{4,5},{5,4},{6,7},{7,6},{8,9},{9,8},{10,11... | collective-permute-start | bytes 2433032 | tf_op jit(solution)/shard_map/ppermute | solution.py:1135
  432.5 29.5 %copy-start.7 = (bf16[528,768]{1,0:T(8,128)(2,1)}, bf16[528,768]{1,0:T(8,128)(2,1)S(1)}, u32[]{:S(2)}) copy-start(bf16[528,768]{1,0:T(8,128)(2,1)S(1)} %collective-permute-done.27.refs_12_.refs_10_) | copy-start | bytes 2433028
  432.5 23.1 %copy-start.6 = (bf16[528,768]{1,0:T(8,128)(2,1)}, bf16[528,768]{1,0:T(8,128)(2,1)S(1)}, u32[]{:S(2)}) copy-start(bf16[528,768]{1,0:T(8,128)(2,1)S(1)} %collective-permute-done.28.refs_9_.refs_7_) | copy-start | bytes 2433028
  432.5 29.5 %collective-permute-start.33 = (bf16[528,768]{1,0:T(8,128)(2,1)S(1)}, bf16[528,768]{1,0:T(8,128)(2,1)}, u32[]{:S(2)}, u32[]{:S(2)}) collective-permute-start(bf16[528,768]{1,0:T(8,128)(2,1)S(1)} %collective-permute-done.23.refs_8_.refs_6_), channel_id=1, source_target_pairs={{0,1},{1,0},{2,3},{3,2},{4,5},{5,4},{6,7},{7,6},{8,9},{9,8},{10,11... | collective-permute-start | bytes 2433032 | tf_op jit(solution)/shard_map/ppermute | solution.py:1135
  432.6 29.4 %collective-permute-start.34 = (bf16[528,768]{1,0:T(8,128)(2,1)S(1)}, bf16[528,768]{1,0:T(8,128)(2,1)}, u32[]{:S(2)}, u32[]{:S(2)}) collective-permute-start(bf16[528,768]{1,0:T(8,128)(2,1)S(1)} %collective-permute-done.28.refs_9_.refs_7_), channel_id=1, source_target_pairs={{0,1},{1,0},{2,3},{3,2},{4,5},{5,4},{6,7},{7,6},{8,9},{9,8},{10,11... | collective-permute-start | bytes 2433032 | tf_op jit(solution)/shard_map/ppermute | solution.py:1135
  434.8 20.9 %collective-permute-start.35 = (bf16[128,768]{1,0:T(8,128)(2,1)}, bf16[128,768]{1,0:T(8,128)(2,1)}, u32[]{:S(2)}, u32[]{:S(2)}) collective-permute-start(bf16[128,768]{1,0:T(8,128)(2,1)} %slice.165), channel_id=1, source_target_pairs={{0,16},{1,17},{2,18},{3,19},{4,20},{5,21},{6,22},{7,23},{8,24},{9,... | collective-permute-start | bytes 589832 | tf_op jit(solution)/shard_map/ppermute | solution.py:1183
  440.7 20.0 %collective-permute-start.32 = (bf16[272,768]{1,0:T(8,128)(2,1)S(1)}, bf16[272,768]{1,0:T(8,128)(2,1)}, u32[]{:S(2)}, u32[]{:S(2)}) collective-permute-start(bf16[272,768]{1,0:T(8,128)(2,1)S(1)} %slice.102), channel_id=1, source_target_pairs={{0,4},{1,5},{2,6},{3,7},{4,8},{5,9},{6,10},{7,11},{8,12},{9,13},{1... | collective-permute-start | bytes 1253384 | tf_op jit(solution)/shard_map/ppermute | solution.py:1135
  441.7 15.7 %collective-permute-start.31 = (bf16[256,768]{1,0:T(8,128)(2,1)}, bf16[256,768]{1,0:T(8,128)(2,1)}, u32[]{:S(2)}, u32[]{:S(2)}) collective-permute-start(bf16[256,768]{1,0:T(8,128)(2,1)} %slice.101), channel_id=1, source_target_pairs={{0,2},{1,3},{2,0},{3,1},{4,6},{5,7},{6,4},{7,5},{8,10},{9,11},{10,... | collective-permute-start | bytes 1179656 | tf_op jit(solution)/shard_map/ppermute | solution.py:1135
  444.7 11.0 %copy-start.22 = (f32[256,768]{1,0:T(8,128)S(1)}, f32[256,768]{1,0:T(8,128)}, u32[]{:S(2)}) copy-start(f32[256,768]{1,0:T(8,128)} %get-tuple-element.335) | copy-start | bytes 2359300
  462.0 3.0 collective-permute-start.36
  462.1 3.5 collective-permute-start.37
  471.1 13.5 %collective-permute-start.38 = (f32[64,48]{0,1:T(8,128)S(1)}, f32[64,48]{0,1:T(8,128)S(1)}, u32[]{:S(2)}, u32[]{:S(2)}) collective-permute-start(f32[64,48]{0,1:T(8,128)S(1)} %fusion.1), channel_id=1, source_target_pairs={{0,16},{16,0},{1,17},{17,1},{2,18},{18,2},{3,19},{19,3},{4,20},{20... | collective-permute-start | bytes 36872 | tf_op jit(solution)/shard_map/ppermute | solution.py:1563
  (21 other events, 42.4 us)
Sparse Core Ops, SparseCore 0:
  21.1 183.2 all-gather.5
  207.2 47.5 all-gather.7
  257.7 91.2 all-gather.9
  352.8 105.5 reduce-scatter.1

commit v4 on v3

--- a/solution.py
+++ b/solution.py
@@ -1535,13 +1535,14 @@
     ring.spread()
     ring.share(1)
     cols += [with_out(step, cols_in_of(step)) for step in (2, 3)]
-    ring.values, ring.rows, ring.steps, cols, input_rows = together(
-        ring.values, ring.rows, ring.steps, cols, input_rows
+    totals = grad_step(cols[:1], ring.steps[0], None)
+    ring.values, ring.rows, ring.steps, cols, input_rows, totals = together(
+        ring.values, ring.rows, ring.steps, cols, input_rows, totals
     )
     ring.spread_last()
     ring.share(2)
     input_grad = to_owners(input_rows, 0)
-    totals = grad_step(cols[:2], ring.steps[0] + ring.steps[1], None)
+    totals = grad_step(cols[1:3], ring.steps[1] + ring.steps[2], totals)
     ring.rows, ring.steps, cols, totals, input_grad, small_grads = together(
         ring.rows, ring.steps, cols, totals, input_grad, small_grads
     )
@@ -1549,7 +1550,7 @@
     qkv_grad = small_grads[:, : 3 * WIDTH]
     out_grad = small_grads[:, 3 * WIDTH : 4 * WIDTH]
     ring.share(3)
-    totals = grad_step(cols[2:], ring.steps[2] + ring.steps[3], totals)
+    totals = grad_step(cols[3:], ring.steps[3], totals)
     conv_out_grad, conv_in_grad = totals[:2]
     gains_grad, biases_grad = summed[:gain_share], summed[gain_share:]
 

time: 498 us -> 505 us (1.014)
  waiting for transfers between devices: 238 us -> 245 us
    ppermute x27, waiting for transfers between devices: 23.4 us -> 29.7 us  [send(): lax.ppermute(value, self.axis, [(i, target(i)) for i in range(self.count)])]
    pallas_call x13 -> x14, Pallas kernels: 92.3 us -> 96.2 us  [call(): pl.pallas_call(kernel, out_shape=list(outputs.values()), in_specs=[IN_VME...]
    unnamed x89 -> x91, local copies, waits for them, and re-layouts: 9.6 us -> 10.5 us
  transfers between devices with their start and end apart: 45 -> 45, of which waited for: 13 -> 15; matrix products, arithmetic and copies ran while one was open for 9% -> 8% of each run, Pallas kernels for 24% -> 25%
where the time goes in v4:
time: 505 us; the launch traced here: 500 us
  waiting for transfers between devices  245 us (49%)
  Pallas kernels  126 us (25%)
  starting transfers between devices  53.7 us (11%)
  local copies, waits for them, and re-layouts  33.6 us (7%)
  other arithmetic  24.3 us (5%)
  between operations  15.1 us (3%)
    all_gather x1, waiting for transfers between devices, section_weights(): lax.all_gather(jnp.where(is_decoder, everything[:first_rows], jnp.concate...  138 us
    pallas_call x14, Pallas kernels, call(): pl.pallas_call(kernel, out_shape=list(outputs.values()), in_specs=[IN_VME...  96.2 us
    ppermute x6, waiting for transfers between devices, moved(): return lax.ppermute(value, SECTION, [(source, target)])  43 us
    ppermute x27, waiting for transfers between devices, send(): lax.ppermute(value, self.axis, [(i, target(i)) for i in range(self.count)])  29.7 us
    pallas_call x4, Pallas kernels, columns_in(): pl.pallas_call(partial(columns_in_kernel, octets, shared), grid_spec=pltp...  29.4 us
    ppermute x27, starting transfers between devices, send(): lax.ppermute(value, self.axis, [(i, target(i)) for i in range(self.count)])  20 us
    all_gather x1, waiting for transfers between devices, section_weights(): second = lax.all_gather(everything[first_rows:], DP, axis=0)  17.2 us
    ppermute x6, starting transfers between devices, moved(): return lax.ppermute(value, SECTION, [(source, target)])  15.3 us
  transfers between devices with their start and end apart: 45, of which 15 were waited for; matrix products, arithmetic and copies ran while one was open for 8% of the time, Pallas kernels for 25%

profile of v4, /device:TPU:0, one launch (start us, length us, event | category | flops | bytes accessed | tf_op | source)
XLA Modules:
  0.0 499.6 jit_solution(18290726640648264605)
XLA Ops:
  8.8 1.9 gather_fusion.3
  13.0 1.1 constant_dynamic-update-slice_fusion.1
  14.2 1.4 pad_maximum_fusion
  15.5 2.2 gather_fusion.4
  18.0 1.2 constant_dynamic-update-slice_fusion.3
  19.3 1.6 broadcast_select_fusion
  22.1 4.7 collective-permute-start.1
  26.9 1.3 collective-permute-start
  29.4 1.6 collective-permute-start.3
  31.0 2.1 collective-permute-done.3
  33.1 1.6 collective-permute-start.4
  34.8 2.4 collective-permute-done.4
  37.2 2.7 collective-permute-start.5
  39.9 2.7 collective-permute-done.5
  46.8 6.2 %all-to-all-start = ((bf16[16,4,1536]{2,1,0:T(4,128)(2,1)}), bf16[16,4,1536]{2,1,0:T(4,128)(2,1)S(1)}, u32[]{:S(2)}, u32[]{:S(2)}) async-start(bf16[16,4,1536]{2,1,0:T(4,128)(2,1)} %reshape.1406), calls=%async_computation | async-start | bytes 393216 | tf_op jit(solution)/shard_map/all_to_all | solution.py:1358
  56.2 9.4 %all-to-all-done = bf16[16,4,1536]{2,1,0:T(4,128)(2,1)S(1)} async-done(((bf16[16,4,1536]{2,1,0:T(4,128)(2,1)}), bf16[16,4,1536]{2,1,0:T(4,128)(2,1)S(1)}, u32[]{:S(2)}, u32[]{:S(2)}) %all-to-all-start) | async-done | bytes 196640 | tf_op jit(solution)/shard_map/all_to_all | solution.py:1358
  66.4 138.0 %all-gather.6.cloned.1.call-done.refs_5_.refs_8_.refs_6_.refs_16_.refs_14_.refs_7_ = bf16[16,1440,768]{2,1,0:T(8,128)(2,1)} async-done(((bf16[1,1440,768]{2,1,0:T(8,128)(2,1)}), bf16[16,1440,768]{2,1,0:T(8,128)(2,1)}) %all-gather.6.cloned.1.call-update) | async-done | bytes 35389456 | tf_op jit(solution)/shard_map/all_gather | solution.py:1270
  204.4 19.8 %encoder_forward.1 = (f32[256,768]{1,0:T(8,128)}, f32[2,32,768]{2,1,0:T(8,128)}, bf16[832,256]{1,0:T(8,128)(2,1)}, bf16[768,256]{1,0:T(8,128)(2,1)}, f32[2,32,76...) custom-call(bf16[256,768]{1,0:T(8,128)(2,1)} %pad_maximum_fusion.6.r, ...), custom_call_target="tpu_custom_call" | custom-call | flops 7247757312 | bytes 6373376 | tf_op jit(solution)/shard_map/encoder_forward/pallas_call | solution.py:741
  224.2 1.3 collective-permute-start.7
  225.5 9.3 %collective-permute-done.7.refs_0_.refs_1_.refs_9_.refs_10_ = bf16[256,768]{1,0:T(8,128)(2,1)S(1)} collective-permute-done((bf16[256,768]{1,0:T(8,128)(2,1)}, bf16[256,768]{1,0:T(8,128)(2,1)S(1)}, u32[]{:S(2)}, u32[]{:S(2)}) %collective-permute-start.7) | collective-permute-done | bytes 393248 | tf_op jit(solution)/shard_map/ppermute | solution.py:1183
  235.6 2.0 conv_in_forward.1
  237.7 17.2 %all-gather.8.cloned.1.call-done = bf16[2304,768]{1,0:T(8,128)(2,1)} async-done(((bf16[144,768]{1,0:T(8,128)(2,1)}), bf16[2304,768]{1,0:T(8,128)(2,1)}) %all-gather.8.cloned.1.call-update) | async-done | bytes 3538960 | tf_op jit(solution)/shard_map/all_gather | solution.py:1273
  254.9 2.3 block_forward.1
  257.9 2.1 collective-permute-start.8
  259.9 1.8 collective-permute-start.9
  262.6 1.4 collective-permute-start.11
  264.1 4.2 section_backward.1
  268.3 13.2 %collective-permute-done.11 = bf16[128,768]{1,0:T(8,128)(2,1)S(1)} collective-permute-done((bf16[128,768]{1,0:T(8,128)(2,1)S(1)}, bf16[128,768]{1,0:T(8,128)(2,1)S(1)}, u32[]{:S(2)}, u32[]{:S(2)}) %collective-permute-start.11) | collective-permute-done | bytes 196640 | tf_op jit(solution)/shard_map/ppermute | solution.py:1183
  282.2 10.5 %collective-permute-done.9.refs_0_ = bf16[768,256]{1,0:T(8,128)(2,1)S(1)} collective-permute-done((bf16[768,256]{1,0:T(8,128)(2,1)S(1)}, bf16[768,256]{1,0:T(8,128)(2,1)S(1)}, u32[]{:S(2)}, u32[]{:S(2)}) %collective-permute-start.9) | collective-permute-done | bytes 393248 | tf_op jit(solution)/shard_map/ppermute | solution.py:1135
  292.8 1.3 collective-permute-start.16
  294.8 1.5 collective-permute-start.13
  296.8 19.6 %collective-permute-done.16.refs_0_ = bf16[256,768]{1,0:T(8,128)(2,1)S(1)} collective-permute-done((bf16[256,768]{1,0:T(8,128)(2,1)}, bf16[256,768]{1,0:T(8,128)(2,1)S(1)}, u32[]{:S(2)}, u32[]{:S(2)}) %collective-permute-start.16) | collective-permute-done | bytes 393248 | tf_op jit(solution)/shard_map/ppermute | solution.py:1183
  317.2 17.7 %block_backward.1 = (f32[16,768]{1,0:T(8,128)}, bf16[768,3072]{1,0:T(8,128)(2,1)}, bf16[528,768]{1,0:T(8,128)(2,1)}, f32[256,768]{1,0:T(8,128)}, bf16[256,768]{1,0:T(8,128)(2,1)}, /*index=5*/bf16[256,768]{1,0:T(8,128)(2,1)}) custom-call(bf16[256,768]{1,0:T(8,128)(2,1)} %copy-done.24, ...), custom_call_target="tpu_custom_call", output_to_operand_aliasing={{1}: (9, {}), {2}: (10, {})} | custom-call | flops 6945767424 | bytes 17645568 | tf_op jit(solution)/shard_map/block_backward/pallas_call | solution.py:741
  335.9 1.1 copy-done.2
  337.3 1.5 collective-permute-start.21
  338.8 1.9 pad_maximum_fusion.4
  340.7 2.1 pad_maximum_fusion.3
  347.1 1.2 copy.72.affine
  348.4 10.6 %conv_in_backward.1 = (f32[16,768]{1,0:T(8,128)}, f32[256,768]{1,0:T(8,128)}) custom-call(bf16[256,768]{1,0:T(8,128)(2,1)} %pad_maximum_fusion.6.refs_0_, f32[2,32,768]{2,1,0:T(8,128)} %get-tuple-element.257.refs_1_, f32[256,768]{1,0:T(8,128)} %get-tuple-element.258.refs_2_, bf16[256,768]{1,0:T(8,128)(2,1)} %get-tuple-element.259.refs_3_, ...), custom_call_target="tpu_custom_call" | custom-call | flops 2717908992 | bytes 3047424 | tf_op jit(solution)/shard_map/conv_in_backward/pallas_call | solution.py:741
  358.9 1.4 add.417
  360.4 7.4 %columns_in.4 = (bf16[864,1024]{1,0:T(8,128)(2,1)}, bf16[96,1024]{1,0:T(8,128)(2,1)}) custom-call(s32[2]{0:T(128)} %pad_add_fusion.place, s32[4]{0:T(128)} %pad_add_fusion.1.order, bf16[16,832,256]{2,1,0:T(8,128)(2,1)} %bitcast.146, f32[1536,2]{1,0:T(8,128)} %copy.72.affine), custom_call_target="tpu_custom_call" | custom-call | bytes 851968 | tf_op jit(solution)/shard_map/columns_in/pallas_call | solution.py:1002
  369.6 1.5 collective-permute-start.24
  371.6 1.9 pad_maximum_fusion.5
  374.8 1.5 reshape.1419
  376.3 1.4 reshape.1418
  379.2 4.9 all-to-all-start.1
  384.7 7.3 %columns_in.5 = (bf16[864,1024]{1,0:T(8,128)(2,1)}, bf16[96,1024]{1,0:T(8,128)(2,1)}) custom-call(s32[2]{0:T(128)} %pad_add_fusion.place, s32[4]{0:T(128)} %pad_add_fusion.2.order, bf16[16,832,256]{2,1,0:T(8,128)(2,1)} %bitcast.147, f32[1536,2]{1,0:T(8,128)} %copy.72.affine), custom_call_target="tpu_custom_call" | custom-call | bytes 851968 | tf_op jit(solution)/shard_map/columns_in/pallas_call | solution.py:1002
  392.0 2.7 columns_out.5.refs_0_
  394.7 2.8 columns_out.4.refs_0_
  398.4 1.9 collective-permute-start.27
  400.4 1.5 collective-permute-start.28
  403.5 7.3 %columns_in.7 = (bf16[864,1024]{1,0:T(8,128)(2,1)}, bf16[96,1024]{1,0:T(8,128)(2,1)}) custom-call(s32[2]{0:T(128)} %pad_add_fusion.place, s32[4]{0:T(128)} %pad_add_fusion.4.order, bf16[16,832,256]{2,1,0:T(8,128)(2,1)} %bitcast.148, f32[1536,2]{1,0:T(8,128)} %copy.72.affine), custom_call_target="tpu_custom_call" | custom-call | bytes 851968 | tf_op jit(solution)/shard_map/columns_in/pallas_call | solution.py:1002
  410.8 7.3 %columns_in.6 = (bf16[864,1024]{1,0:T(8,128)(2,1)}, bf16[96,1024]{1,0:T(8,128)(2,1)}) custom-call(s32[2]{0:T(128)} %pad_add_fusion.place, s32[4]{0:T(128)} %pad_add_fusion.3.order, bf16[16,832,256]{2,1,0:T(8,128)(2,1)} %bitcast.149, f32[1536,2]{1,0:T(8,128)} %copy.72.affine), custom_call_target="tpu_custom_call" | custom-call | bytes 851968 | tf_op jit(solution)/shard_map/columns_in/pallas_call | solution.py:1002
  418.2 2.7 columns_out.7.refs_0_
  420.9 2.8 columns_out.6.refs_3_
  423.7 6.8 %grad_step.3 = (f32[432,768]{1,0:T(8,128)}, f32[864,768]{1,0:T(8,128)}, f32[96,768]{1,0:T(8,128)}) custom-call(bf16[432,1024]{1,0:T(8,128)(2,1)} %columns_out.4.refs_0_, bf16[864,1024]{1,0:T(8,128)(2,1)} %get-tuple-element.292.refs_1_, bf16[96,1024]{1,0:T(8,128)(2,1)} %get-tuple-element.293.refs_2_, bf16[528,768]{1,0:T(8,128)(2,1)} %get-tuple-element.342.refs_3_.refs_0_, ...), custom_call_target="tpu_custom_call" | custom-call | flops 547356672 | bytes 2592768 | tf_op jit(solution)/shard_map/grad_step/pallas_call | solution.py:741
  430.5 2.4 collective-permute-done.27.refs_12_.refs_3_
  434.4 5.2 %collective-permute-start.35 = (bf16[128,768]{1,0:T(8,128)(2,1)S(1)}, bf16[128,768]{1,0:T(8,128)(2,1)S(1)}, u32[]{:S(2)}, u32[]{:S(2)}) collective-permute-start(bf16[128,768]{1,0:T(8,128)(2,1)S(1)} %slice.165), channel_id=1, source_target_pairs={{0,16},{1,17},{2,18},{3,19},{4,20},{5,21},{6,22},{7,23},{8,24},{9,... | collective-permute-start | bytes 589832 | tf_op jit(solution)/shard_map/ppermute | solution.py:1183
  440.0 2.0 collective-permute-start.31
  444.9 7.6 %collective-permute-done.31 = bf16[256,768]{1,0:T(8,128)(2,1)S(1)} collective-permute-done((bf16[256,768]{1,0:T(8,128)(2,1)S(1)}, bf16[256,768]{1,0:T(8,128)(2,1)S(1)}, u32[]{:S(2)}, u32[]{:S(2)}) %collective-permute-start.31) | collective-permute-done | bytes 393248 | tf_op jit(solution)/shard_map/ppermute | solution.py:1135
  452.4 8.7 %collective-permute-done.32 = bf16[272,768]{1,0:T(8,128)(2,1)S(1)} collective-permute-done((bf16[272,768]{1,0:T(8,128)(2,1)S(1)}, bf16[272,768]{1,0:T(8,128)(2,1)S(1)}, u32[]{:S(2)}, u32[]{:S(2)}) %collective-permute-start.32) | collective-permute-done | bytes 417824 | tf_op jit(solution)/shard_map/ppermute | solution.py:1135
  462.2 12.1 %grad_step.4 = (f32[432,768]{1,0:T(8,128)}, f32[864,768]{1,0:T(8,128)}, f32[96,768]{1,0:T(8,128)}) custom-call(bf16[432,1024]{1,0:T(8,128)(2,1)} %columns_out.5.refs_0_, bf16[864,1024]{1,0:T(8,128)(2,1)} %get-tuple-element.324.refs_1_, bf16[96,1024]{1,0:T(8,128)(2,1)} %get-tuple-element.325.refs_2_, bf16[432,1024]{1,0:T(8,128)(2,1)} %columns_out.6.refs_3_, ...), custom_call_target="tpu_custom_call" | custom-call | flops 1094713344 | bytes 5185536 | tf_op jit(solution)/shard_map/grad_step/pallas_call | solution.py:741
  479.2 1.9 last_rows.1
  483.9 8.0 %grad_step.5 = (f32[432,768]{1,0:T(8,128)}, f32[864,768]{1,0:T(8,128)}, f32[96,768]{1,0:T(8,128)}) custom-call(bf16[432,1024]{1,0:T(8,128)(2,1)} %columns_out.7.refs_0_, bf16[864,1024]{1,0:T(8,128)(2,1)} %get-tuple-element.358.refs_1_, bf16[96,1024]{1,0:T(8,128)(2,1)} %get-tuple-element.359.refs_2_, bf16[528,768]{1,0:T(8,128)(2,1)} %copy-done.7, ...), custom_call_target="tpu_custom_call" | custom-call | flops 547356672 | bytes 3661824 | tf_op jit(solution)/shard_map/grad_step/pallas_call | solution.py:741
  (259 shorter events, 47.9 us)
Async XLA Ops:
  7.2 38.7 %copy-start = (bf16[1,48,1536]{2,1,0:T(8,128)(2,1)S(1)}, bf16[1,48,1536]{2,1,0:T(8,128)(2,1)}, u32[]{:S(2)}) copy-start(bf16[1,48,1536]{2,1,0:T(8,128)(2,1)} %param.22) | copy-start | bytes 442372
  7.2 197.2 %all-gather.6.cloned.1.call-start = ((), (), s32[]{:S(2)}) async-start(), calls=%async_computation.3 | async-start | bytes 37601280 | tf_op jit(solution)/shard_map/all_gather | solution.py:1270
  10.8 3.4 collective-permute-start.6
  20.9 23.1 %copy-start.39 = (bf16[1000,48]{0,1:T(8,128)(2,1)S(1)}, bf16[1000,48]{0,1:T(8,128)(2,1)}, u32[]{:S(2)}) copy-start(bf16[1000,48]{0,1:T(8,128)(2,1)} %param.19) | copy-start | bytes 288004
  21.0 233.9 %all-gather.8.cloned.1.call-start = ((), (), s32[]{:S(2)}) async-start(), calls=%async_computation.5 | async-start | bytes 3760128 | tf_op jit(solution)/shard_map/all_gather | solution.py:1273
  21.9 7.5 %collective-permute-start.2 = (f32[1,1,896]{2,0,1:T(1,128)S(1)}, f32[1,1,896]{2,0,1:T(1,128)S(1)}, u32[]{:S(2)}, u32[]{:S(2)}) collective-permute-start(f32[1,1,896]{2,0,1:T(1,128)S(1)} %broadcast_in_dim_broadcast_in_dim.3), channel_id=1, source_target_pairs={{0,1},{1,0},{2,3},{3,2},{4,5},{5,4},{6,7},{7,6},{8,9},{9,8},{10,11... | collective-permute-start | bytes 10760 | tf_op jit(solution)/shard_map/ppermute | solution.py:1113
  22.1 32.4 %collective-permute-start.1 = (bf16[128,768]{1,0:T(8,128)(2,1)S(1)}, bf16[128,768]{1,0:T(8,128)(2,1)S(1)}, u32[]{:S(2)}, u32[]{:S(2)}) collective-permute-start(bf16[128,768]{1,0:T(8,128)(2,1)S(1)} %bitcast.157), channel_id=1, source_target_pairs={{0,16},{1,17},{2,18},{3,19},{4,20},{5,21},{6,22},{7,23},{8,24},{9,... | collective-permute-start | bytes 589832 | tf_op jit(solution)/shard_map/ppermute | solution.py:1183
  26.9 28.5 %collective-permute-start = (bf16[128,768]{1,0:T(8,128)(2,1)S(1)}, bf16[128,768]{1,0:T(8,128)(2,1)S(1)}, u32[]{:S(2)}, u32[]{:S(2)}) collective-permute-start(bf16[128,768]{1,0:T(8,128)(2,1)S(1)} %bitcast.155), channel_id=1, source_target_pairs={{16,0},{17,1},{18,2},{19,3},{20,4},{21,5},{22,6},{23,7},{24,8},{25... | collective-permute-start | bytes 589832 | tf_op jit(solution)/shard_map/ppermute | solution.py:1183
  29.4 3.7 collective-permute-start.3
  33.1 4.1 collective-permute-start.4
  37.2 5.4 %collective-permute-start.5 = (f32[8,1,896]{2,0,1:T(8,128)S(1)}, f32[8,1,896]{2,0,1:T(8,128)S(1)}, u32[]{:S(2)}, u32[]{:S(2)}) collective-permute-start(f32[8,1,896]{2,0,1:T(8,128)S(1)} %maximum_select_fusion.2), channel_id=1, source_target_pairs={{0,8},{1,9},{2,10},{3,11},{4,12},{5,13},{6,14},{7,15},{8,0},{9,1},... | collective-permute-start | bytes 86024 | tf_op jit(solution)/shard_map/ppermute | solution.py:1113
  42.7 13.5 %copy-start.26 = (f32[16,896]{1,0:T(8,128)}, f32[16,896]{1,0:T(8,128)S(1)}, u32[]{:S(2)}) copy-start(f32[16,896]{1,0:T(8,128)S(1)} %maximum_select_fusion) | copy-start | bytes 172036
  46.8 18.7 %all-to-all-start = ((bf16[16,4,1536]{2,1,0:T(4,128)(2,1)}), bf16[16,4,1536]{2,1,0:T(4,128)(2,1)S(1)}, u32[]{:S(2)}, u32[]{:S(2)}) async-start(bf16[16,4,1536]{2,1,0:T(4,128)(2,1)} %reshape.1406), calls=%async_computation | async-start | bytes 393216 | tf_op jit(solution)/shard_map/all_to_all | solution.py:1358
  53.1 307.3 %all-gather.10.cloned.1.call-start = ((), (), s32[]{:S(2)}) async-start(), calls=%async_computation.6 | async-start | bytes 7241728 | tf_op jit(solution)/shard_map/all_gather | solution.py:1428
  224.2 10.7 %collective-permute-start.7 = (bf16[256,768]{1,0:T(8,128)(2,1)}, bf16[256,768]{1,0:T(8,128)(2,1)S(1)}, u32[]{:S(2)}, u32[]{:S(2)}) collective-permute-start(bf16[256,768]{1,0:T(8,128)(2,1)} %get-tuple-element.192), channel_id=1, source_target_pairs={{0,16},{1,17},{2,18},{3,19},{4,20},{5,21},{6,22},{7,23},{8,24},{9,... | collective-permute-start | bytes 1179656 | tf_op jit(solution)/shard_map/ppermute | solution.py:1183
  237.7 236.6 %reduce-scatter.2.cloned.1.call-start = ((), (), s32[]{:S(2)}) async-start(), calls=%async_computation.4 | async-start | bytes 5013504 | tf_op jit(solution)/shard_map/reduce_scatter | solution.py:1516
  257.2 25.0 %collective-permute-start.10 = (bf16[768,256]{1,0:T(8,128)(2,1)S(1)}, bf16[768,256]{1,0:T(8,128)(2,1)S(1)}, u32[]{:S(2)}, u32[]{:S(2)}) collective-permute-start(bf16[768,256]{1,0:T(8,128)(2,1)S(1)} %copy-done.8), channel_id=1, source_target_pairs={{0,2},{1,3},{2,0},{3,1},{4,6},{5,7},{6,4},{7,5},{8,10},{9,11},{10,... | collective-permute-start | bytes 1179656 | tf_op jit(solution)/shard_map/ppermute | solution.py:1135
  257.9 24.3 %collective-permute-start.8 = (bf16[768,256]{1,0:T(8,128)(2,1)S(1)}, bf16[768,256]{1,0:T(8,128)(2,1)S(1)}, u32[]{:S(2)}, u32[]{:S(2)}) collective-permute-start(bf16[768,256]{1,0:T(8,128)(2,1)S(1)} %copy-done.8), channel_id=1, source_target_pairs={{0,4},{1,5},{2,6},{3,7},{4,8},{5,9},{6,10},{7,11},{8,12},{9,13},{1... | collective-permute-start | bytes 1179656 | tf_op jit(solution)/shard_map/ppermute | solution.py:1135
  259.9 32.8 %collective-permute-start.9 = (bf16[768,256]{1,0:T(8,128)(2,1)S(1)}, bf16[768,256]{1,0:T(8,128)(2,1)S(1)}, u32[]{:S(2)}, u32[]{:S(2)}) collective-permute-start(bf16[768,256]{1,0:T(8,128)(2,1)S(1)} %copy-done.8), channel_id=1, source_target_pairs={{0,12},{1,13},{2,14},{3,15},{4,0},{5,1},{6,2},{7,3},{8,4},{9,5},{1... | collective-permute-start | bytes 1179656 | tf_op jit(solution)/shard_map/ppermute | solution.py:1135
  262.6 18.8 %copy-start.25 = (bf16[256,768]{1,0:T(8,128)(2,1)S(1)}, bf16[256,768]{1,0:T(8,128)(2,1)}, u32[]{:S(2)}) copy-start(bf16[256,768]{1,0:T(8,128)(2,1)} %get-tuple-element.223) | copy-start | bytes 1179652
  262.6 18.8 %collective-permute-start.11 = (bf16[128,768]{1,0:T(8,128)(2,1)S(1)}, bf16[128,768]{1,0:T(8,128)(2,1)S(1)}, u32[]{:S(2)}, u32[]{:S(2)}) collective-permute-start(bf16[128,768]{1,0:T(8,128)(2,1)S(1)} %slice.96), channel_id=1, source_target_pairs={{16,0},{17,1},{18,2},{19,3},{20,4},{21,5},{22,6},{23,7},{24,8},{25... | collective-permute-start | bytes 589832 | tf_op jit(solution)/shard_map/ppermute | solution.py:1183
  282.2 52.7 %copy-start.18 = (bf16[768,256]{1,0:T(8,128)(2,1)}, bf16[768,256]{1,0:T(8,128)(2,1)S(1)}, u32[]{:S(2)}) copy-start(bf16[768,256]{1,0:T(8,128)(2,1)S(1)} %collective-permute-done.10.refs_1_) | copy-start | bytes 1179652
  282.2 52.7 %copy-start.20 = (bf16[768,256]{1,0:T(8,128)(2,1)}, bf16[768,256]{1,0:T(8,128)(2,1)S(1)}, u32[]{:S(2)}) copy-start(bf16[768,256]{1,0:T(8,128)(2,1)S(1)} %collective-permute-done.8.refs_0_) | copy-start | bytes 1179652
  292.8 46.0 %copy-start.15 = (bf16[768,256]{1,0:T(8,128)(2,1)}, bf16[768,256]{1,0:T(8,128)(2,1)S(1)}, u32[]{:S(2)}) copy-start(bf16[768,256]{1,0:T(8,128)(2,1)S(1)} %collective-permute-done.9.refs_0_) | copy-start | bytes 1179652
  292.8 23.6 %collective-permute-start.16 = (bf16[256,768]{1,0:T(8,128)(2,1)}, bf16[256,768]{1,0:T(8,128)(2,1)S(1)}, u32[]{:S(2)}, u32[]{:S(2)}) collective-permute-start(bf16[256,768]{1,0:T(8,128)(2,1)} %get-tuple-element.229), channel_id=1, source_target_pairs={{16,0},{17,1},{18,2},{19,3},{20,4},{21,5},{22,6},{23,7},{24,8},{25... | collective-permute-start | bytes 1179656 | tf_op jit(solution)/shard_map/ppermute | solution.py:1183
  294.1 41.7 %collective-permute-start.15 = (bf16[1536,256]{1,0:T(8,128)(2,1)S(1)}, bf16[1536,256]{1,0:T(8,128)(2,1)}, u32[]{:S(2)}, u32[]{:S(2)}) collective-permute-start(bf16[1536,256]{1,0:T(8,128)(2,1)S(1)} %pad_maximum_fusion.2), channel_id=1, source_target_pairs={{0,1},{1,0},{2,3},{3,2},{4,5},{5,4},{6,7},{7,6},{8,9},{9,8},{10,11... | collective-permute-start | bytes 2359304 | tf_op jit(solution)/shard_map/ppermute | solution.py:1135
  294.2 40.7 %collective-permute-start.12 = (bf16[768,256]{1,0:T(8,128)(2,1)S(1)}, bf16[768,256]{1,0:T(8,128)(2,1)S(1)}, u32[]{:S(2)}, u32[]{:S(2)}) collective-permute-start(bf16[768,256]{1,0:T(8,128)(2,1)S(1)} %collective-permute-done.8.refs_0_), channel_id=1, source_target_pairs={{0,4},{1,5},{2,6},{3,7},{4,8},{5,9},{6,10},{7,11},{8,12},{9,13},{1... | collective-permute-start | bytes 1179656 | tf_op jit(solution)/shard_map/ppermute | solution.py:1135
  294.8 40.1 %collective-permute-start.13 = (bf16[768,256]{1,0:T(8,128)(2,1)S(1)}, bf16[768,256]{1,0:T(8,128)(2,1)S(1)}, u32[]{:S(2)}, u32[]{:S(2)}) collective-permute-start(bf16[768,256]{1,0:T(8,128)(2,1)S(1)} %collective-permute-done.8.refs_0_), channel_id=1, source_target_pairs={{0,2},{1,3},{2,0},{3,1},{4,6},{5,7},{6,4},{7,5},{8,10},{9,11},{10,... | collective-permute-start | bytes 1179656 | tf_op jit(solution)/shard_map/ppermute | solution.py:1135
  296.3 38.6 %collective-permute-start.14 = (bf16[768,256]{1,0:T(8,128)(2,1)S(1)}, bf16[768,256]{1,0:T(8,128)(2,1)S(1)}, u32[]{:S(2)}, u32[]{:S(2)}) collective-permute-start(bf16[768,256]{1,0:T(8,128)(2,1)S(1)} %collective-permute-done.9.refs_0_), channel_id=1, source_target_pairs={{0,2},{1,3},{2,0},{3,1},{4,6},{5,7},{6,4},{7,5},{8,10},{9,11},{10,... | collective-permute-start | bytes 1179656 | tf_op jit(solution)/shard_map/ppermute | solution.py:1135
  334.9 10.9 %copy-start.16 = (bf16[768,256]{1,0:T(8,128)(2,1)}, bf16[768,256]{1,0:T(8,128)(2,1)S(1)}, u32[]{:S(2)}) copy-start(bf16[768,256]{1,0:T(8,128)(2,1)S(1)} %collective-permute-done.12.refs_0_) | copy-start | bytes 1179652
  337.0 30.8 %collective-permute-start.20 = (bf16[528,768]{1,0:T(8,128)(2,1)S(1)}, bf16[528,768]{1,0:T(8,128)(2,1)S(1)}, u32[]{:S(2)}, u32[]{:S(2)}) collective-permute-start(bf16[528,768]{1,0:T(8,128)(2,1)S(1)} %copy-done.2), channel_id=1, source_target_pairs={{0,4},{1,5},{2,6},{3,7},{4,8},{5,9},{6,10},{7,11},{8,12},{9,13},{1... | collective-permute-start | bytes 2433032 | tf_op jit(solution)/shard_map/ppermute | solution.py:1135
  337.3 30.6 %collective-permute-start.21 = (bf16[528,768]{1,0:T(8,128)(2,1)S(1)}, bf16[528,768]{1,0:T(8,128)(2,1)S(1)}, u32[]{:S(2)}, u32[]{:S(2)}) collective-permute-start(bf16[528,768]{1,0:T(8,128)(2,1)S(1)} %copy-done.2), channel_id=1, source_target_pairs={{0,2},{1,3},{2,0},{3,1},{4,6},{5,7},{6,4},{7,5},{8,10},{9,11},{10,... | collective-permute-start | bytes 2433032 | tf_op jit(solution)/shard_map/ppermute | solution.py:1135
  340.7 27.1 %collective-permute-start.19 = (bf16[1536,256]{1,0:T(8,128)(2,1)}, bf16[1536,256]{1,0:T(8,128)(2,1)}, u32[]{:S(2)}, u32[]{:S(2)}) collective-permute-start(bf16[1536,256]{1,0:T(8,128)(2,1)} %pad_maximum_fusion.4), channel_id=1, source_target_pairs={{0,1},{1,0},{2,3},{3,2},{4,5},{5,4},{6,7},{7,6},{8,9},{9,8},{10,11... | collective-permute-start | bytes 2359304 | tf_op jit(solution)/shard_map/ppermute | solution.py:1135
  342.8 25.1 %collective-permute-start.18 = (bf16[1536,256]{1,0:T(8,128)(2,1)}, bf16[1536,256]{1,0:T(8,128)(2,1)}, u32[]{:S(2)}, u32[]{:S(2)}) collective-permute-start(bf16[1536,256]{1,0:T(8,128)(2,1)} %pad_maximum_fusion.3), channel_id=1, source_target_pairs={{0,1},{1,0},{2,3},{3,2},{4,5},{5,4},{6,7},{7,6},{8,9},{9,8},{10,11... | collective-permute-start | bytes 2359304 | tf_op jit(solution)/shard_map/ppermute | solution.py:1135
  345.9 22.0 %collective-permute-start.17 = (bf16[768,256]{1,0:T(8,128)(2,1)S(1)}, bf16[768,256]{1,0:T(8,128)(2,1)S(1)}, u32[]{:S(2)}, u32[]{:S(2)}) collective-permute-start(bf16[768,256]{1,0:T(8,128)(2,1)S(1)} %collective-permute-done.12.refs_0_), channel_id=1, source_target_pairs={{0,2},{1,3},{2,0},{3,1},{4,6},{5,7},{6,4},{7,5},{8,10},{9,11},{10,... | collective-permute-start | bytes 1179656 | tf_op jit(solution)/shard_map/ppermute | solution.py:1135
  348.4 10.6 %copy-start.34 = (f32[16,768]{1,0:T(8,128)S(1)}, f32[16,768]{1,0:T(8,128)}, u32[]{:S(2)}) copy-start(f32[16,768]{1,0:T(8,128)} %get-tuple-element.256) | copy-start | bytes 147460
  360.4 11.2 %copy-start.17 = (bf16[768,256]{1,0:T(8,128)(2,1)S(1)}, bf16[768,256]{1,0:T(8,128)(2,1)}, u32[]{:S(2)}) copy-start(bf16[768,256]{1,0:T(8,128)(2,1)} %copy-done.16) | copy-start | bytes 1179652
  360.4 13.2 %copy-start.31 = (f32[16,768]{1,0:T(8,128)S(1)}, f32[16,768]{1,0:T(8,128)}, u32[]{:S(2)}) copy-start(f32[16,768]{1,0:T(8,128)} %add.417) | copy-start | bytes 147460
  360.4 13.2 %copy-start.33 = (f32[16,768]{1,0:T(8,128)S(1)}, f32[16,768]{1,0:T(8,128)}, u32[]{:S(2)}) copy-start(f32[16,768]{1,0:T(8,128)} %get-tuple-element.282) | copy-start | bytes 147460
  367.8 34.0 %copy-start.9 = (bf16[528,768]{1,0:T(8,128)(2,1)}, bf16[528,768]{1,0:T(8,128)(2,1)S(1)}, u32[]{:S(2)}) copy-start(bf16[528,768]{1,0:T(8,128)(2,1)S(1)} %collective-permute-done.20.refs_6_.refs_4_) | copy-start | bytes 2433028
  367.9 24.1 %copy-start.14 = (bf16[528,768]{1,0:T(8,128)(2,1)}, bf16[528,768]{1,0:T(8,128)(2,1)S(1)}, u32[]{:S(2)}) copy-start(bf16[528,768]{1,0:T(8,128)(2,1)S(1)} %collective-permute-done.21.refs_4_.refs_1_) | copy-start | bytes 2433028
  368.8 29.6 %collective-permute-start.23 = (bf16[528,768]{1,0:T(8,128)(2,1)S(1)}, bf16[528,768]{1,0:T(8,128)(2,1)}, u32[]{:S(2)}, u32[]{:S(2)}) collective-permute-start(bf16[528,768]{1,0:T(8,128)(2,1)S(1)} %collective-permute-done.20.refs_6_.refs_4_), channel_id=1, source_target_pairs={{0,4},{1,5},{2,6},{3,7},{4,8},{5,9},{6,10},{7,11},{8,12},{9,13},{1... | collective-permute-start | bytes 2433032 | tf_op jit(solution)/shard_map/ppermute | solution.py:1135
  369.6 28.8 %collective-permute-start.24 = (bf16[528,768]{1,0:T(8,128)(2,1)S(1)}, bf16[528,768]{1,0:T(8,128)(2,1)S(1)}, u32[]{:S(2)}, u32[]{:S(2)}) collective-permute-start(bf16[528,768]{1,0:T(8,128)(2,1)S(1)} %collective-permute-done.20.refs_6_.refs_4_), channel_id=1, source_target_pairs={{0,2},{1,3},{2,0},{3,1},{4,6},{5,7},{6,4},{7,5},{8,10},{9,11},{10,... | collective-permute-start | bytes 2433032 | tf_op jit(solution)/shard_map/ppermute | solution.py:1135
  371.1 27.4 %collective-permute-start.25 = (bf16[528,768]{1,0:T(8,128)(2,1)S(1)}, bf16[528,768]{1,0:T(8,128)(2,1)}, u32[]{:S(2)}, u32[]{:S(2)}) collective-permute-start(bf16[528,768]{1,0:T(8,128)(2,1)S(1)} %copy-done.2), channel_id=1, source_target_pairs={{0,1},{1,0},{2,3},{3,2},{4,5},{5,4},{6,7},{7,6},{8,9},{9,8},{10,11... | collective-permute-start | bytes 2433032 | tf_op jit(solution)/shard_map/ppermute | solution.py:1135
  371.1 27.4 %collective-permute-start.26 = (bf16[528,768]{1,0:T(8,128)(2,1)S(1)}, bf16[528,768]{1,0:T(8,128)(2,1)}, u32[]{:S(2)}, u32[]{:S(2)}) collective-permute-start(bf16[528,768]{1,0:T(8,128)(2,1)S(1)} %collective-permute-done.21.refs_4_.refs_1_), channel_id=1, source_target_pairs={{0,1},{1,0},{2,3},{3,2},{4,5},{5,4},{6,7},{7,6},{8,9},{9,8},{10,11... | collective-permute-start | bytes 2433032 | tf_op jit(solution)/shard_map/ppermute | solution.py:1135
  373.5 24.9 %collective-permute-start.22 = (bf16[1536,256]{1,0:T(8,128)(2,1)}, bf16[1536,256]{1,0:T(8,128)(2,1)}, u32[]{:S(2)}, u32[]{:S(2)}) collective-permute-start(bf16[1536,256]{1,0:T(8,128)(2,1)} %pad_maximum_fusion.5), channel_id=1, source_target_pairs={{0,1},{1,0},{2,3},{3,2},{4,5},{5,4},{6,7},{7,6},{8,9},{9,8},{10,11... | collective-permute-start | bytes 2359304 | tf_op jit(solution)/shard_map/ppermute | solution.py:1135
  379.2 18.3 %all-to-all-start.1 = ((f32[16,1,768]{2,1,0:T(1,128)}), f32[16,1,768]{2,1,0:T(1,128)}, u32[]{:S(2)}, u32[]{:S(2)}) async-start(f32[16,1,768]{2,1,0:T(1,128)} %all_to_all.10), calls=%async_computation.1 | async-start | bytes 98304 | tf_op jit(solution)/shard_map/all_to_all | solution.py:1526
  398.4 12.4 %copy-start.10 = (bf16[528,768]{1,0:T(8,128)(2,1)}, bf16[528,768]{1,0:T(8,128)(2,1)S(1)}, u32[]{:S(2)}) copy-start(bf16[528,768]{1,0:T(8,128)(2,1)S(1)} %collective-permute-done.24.refs_7_.refs_5_) | copy-start | bytes 2433028
  398.4 34.4 %collective-permute-start.27 = (bf16[528,768]{1,0:T(8,128)(2,1)}, bf16[528,768]{1,0:T(8,128)(2,1)S(1)}, u32[]{:S(2)}, u32[]{:S(2)}) collective-permute-start(bf16[528,768]{1,0:T(8,128)(2,1)} %collective-permute-done.23.refs_10_.refs_8_), channel_id=1, source_target_pairs={{0,4},{1,5},{2,6},{3,7},{4,8},{5,9},{6,10},{7,11},{8,12},{9,13},{1... | collective-permute-start | bytes 2433032 | tf_op jit(solution)/shard_map/ppermute | solution.py:1135
  400.4 32.5 %collective-permute-start.28 = (bf16[528,768]{1,0:T(8,128)(2,1)}, bf16[528,768]{1,0:T(8,128)(2,1)S(1)}, u32[]{:S(2)}, u32[]{:S(2)}) collective-permute-start(bf16[528,768]{1,0:T(8,128)(2,1)} %collective-permute-done.23.refs_10_.refs_8_), channel_id=1, source_target_pairs={{0,2},{1,3},{2,0},{3,1},{4,6},{5,7},{6,4},{7,5},{8,10},{9,11},{10,... | collective-permute-start | bytes 2433032 | tf_op jit(solution)/shard_map/ppermute | solution.py:1135
  401.8 31.0 %collective-permute-start.29 = (bf16[528,768]{1,0:T(8,128)(2,1)S(1)}, bf16[528,768]{1,0:T(8,128)(2,1)}, u32[]{:S(2)}, u32[]{:S(2)}) collective-permute-start(bf16[528,768]{1,0:T(8,128)(2,1)S(1)} %collective-permute-done.20.refs_6_.refs_4_), channel_id=1, source_target_pairs={{0,1},{1,0},{2,3},{3,2},{4,5},{5,4},{6,7},{7,6},{8,9},{9,8},{10,11... | collective-permute-start | bytes 2433032 | tf_op jit(solution)/shard_map/ppermute | solution.py:1135
  401.8 31.0 %collective-permute-start.30 = (bf16[528,768]{1,0:T(8,128)(2,1)S(1)}, bf16[528,768]{1,0:T(8,128)(2,1)}, u32[]{:S(2)}, u32[]{:S(2)}) collective-permute-start(bf16[528,768]{1,0:T(8,128)(2,1)S(1)} %collective-permute-done.24.refs_7_.refs_5_), channel_id=1, source_target_pairs={{0,1},{1,0},{2,3},{3,2},{4,5},{5,4},{6,7},{7,6},{8,9},{9,8},{10,11... | collective-permute-start | bytes 2433032 | tf_op jit(solution)/shard_map/ppermute | solution.py:1135
  430.4 13.6 %copy-start.23 = (f32[256,768]{1,0:T(8,128)S(1)}, f32[256,768]{1,0:T(8,128)}, u32[]{:S(2)}) copy-start(f32[256,768]{1,0:T(8,128)} %get-tuple-element.338) | copy-start | bytes 2359300
  432.8 41.4 %copy-start.7 = (bf16[528,768]{1,0:T(8,128)(2,1)}, bf16[528,768]{1,0:T(8,128)(2,1)S(1)}, u32[]{:S(2)}) copy-start(bf16[528,768]{1,0:T(8,128)(2,1)S(1)} %collective-permute-done.27.refs_12_.refs_3_) | copy-start | bytes 2433028
  432.8 28.4 %copy-start.6 = (bf16[528,768]{1,0:T(8,128)(2,1)}, bf16[528,768]{1,0:T(8,128)(2,1)S(1)}, u32[]{:S(2)}) copy-start(bf16[528,768]{1,0:T(8,128)(2,1)S(1)} %collective-permute-done.28.refs_11_.refs_9_) | copy-start | bytes 2433028
  432.8 28.4 %collective-permute-start.33 = (bf16[528,768]{1,0:T(8,128)(2,1)}, bf16[528,768]{1,0:T(8,128)(2,1)S(1)}, u32[]{:S(2)}, u32[]{:S(2)}) collective-permute-start(bf16[528,768]{1,0:T(8,128)(2,1)} %collective-permute-done.23.refs_10_.refs_8_), channel_id=1, source_target_pairs={{0,1},{1,0},{2,3},{3,2},{4,5},{5,4},{6,7},{7,6},{8,9},{9,8},{10,11... | collective-permute-start | bytes 2433032 | tf_op jit(solution)/shard_map/ppermute | solution.py:1135
  432.9 28.3 %collective-permute-start.34 = (bf16[528,768]{1,0:T(8,128)(2,1)S(1)}, bf16[528,768]{1,0:T(8,128)(2,1)}, u32[]{:S(2)}, u32[]{:S(2)}) collective-permute-start(bf16[528,768]{1,0:T(8,128)(2,1)S(1)} %collective-permute-done.28.refs_11_.refs_9_), channel_id=1, source_target_pairs={{0,1},{1,0},{2,3},{3,2},{4,5},{5,4},{6,7},{7,6},{8,9},{9,8},{10,11... | collective-permute-start | bytes 2433032 | tf_op jit(solution)/shard_map/ppermute | solution.py:1135
  434.4 9.6 %collective-permute-start.35 = (bf16[128,768]{1,0:T(8,128)(2,1)S(1)}, bf16[128,768]{1,0:T(8,128)(2,1)S(1)}, u32[]{:S(2)}, u32[]{:S(2)}) collective-permute-start(bf16[128,768]{1,0:T(8,128)(2,1)S(1)} %slice.165), channel_id=1, source_target_pairs={{0,16},{1,17},{2,18},{3,19},{4,20},{5,21},{6,22},{7,23},{8,24},{9,... | collective-permute-start | bytes 589832 | tf_op jit(solution)/shard_map/ppermute | solution.py:1183
  439.7 21.4 %collective-permute-start.32 = (bf16[272,768]{1,0:T(8,128)(2,1)S(1)}, bf16[272,768]{1,0:T(8,128)(2,1)S(1)}, u32[]{:S(2)}, u32[]{:S(2)}) collective-permute-start(bf16[272,768]{1,0:T(8,128)(2,1)S(1)} %slice.102), channel_id=1, source_target_pairs={{0,4},{1,5},{2,6},{3,7},{4,8},{5,9},{6,10},{7,11},{8,12},{9,13},{1... | collective-permute-start | bytes 1253384 | tf_op jit(solution)/shard_map/ppermute | solution.py:1135
  440.0 12.5 %collective-permute-start.31 = (bf16[256,768]{1,0:T(8,128)(2,1)S(1)}, bf16[256,768]{1,0:T(8,128)(2,1)S(1)}, u32[]{:S(2)}, u32[]{:S(2)}) collective-permute-start(bf16[256,768]{1,0:T(8,128)(2,1)S(1)} %slice.101), channel_id=1, source_target_pairs={{0,2},{1,3},{2,0},{3,1},{4,6},{5,7},{6,4},{7,5},{8,10},{9,11},{10,... | collective-permute-start | bytes 1179656 | tf_op jit(solution)/shard_map/ppermute | solution.py:1135
  461.2 13.1 %copy-start.1 = (bf16[528,768]{1,0:T(8,128)(2,1)}, bf16[528,768]{1,0:T(8,128)(2,1)S(1)}, u32[]{:S(2)}) copy-start(bf16[528,768]{1,0:T(8,128)(2,1)S(1)} %pad_maximum_fusion.1.refs_13_.refs_4_) | copy-start | bytes 2433028
  474.3 3.1 collective-permute-start.36
  474.4 3.5 collective-permute-start.37
  483.3 8.6 %collective-permute-start.38 = (f32[64,48]{0,1:T(8,128)S(1)}, f32[64,48]{0,1:T(8,128)S(1)}, u32[]{:S(2)}, u32[]{:S(2)}) collective-permute-start(f32[64,48]{0,1:T(8,128)S(1)} %fusion.1), channel_id=1, source_target_pairs={{0,16},{16,0},{1,17},{17,1},{2,18},{18,2},{3,19},{19,3},{4,20},{20... | collective-permute-start | bytes 36872 | tf_op jit(solution)/shard_map/ppermute | solution.py:1564
  (22 other events, 46.9 us)
Sparse Core Ops, SparseCore 0:
  21.1 183.2 all-gather.5
  207.2 47.5 all-gather.7
  257.8 91.1 all-gather.9
  352.7 106.6 reduce-scatter.1
